TPU v7x, 1024 devices: a whole 4x4x32 slice. The times are simulated.
1024 devices in a mesh: bricks: 256 (over x, z, core), gz: 4 (over y).
Axes of the slice: x: 4, y: 4, z: 32, core: 2. Of those that a mesh axis runs over, the one named last changes fastest.
Arguments:
- source: float32 [12, 512, 16, 128], P(None, 'bricks', 'gz'), may hold values from -6 to 6
- reaction: bfloat16 [12, 12, 512, 16, 128], P(None, None, 'bricks', 'gz'), may hold values from -0.1 to 2, as said below
- smoother: bfloat16 [12, 12, 512, 16, 128], P(None, None, 'bricks', 'gz'), may hold values from -0.025 to 0.5
- diffusion: float32 [12], replicated, may hold values from 0.3 to 1.5
- active: int32 [256, 4, 4], P('bricks', 'gz'), may hold values 0 or 1
Outputs:
- update: float32 [12, 512, 16, 128], P(None, 'bricks', 'gz')
- new_residual: float32 [12, 512, 16, 128], P(None, 'bricks', 'gz')
Inputs may be any that keep to these rules, and one draw needn't show every extreme that they name: `reaction`: each cell's block has diagonal entries of 0.2 to 2.0 and other entries of magnitude 0.1 or less.
All inputs are finite; a program needn't handle non-finite values. No bound on the sum of `active` on one device may be relied on, other than what follows from the above.
Results may differ from a plain program's by a relative error of at most 0.0003.
Values sent between devices are 32-bit elements; how exact they have to be, the bound alone decides.
No kernel may reach another device: no remote copies, remote signals or barrier semaphores. Data moves between devices by JAX's collectives and lax.ppermute only.
A program may use at most 32 MiB of HBM per device.

v0:
```python
import jax
import jax.numpy as jnp
from jax import lax
from jax.sharding import PartitionSpec as P

BX = 2
BZ = 4
BY = 32
CYCLES = 2
CSWEEPS = 3


def with_halo(block, sides, width):
    for axis, dim in sides:
        count = lax.axis_size(axis)
        forward = [(i, i + 1) for i in range(count - 1)]
        backward = [(target, source) for source, target in forward]
        low = lax.ppermute(
            lax.slice_in_dim(block, block.shape[dim] - width, None, axis=dim), axis, forward
        )
        high = lax.ppermute(lax.slice_in_dim(block, 0, width, axis=dim), axis, backward)
        block = jnp.concatenate([low, block, high], axis=dim)
    return block


def spread_mask(bricks_on, size_x, size_z, size_y):
    weights = bricks_on.astype(jnp.float32)
    count_x, count_z, count_y = weights.shape
    tiled = jnp.broadcast_to(
        weights[:, None, :, None, :, None], (count_x, size_x, count_z, size_z, count_y, size_y)
    )
    return tiled.reshape(count_x * size_x, count_z * size_z, count_y * size_y)


def brick_mean(blocks, size_x, size_z, size_y):
    comps = blocks.shape[0]
    shaped = blocks.reshape(
        comps,
        comps,
        blocks.shape[2] // size_x,
        size_x,
        blocks.shape[3] // size_z,
        size_z,
        blocks.shape[4] // size_y,
        size_y,
    )
    return jnp.mean(shaped.astype(jnp.float32), axis=(3, 5, 7))


def brick_apply(blocks, vector, size_x, size_z, size_y):
    comps = blocks.shape[1]
    shaped = vector.reshape(
        comps, blocks.shape[2], size_x, blocks.shape[3], size_z, blocks.shape[4], size_y
    )
    result = jnp.sum(blocks[:, :, :, None, :, None, :, None] * shaped[None], axis=1)
    return result.reshape(vector.shape)


def cell_apply(blocks, vector):
    return jnp.sum(blocks.astype(jnp.float32) * vector[None], axis=1)


def neighbor_sum(padded):
    totals = padded[:, 2:, 1:-1, 1:-1] + padded[:, :-2, 1:-1, 1:-1]
    totals = totals + padded[:, 1:-1, 2:, 1:-1] + padded[:, 1:-1, :-2, 1:-1]
    return totals + padded[:, 1:-1, 1:-1, 2:] + padded[:, 1:-1, 1:-1, :-2]


def squeeze_dim(padded, axis):
    length = (padded.shape[axis] - 2) // 2
    parts = [
        lax.slice_in_dim(padded, offset, offset + 2 * length - 1, 2, axis) for offset in range(4)
    ]
    return (parts[0] + 3.0 * parts[1] + 3.0 * parts[2] + parts[3]) * 0.125


def coarsen(padded):
    return squeeze_dim(squeeze_dim(squeeze_dim(padded, 1), 2), 3)


def stretch_dim(padded, axis):
    length = padded.shape[axis] - 2
    lower = lax.slice_in_dim(padded, 0, length, 1, axis)
    middle = lax.slice_in_dim(padded, 1, length + 1, 1, axis)
    upper = lax.slice_in_dim(padded, 2, length + 2, 1, axis)
    even_rows = 0.75 * middle + 0.25 * lower
    odd_rows = 0.75 * middle + 0.25 * upper
    joined = jnp.stack([even_rows, odd_rows], axis=axis + 1)
    new_shape = list(even_rows.shape)
    new_shape[axis] = 2 * length
    return joined.reshape(new_shape)


def refine(padded):
    return stretch_dim(stretch_dim(stretch_dim(padded, 1), 2), 3)


def fine_widen(values):
    extended = with_halo(values, (("bricks", 1), ("gz", 2)), 1)
    return jnp.pad(extended, ((0, 0), (0, 0), (0, 0), (1, 1)))


def coarse_widen(values):
    extended = with_halo(values, (("bricks", 1), ("gz", 2)), 1)
    return jnp.pad(extended, ((0, 0), (0, 0), (0, 0), (1, 1)))


def coarse_solve(coarse_rhs, coarse_react, coarse_smooth, coarse_mask, coeffs, widener):

    def smooth_step(resid):
        return (
            coarse_mask * brick_apply(coarse_smooth, resid, BX // 2, BZ // 2, BY // 2)
            + (1.0 - coarse_mask) * resid
        )

    solution = smooth_step(coarse_rhs)
    for sweep_no in range(CSWEEPS - 1):
        padded = widener(coarse_mask * solution)
        inner = brick_apply(coarse_react, solution, BX // 2, BZ // 2, BY // 2) + 0.25 * coeffs * (
            6.0 * solution - neighbor_sum(padded)
        )
        solution = solution + smooth_step(
            coarse_rhs - (coarse_mask * inner + (1.0 - coarse_mask) * solution)
        )
    return solution


def local(source, reaction, smoother, diffusion, active):
    fine_mask = spread_mask(active, BX, BZ, BY)
    coeffs = diffusion[:, None, None, None]
    coarse_react = brick_mean(reaction, BX, BZ, BY)
    coarse_smooth = brick_mean(smoother, BX, BZ, BY)
    coarse_mask = spread_mask(active, BX // 2, BZ // 2, BY // 2)

    def fine_operator(vector):
        padded = fine_widen(fine_mask * vector)
        inner = cell_apply(reaction, vector) + coeffs * (6.0 * vector - neighbor_sum(padded))
        return fine_mask * inner + (1.0 - fine_mask) * vector

    def fine_smooth(resid):
        return fine_mask * cell_apply(smoother, resid) + (1.0 - fine_mask) * resid

    update = source
    for cycle_no in range(CYCLES):
        if cycle_no == 0:
            update = fine_smooth(source)
        else:
            update = update + fine_smooth(source - fine_operator(update))
        coarse_rhs = coarsen(fine_widen(source - fine_operator(update)))
        coarse_sol = coarse_solve(
            coarse_rhs, coarse_react, coarse_smooth, coarse_mask, coeffs, coarse_widen
        )
        update = update + refine(coarse_widen(coarse_sol))
        update = update + fine_smooth(source - fine_operator(update))
    return (update, source - fine_operator(update))


def solution(mesh):
    in_specs = (
        P(None, "bricks", "gz", None),
        P(None, None, "bricks", "gz", None),
        P(None, None, "bricks", "gz", None),
        P(),
        P("bricks", "gz", None),
    )
    out_specs = (P(None, "bricks", "gz", None), P(None, "bricks", "gz", None))
    return jax.shard_map(local, mesh=mesh, in_specs=in_specs, out_specs=out_specs, check_vma=False)
```

profile of v0, /device:TPU:30, one launch (start us, length us, event | category | flops | bytes accessed | tf_op | source)
XLA Modules:
  0.0 303.3 jit_solution(724955890467282494)
XLA Ops:
  2.9 18.4 %collective-permute-start = (f32[12,1,4,128]{3,2,1,0:T(4,128)S(1)}, f32[12,1,4,128]{3,2,1,0:T(4,128)S(1)}, u32[]{:S(2)}, u32[]{:S(2)}) collective-permute-start(f32[12,1,4,128]{3,2,1,0:T(4,128)S(1)} %get-tuple-element.99), channel_id=1, source_target_pairs={{4,0},{8,4},{12,8},{16,12},{20,16},{24,20},{28,24},{32,28},{36,32}... | collective-permute-start | bytes 73736 | tf_op jit(solution)/shard_map/ppermute | solution.py:21
  23.6 4.9 %collective-permute-done.1 = f32[12,1,4,128]{3,2,1,0:T(4,128)S(1)} collective-permute-done((f32[12,1,4,128]{3,2,1,0:T(4,128)S(1)}, f32[12,1,4,128]{3,2,1,0:T(4,128)S(1)}, u32[]{:S(2)}, u32[]{:S(2)}) %collective-permute-start.1) | collective-permute-done | bytes 24608 | tf_op jit(solution)/shard_map/ppermute | solution.py:18
  28.6 2.6 collective-permute-start.2
  33.3 3.6 %collective-permute-done.3 = f32[12,4,1,128]{3,2,1,0:T(1,128)S(1)} collective-permute-done((f32[12,4,1,128]{3,2,1,0:T(1,128)S(1)}, f32[12,4,1,128]{3,2,1,0:T(1,128)S(1)}, u32[]{:S(2)}, u32[]{:S(2)}) %collective-permute-start.3) | collective-permute-done | bytes 24608 | tf_op jit(solution)/shard_map/ppermute | solution.py:18
  40.0 5.8 %collective-permute-start.5 = (f32[12,1,4,128]{3,2,1,0:T(4,128)S(1)}, f32[12,1,4,128]{3,2,1,0:T(4,128)S(1)}, u32[]{:S(2)}, u32[]{:S(2)}) collective-permute-start(f32[12,1,4,128]{3,2,1,0:T(4,128)S(1)} %get-tuple-element.97), channel_id=1, source_target_pairs={{4,0},{8,4},{12,8},{16,12},{20,16},{24,20},{28,24},{32,28},{36,32}... | collective-permute-start | bytes 73736 | tf_op jit(solution)/shard_map/ppermute | solution.py:21
  48.7 4.5 %collective-permute-start.7 = (f32[12,4,1,128]{3,2,1,0:T(1,128)S(1)}, f32[12,4,1,128]{3,2,1,0:T(1,128)S(1)}, u32[]{:S(2)}, u32[]{:S(2)}) collective-permute-start(f32[12,4,1,128]{3,2,1,0:T(1,128)S(1)} %get-tuple-element.53), channel_id=1, source_target_pairs={{1,0},{2,1},{3,2},{5,4},{6,5},{7,6},{9,8},{10,9},{11,10},{13,12},{... | collective-permute-start | bytes 73736 | tf_op jit(solution)/shard_map/ppermute | solution.py:21
  63.3 4.6 %collective-permute-start.8 = (f32[12,1,2,64]{3,1,2,0:T(1,128)S(1)}, f32[12,1,2,64]{3,1,2,0:T(1,128)S(1)}, u32[]{:S(2)}, u32[]{:S(2)}) collective-permute-start(f32[12,1,2,64]{3,1,2,0:T(1,128)S(1)} %get-tuple-element.34), channel_id=1, source_target_pairs={{4,0},{8,4},{12,8},{16,12},{20,16},{24,20},{28,24},{32,28},{36,32}... | collective-permute-start | bytes 18440 | tf_op jit(solution)/shard_map/ppermute | solution.py:21
  71.2 3.9 %collective-permute-done.9 = f32[12,1,2,64]{3,1,2,0:T(1,128)S(1)} collective-permute-done((f32[12,1,2,64]{3,1,2,0:T(1,128)S(1)}, f32[12,1,2,64]{3,1,2,0:T(1,128)S(1)}, u32[]{:S(2)}, u32[]{:S(2)}) %collective-permute-start.9) | collective-permute-done | bytes 6176 | tf_op jit(solution)/shard_map/ppermute | solution.py:18
  75.2 3.9 %collective-permute-start.10 = (f32[12,3,1,64]{3,1,2,0:T(4,128)S(1)}, f32[12,3,1,64]{3,1,2,0:T(4,128)S(1)}, u32[]{:S(2)}, u32[]{:S(2)}) collective-permute-start(f32[12,3,1,64]{3,1,2,0:T(4,128)S(1)} %get-tuple-element.95), channel_id=1, source_target_pairs={{1,0},{2,1},{3,2},{5,4},{6,5},{7,6},{9,8},{10,9},{11,10},{13,12},{... | collective-permute-start | bytes 27656 | tf_op jit(solution)/shard_map/ppermute | solution.py:21
  80.8 4.0 %collective-permute-done.11 = f32[12,3,1,64]{3,1,2,0:T(4,128)S(1)} collective-permute-done((f32[12,3,1,64]{3,1,2,0:T(4,128)S(1)}, f32[12,3,1,64]{3,1,2,0:T(4,128)S(1)}, u32[]{:S(2)}, u32[]{:S(2)}) %collective-permute-start.11) | collective-permute-done | bytes 9248 | tf_op jit(solution)/shard_map/ppermute | solution.py:18
  88.2 2.4 collective-permute-start.13
  91.4 3.9 %collective-permute-done.13 = f32[12,1,2,64]{3,1,2,0:T(1,128)S(1)} collective-permute-done((f32[12,1,2,64]{3,1,2,0:T(1,128)S(1)}, f32[12,1,2,64]{3,1,2,0:T(1,128)S(1)}, u32[]{:S(2)}, u32[]{:S(2)}) %collective-permute-start.13) | collective-permute-done | bytes 6176 | tf_op jit(solution)/shard_map/ppermute | solution.py:18
  95.4 2.4 collective-permute-start.14
  99.4 4.0 %collective-permute-done.15 = f32[12,3,1,64]{3,1,2,0:T(4,128)S(1)} collective-permute-done((f32[12,3,1,64]{3,1,2,0:T(4,128)S(1)}, f32[12,3,1,64]{3,1,2,0:T(4,128)S(1)}, u32[]{:S(2)}, u32[]{:S(2)}) %collective-permute-start.15) | collective-permute-done | bytes 9248 | tf_op jit(solution)/shard_map/ppermute | solution.py:18
  106.9 2.4 collective-permute-start.16
  109.3 4.7 %collective-permute-done.16 = f32[12,1,2,64]{3,1,2,0:T(1,128)S(1)} collective-permute-done((f32[12,1,2,64]{3,1,2,0:T(1,128)S(1)}, f32[12,1,2,64]{3,1,2,0:T(1,128)S(1)}, u32[]{:S(2)}, u32[]{:S(2)}) %collective-permute-start.16) | collective-permute-done | bytes 6176 | tf_op jit(solution)/shard_map/ppermute | solution.py:18
  115.4 4.5 %collective-permute-start.19 = (f32[12,3,1,64]{3,2,1,0:T(1,128)S(1)}, f32[12,3,1,64]{3,2,1,0:T(1,128)S(1)}, u32[]{:S(2)}, u32[]{:S(2)}) collective-permute-start(f32[12,3,1,64]{3,2,1,0:T(1,128)S(1)} %get-tuple-element.103), channel_id=1, source_target_pairs={{1,0},{2,1},{3,2},{5,4},{6,5},{7,6},{9,8},{10,9},{11,10},{13,12},{... | collective-permute-start | bytes 27656 | tf_op jit(solution)/shard_map/ppermute | solution.py:21
  124.3 2.4 collective-permute-start.21
  126.8 4.8 %collective-permute-done.21 = f32[12,1,4,128]{3,2,1,0:T(4,128)S(1)} collective-permute-done((f32[12,1,4,128]{3,2,1,0:T(4,128)S(1)}, f32[12,1,4,128]{3,2,1,0:T(4,128)S(1)}, u32[]{:S(2)}, u32[]{:S(2)}) %collective-permute-start.21) | collective-permute-done | bytes 24608 | tf_op jit(solution)/shard_map/ppermute | solution.py:18
  131.6 4.2 %collective-permute-start.22 = (f32[12,4,1,128]{3,2,1,0:T(1,128)S(1)}, f32[12,4,1,128]{3,2,1,0:T(1,128)S(1)}, u32[]{:S(2)}, u32[]{:S(2)}) collective-permute-start(f32[12,4,1,128]{3,2,1,0:T(1,128)S(1)} %get-tuple-element.51), channel_id=1, source_target_pairs={{1,0},{2,1},{3,2},{5,4},{6,5},{7,6},{9,8},{10,9},{11,10},{13,12},{... | collective-permute-start | bytes 73736 | tf_op jit(solution)/shard_map/ppermute | solution.py:21
  137.4 4.2 %collective-permute-done.23 = f32[12,4,1,128]{3,2,1,0:T(1,128)S(1)} collective-permute-done((f32[12,4,1,128]{3,2,1,0:T(1,128)S(1)}, f32[12,4,1,128]{3,2,1,0:T(1,128)S(1)}, u32[]{:S(2)}, u32[]{:S(2)}) %collective-permute-start.23) | collective-permute-done | bytes 24608 | tf_op jit(solution)/shard_map/ppermute | solution.py:18
  145.1 2.4 collective-permute-start.25
  147.5 4.8 %collective-permute-done.25 = f32[12,1,4,128]{3,2,1,0:T(4,128)S(1)} collective-permute-done((f32[12,1,4,128]{3,2,1,0:T(4,128)S(1)}, f32[12,1,4,128]{3,2,1,0:T(4,128)S(1)}, u32[]{:S(2)}, u32[]{:S(2)}) %collective-permute-start.25) | collective-permute-done | bytes 24608 | tf_op jit(solution)/shard_map/ppermute | solution.py:18
  152.4 2.4 collective-permute-start.26
  156.2 4.2 %collective-permute-done.27 = f32[12,4,1,128]{3,2,1,0:T(1,128)S(1)} collective-permute-done((f32[12,4,1,128]{3,2,1,0:T(1,128)S(1)}, f32[12,4,1,128]{3,2,1,0:T(1,128)S(1)}, u32[]{:S(2)}, u32[]{:S(2)}) %collective-permute-start.27) | collective-permute-done | bytes 24608 | tf_op jit(solution)/shard_map/ppermute | solution.py:18
  163.1 2.4 collective-permute-start.29
  165.5 4.8 %collective-permute-done.29 = f32[12,1,4,128]{3,2,1,0:T(4,128)S(1)} collective-permute-done((f32[12,1,4,128]{3,2,1,0:T(4,128)S(1)}, f32[12,1,4,128]{3,2,1,0:T(4,128)S(1)}, u32[]{:S(2)}, u32[]{:S(2)}) %collective-permute-start.29) | collective-permute-done | bytes 24608 | tf_op jit(solution)/shard_map/ppermute | solution.py:18
  173.8 4.2 %collective-permute-done.31 = f32[12,4,1,128]{3,2,1,0:T(1,128)S(1)} collective-permute-done((f32[12,4,1,128]{3,2,1,0:T(1,128)S(1)}, f32[12,4,1,128]{3,2,1,0:T(1,128)S(1)}, u32[]{:S(2)}, u32[]{:S(2)}) %collective-permute-start.31) | collective-permute-done | bytes 24608 | tf_op jit(solution)/shard_map/ppermute | solution.py:18
  180.5 5.8 %collective-permute-start.33 = (f32[12,1,4,128]{3,2,1,0:T(4,128)S(1)}, f32[12,1,4,128]{3,2,1,0:T(4,128)S(1)}, u32[]{:S(2)}, u32[]{:S(2)}) collective-permute-start(f32[12,1,4,128]{3,2,1,0:T(4,128)S(1)} %get-tuple-element.77), channel_id=1, source_target_pairs={{4,0},{8,4},{12,8},{16,12},{20,16},{24,20},{28,24},{32,28},{36,32}... | collective-permute-start | bytes 73736 | tf_op jit(solution)/shard_map/ppermute | solution.py:21
  189.1 4.7 %collective-permute-start.35 = (f32[12,4,1,128]{3,2,1,0:T(1,128)S(1)}, f32[12,4,1,128]{3,2,1,0:T(1,128)S(1)}, u32[]{:S(2)}, u32[]{:S(2)}) collective-permute-start(f32[12,4,1,128]{3,2,1,0:T(1,128)S(1)} %get-tuple-element.45), channel_id=1, source_target_pairs={{1,0},{2,1},{3,2},{5,4},{6,5},{7,6},{9,8},{10,9},{11,10},{13,12},{... | collective-permute-start | bytes 73736 | tf_op jit(solution)/shard_map/ppermute | solution.py:21
  203.8 4.6 %collective-permute-start.36 = (f32[12,1,2,64]{3,1,2,0:T(1,128)S(1)}, f32[12,1,2,64]{3,1,2,0:T(1,128)S(1)}, u32[]{:S(2)}, u32[]{:S(2)}) collective-permute-start(f32[12,1,2,64]{3,1,2,0:T(1,128)S(1)} %get-tuple-element.18), channel_id=1, source_target_pairs={{4,0},{8,4},{12,8},{16,12},{20,16},{24,20},{28,24},{32,28},{36,32}... | collective-permute-start | bytes 18440 | tf_op jit(solution)/shard_map/ppermute | solution.py:21
  211.2 4.4 %collective-permute-done.37 = f32[12,1,2,64]{3,1,2,0:T(1,128)S(1)} collective-permute-done((f32[12,1,2,64]{3,1,2,0:T(1,128)S(1)}, f32[12,1,2,64]{3,1,2,0:T(1,128)S(1)}, u32[]{:S(2)}, u32[]{:S(2)}) %collective-permute-start.37) | collective-permute-done | bytes 6176 | tf_op jit(solution)/shard_map/ppermute | solution.py:18
  215.6 3.9 %collective-permute-start.38 = (f32[12,3,1,64]{3,1,2,0:T(4,128)S(1)}, f32[12,3,1,64]{3,1,2,0:T(4,128)S(1)}, u32[]{:S(2)}, u32[]{:S(2)}) collective-permute-start(f32[12,3,1,64]{3,1,2,0:T(4,128)S(1)} %get-tuple-element.75), channel_id=1, source_target_pairs={{1,0},{2,1},{3,2},{5,4},{6,5},{7,6},{9,8},{10,9},{11,10},{13,12},{... | collective-permute-start | bytes 27656 | tf_op jit(solution)/shard_map/ppermute | solution.py:21
  221.2 4.0 %collective-permute-done.39 = f32[12,3,1,64]{3,1,2,0:T(4,128)S(1)} collective-permute-done((f32[12,3,1,64]{3,1,2,0:T(4,128)S(1)}, f32[12,3,1,64]{3,1,2,0:T(4,128)S(1)}, u32[]{:S(2)}, u32[]{:S(2)}) %collective-permute-start.39) | collective-permute-done | bytes 9248 | tf_op jit(solution)/shard_map/ppermute | solution.py:18
  228.7 2.4 collective-permute-start.41
  231.9 3.9 %collective-permute-done.41 = f32[12,1,2,64]{3,1,2,0:T(1,128)S(1)} collective-permute-done((f32[12,1,2,64]{3,1,2,0:T(1,128)S(1)}, f32[12,1,2,64]{3,1,2,0:T(1,128)S(1)}, u32[]{:S(2)}, u32[]{:S(2)}) %collective-permute-start.41) | collective-permute-done | bytes 6176 | tf_op jit(solution)/shard_map/ppermute | solution.py:18
  235.9 2.2 collective-permute-start.42
  239.8 4.0 %collective-permute-done.43 = f32[12,3,1,64]{3,1,2,0:T(4,128)S(1)} collective-permute-done((f32[12,3,1,64]{3,1,2,0:T(4,128)S(1)}, f32[12,3,1,64]{3,1,2,0:T(4,128)S(1)}, u32[]{:S(2)}, u32[]{:S(2)}) %collective-permute-start.43) | collective-permute-done | bytes 9248 | tf_op jit(solution)/shard_map/ppermute | solution.py:18
  247.2 5.8 %collective-permute-start.45 = (f32[12,1,2,64]{3,1,2,0:T(1,128)S(1)}, f32[12,1,2,64]{3,1,2,0:T(1,128)S(1)}, u32[]{:S(2)}, u32[]{:S(2)}) collective-permute-start(f32[12,1,2,64]{3,1,2,0:T(1,128)S(1)} %add_add_fusion.3), channel_id=1, source_target_pairs={{4,0},{8,4},{12,8},{16,12},{20,16},{24,20},{28,24},{32,28},{36,32}... | collective-permute-start | bytes 18440 | tf_op jit(solution)/shard_map/ppermute | solution.py:21
  255.7 4.5 %collective-permute-start.47 = (f32[12,3,1,64]{3,2,1,0:T(1,128)S(1)}, f32[12,3,1,64]{3,2,1,0:T(1,128)S(1)}, u32[]{:S(2)}, u32[]{:S(2)}) collective-permute-start(f32[12,3,1,64]{3,2,1,0:T(1,128)S(1)} %get-tuple-element.101), channel_id=1, source_target_pairs={{1,0},{2,1},{3,2},{5,4},{6,5},{7,6},{9,8},{10,9},{11,10},{13,12},{... | collective-permute-start | bytes 27656 | tf_op jit(solution)/shard_map/ppermute | solution.py:21
  262.7 4.6 %collective-permute-start.48 = (f32[12,1,4,128]{3,2,1,0:T(4,128)S(1)}, f32[12,1,4,128]{3,2,1,0:T(4,128)S(1)}, u32[]{:S(2)}, u32[]{:S(2)}) collective-permute-start(f32[12,1,4,128]{3,2,1,0:T(4,128)S(1)} %get-tuple-element.63), channel_id=1, source_target_pairs={{4,0},{8,4},{12,8},{16,12},{20,16},{24,20},{28,24},{32,28},{36,32}... | collective-permute-start | bytes 73736 | tf_op jit(solution)/shard_map/ppermute | solution.py:21
  269.3 5.3 %collective-permute-done.49 = f32[12,1,4,128]{3,2,1,0:T(4,128)S(1)} collective-permute-done((f32[12,1,4,128]{3,2,1,0:T(4,128)S(1)}, f32[12,1,4,128]{3,2,1,0:T(4,128)S(1)}, u32[]{:S(2)}, u32[]{:S(2)}) %collective-permute-start.49) | collective-permute-done | bytes 24608 | tf_op jit(solution)/shard_map/ppermute | solution.py:18
  274.7 3.9 %collective-permute-start.50 = (f32[12,4,1,128]{3,2,1,0:T(1,128)S(1)}, f32[12,4,1,128]{3,2,1,0:T(1,128)S(1)}, u32[]{:S(2)}, u32[]{:S(2)}) collective-permute-start(f32[12,4,1,128]{3,2,1,0:T(1,128)S(1)} %get-tuple-element.43), channel_id=1, source_target_pairs={{1,0},{2,1},{3,2},{5,4},{6,5},{7,6},{9,8},{10,9},{11,10},{13,12},{... | collective-permute-start | bytes 73736 | tf_op jit(solution)/shard_map/ppermute | solution.py:21
  280.1 4.2 %collective-permute-done.51 = f32[12,4,1,128]{3,2,1,0:T(1,128)S(1)} collective-permute-done((f32[12,4,1,128]{3,2,1,0:T(1,128)S(1)}, f32[12,4,1,128]{3,2,1,0:T(1,128)S(1)}, u32[]{:S(2)}, u32[]{:S(2)}) %collective-permute-start.51) | collective-permute-done | bytes 24608 | tf_op jit(solution)/shard_map/ppermute | solution.py:18
  287.0 2.4 collective-permute-start.53
  289.4 4.8 %collective-permute-done.53 = f32[12,1,4,128]{3,2,1,0:T(4,128)S(1)} collective-permute-done((f32[12,1,4,128]{3,2,1,0:T(4,128)S(1)}, f32[12,1,4,128]{3,2,1,0:T(4,128)S(1)}, u32[]{:S(2)}, u32[]{:S(2)}) %collective-permute-start.53) | collective-permute-done | bytes 24608 | tf_op jit(solution)/shard_map/ppermute | solution.py:18
  294.3 2.2 collective-permute-start.54
  298.0 4.2 %collective-permute-done.55 = f32[12,4,1,128]{3,2,1,0:T(1,128)S(1)} collective-permute-done((f32[12,4,1,128]{3,2,1,0:T(1,128)S(1)}, f32[12,4,1,128]{3,2,1,0:T(1,128)S(1)}, u32[]{:S(2)}, u32[]{:S(2)}) %collective-permute-start.55) | collective-permute-done | bytes 24608 | tf_op jit(solution)/shard_map/ppermute | solution.py:18
  (247 shorter events, 97.6 us)
Async XLA Ops:
  2.9 20.8 %collective-permute-start = (f32[12,1,4,128]{3,2,1,0:T(4,128)S(1)}, f32[12,1,4,128]{3,2,1,0:T(4,128)S(1)}, u32[]{:S(2)}, u32[]{:S(2)}) collective-permute-start(f32[12,1,4,128]{3,2,1,0:T(4,128)S(1)} %get-tuple-element.99), channel_id=1, source_target_pairs={{4,0},{8,4},{12,8},{16,12},{20,16},{24,20},{28,24},{32,28},{36,32}... | collective-permute-start | bytes 73736 | tf_op jit(solution)/shard_map/ppermute | solution.py:21
  21.3 7.3 %collective-permute-start.1 = (f32[12,1,4,128]{3,2,1,0:T(4,128)S(1)}, f32[12,1,4,128]{3,2,1,0:T(4,128)S(1)}, u32[]{:S(2)}, u32[]{:S(2)}) collective-permute-start(f32[12,1,4,128]{3,2,1,0:T(4,128)S(1)} %get-tuple-element.98), channel_id=1, source_target_pairs={{0,4},{4,8},{8,12},{12,16},{16,20},{20,24},{24,28},{28,32},{32,36}... | collective-permute-start | bytes 73736 | tf_op jit(solution)/shard_map/ppermute | solution.py:18
  28.6 4.8 %collective-permute-start.2 = (f32[12,4,1,128]{3,2,1,0:T(1,128)S(1)}, f32[12,4,1,128]{3,2,1,0:T(1,128)S(1)}, u32[]{:S(2)}, u32[]{:S(2)}) collective-permute-start(f32[12,4,1,128]{3,2,1,0:T(1,128)S(1)} %get-tuple-element.55), channel_id=1, source_target_pairs={{1,0},{2,1},{3,2},{5,4},{6,5},{7,6},{9,8},{10,9},{11,10},{13,12},{... | collective-permute-start | bytes 73736 | tf_op jit(solution)/shard_map/ppermute | solution.py:21
  31.2 5.7 %collective-permute-start.3 = (f32[12,4,1,128]{3,2,1,0:T(1,128)S(1)}, f32[12,4,1,128]{3,2,1,0:T(1,128)S(1)}, u32[]{:S(2)}, u32[]{:S(2)}) collective-permute-start(f32[12,4,1,128]{3,2,1,0:T(1,128)S(1)} %get-tuple-element.54), channel_id=1, source_target_pairs={{0,1},{1,2},{2,3},{4,5},{5,6},{6,7},{8,9},{9,10},{10,11},{12,13},{... | collective-permute-start | bytes 73736 | tf_op jit(solution)/shard_map/ppermute | solution.py:18
  38.1 7.9 %collective-permute-start.4 = (f32[12,1,4,128]{3,2,1,0:T(4,128)S(1)}, f32[12,1,4,128]{3,2,1,0:T(4,128)S(1)}, u32[]{:S(2)}, u32[]{:S(2)}) collective-permute-start(f32[12,1,4,128]{3,2,1,0:T(4,128)S(1)} %get-tuple-element.96), channel_id=1, source_target_pairs={{0,4},{4,8},{8,12},{12,16},{16,20},{20,24},{24,28},{28,32},{32,36}... | collective-permute-start | bytes 73736 | tf_op jit(solution)/shard_map/ppermute | solution.py:18
  40.0 7.3 %collective-permute-start.5 = (f32[12,1,4,128]{3,2,1,0:T(4,128)S(1)}, f32[12,1,4,128]{3,2,1,0:T(4,128)S(1)}, u32[]{:S(2)}, u32[]{:S(2)}) collective-permute-start(f32[12,1,4,128]{3,2,1,0:T(4,128)S(1)} %get-tuple-element.97), channel_id=1, source_target_pairs={{4,0},{8,4},{12,8},{16,12},{20,16},{24,20},{28,24},{32,28},{36,32}... | collective-permute-start | bytes 73736 | tf_op jit(solution)/shard_map/ppermute | solution.py:21
  47.4 5.9 %collective-permute-start.6 = (f32[12,4,1,128]{3,2,1,0:T(1,128)S(1)}, f32[12,4,1,128]{3,2,1,0:T(1,128)S(1)}, u32[]{:S(2)}, u32[]{:S(2)}) collective-permute-start(f32[12,4,1,128]{3,2,1,0:T(1,128)S(1)} %get-tuple-element.52), channel_id=1, source_target_pairs={{0,1},{1,2},{2,3},{4,5},{5,6},{6,7},{8,9},{9,10},{10,11},{12,13},{... | collective-permute-start | bytes 73736 | tf_op jit(solution)/shard_map/ppermute | solution.py:18
  48.7 6.1 %collective-permute-start.7 = (f32[12,4,1,128]{3,2,1,0:T(1,128)S(1)}, f32[12,4,1,128]{3,2,1,0:T(1,128)S(1)}, u32[]{:S(2)}, u32[]{:S(2)}) collective-permute-start(f32[12,4,1,128]{3,2,1,0:T(1,128)S(1)} %get-tuple-element.53), channel_id=1, source_target_pairs={{1,0},{2,1},{3,2},{5,4},{6,5},{7,6},{9,8},{10,9},{11,10},{13,12},{... | collective-permute-start | bytes 73736 | tf_op jit(solution)/shard_map/ppermute | solution.py:21
  63.3 7.9 %collective-permute-start.8 = (f32[12,1,2,64]{3,1,2,0:T(1,128)S(1)}, f32[12,1,2,64]{3,1,2,0:T(1,128)S(1)}, u32[]{:S(2)}, u32[]{:S(2)}) collective-permute-start(f32[12,1,2,64]{3,1,2,0:T(1,128)S(1)} %get-tuple-element.34), channel_id=1, source_target_pairs={{4,0},{8,4},{12,8},{16,12},{20,16},{24,20},{28,24},{32,28},{36,32}... | collective-permute-start | bytes 18440 | tf_op jit(solution)/shard_map/ppermute | solution.py:21
  68.0 7.1 %collective-permute-start.9 = (f32[12,1,2,64]{3,1,2,0:T(1,128)S(1)}, f32[12,1,2,64]{3,1,2,0:T(1,128)S(1)}, u32[]{:S(2)}, u32[]{:S(2)}) collective-permute-start(f32[12,1,2,64]{3,1,2,0:T(1,128)S(1)} %get-tuple-element.34), channel_id=1, source_target_pairs={{0,4},{4,8},{8,12},{12,16},{16,20},{20,24},{24,28},{28,32},{32,36}... | collective-permute-start | bytes 18440 | tf_op jit(solution)/shard_map/ppermute | solution.py:18
  75.2 5.6 %collective-permute-start.10 = (f32[12,3,1,64]{3,1,2,0:T(4,128)S(1)}, f32[12,3,1,64]{3,1,2,0:T(4,128)S(1)}, u32[]{:S(2)}, u32[]{:S(2)}) collective-permute-start(f32[12,3,1,64]{3,1,2,0:T(4,128)S(1)} %get-tuple-element.95), channel_id=1, source_target_pairs={{1,0},{2,1},{3,2},{5,4},{6,5},{7,6},{9,8},{10,9},{11,10},{13,12},{... | collective-permute-start | bytes 27656 | tf_op jit(solution)/shard_map/ppermute | solution.py:21
  79.1 5.7 %collective-permute-start.11 = (f32[12,3,1,64]{3,1,2,0:T(4,128)S(1)}, f32[12,3,1,64]{3,1,2,0:T(4,128)S(1)}, u32[]{:S(2)}, u32[]{:S(2)}) collective-permute-start(f32[12,3,1,64]{3,1,2,0:T(4,128)S(1)} %get-tuple-element.94), channel_id=1, source_target_pairs={{0,1},{1,2},{2,3},{4,5},{5,6},{6,7},{8,9},{9,10},{10,11},{12,13},{... | collective-permute-start | bytes 27656 | tf_op jit(solution)/shard_map/ppermute | solution.py:18
  86.3 5.1 %collective-permute-start.12 = (f32[12,1,2,64]{3,1,2,0:T(1,128)S(1)}, f32[12,1,2,64]{3,1,2,0:T(1,128)S(1)}, u32[]{:S(2)}, u32[]{:S(2)}) collective-permute-start(f32[12,1,2,64]{3,1,2,0:T(1,128)S(1)} %get-tuple-element.30), channel_id=1, source_target_pairs={{4,0},{8,4},{12,8},{16,12},{20,16},{24,20},{28,24},{32,28},{36,32}... | collective-permute-start | bytes 18440 | tf_op jit(solution)/shard_map/ppermute | solution.py:21
  88.2 7.1 %collective-permute-start.13 = (f32[12,1,2,64]{3,1,2,0:T(1,128)S(1)}, f32[12,1,2,64]{3,1,2,0:T(1,128)S(1)}, u32[]{:S(2)}, u32[]{:S(2)}) collective-permute-start(f32[12,1,2,64]{3,1,2,0:T(1,128)S(1)} %get-tuple-element.30), channel_id=1, source_target_pairs={{0,4},{4,8},{8,12},{12,16},{16,20},{20,24},{24,28},{28,32},{32,36}... | collective-permute-start | bytes 18440 | tf_op jit(solution)/shard_map/ppermute | solution.py:18
  97.8 5.7 %collective-permute-start.15 = (f32[12,3,1,64]{3,1,2,0:T(4,128)S(1)}, f32[12,3,1,64]{3,1,2,0:T(4,128)S(1)}, u32[]{:S(2)}, u32[]{:S(2)}) collective-permute-start(f32[12,3,1,64]{3,1,2,0:T(4,128)S(1)} %get-tuple-element.90), channel_id=1, source_target_pairs={{0,1},{1,2},{2,3},{4,5},{5,6},{6,7},{8,9},{9,10},{10,11},{12,13},{... | collective-permute-start | bytes 27656 | tf_op jit(solution)/shard_map/ppermute | solution.py:18
  105.0 4.3 %collective-permute-start.17 = (f32[12,1,2,64]{3,1,2,0:T(1,128)S(1)}, f32[12,1,2,64]{3,1,2,0:T(1,128)S(1)}, u32[]{:S(2)}, u32[]{:S(2)}) collective-permute-start(f32[12,1,2,64]{3,1,2,0:T(1,128)S(1)} %add_add_fusion.6), channel_id=1, source_target_pairs={{4,0},{8,4},{12,8},{16,12},{20,16},{24,20},{28,24},{32,28},{36,32}... | collective-permute-start | bytes 18440 | tf_op jit(solution)/shard_map/ppermute | solution.py:21
  106.9 7.1 %collective-permute-start.16 = (f32[12,1,2,64]{3,1,2,0:T(1,128)S(1)}, f32[12,1,2,64]{3,1,2,0:T(1,128)S(1)}, u32[]{:S(2)}, u32[]{:S(2)}) collective-permute-start(f32[12,1,2,64]{3,1,2,0:T(1,128)S(1)} %add_add_fusion.6), channel_id=1, source_target_pairs={{0,4},{4,8},{8,12},{12,16},{16,20},{20,24},{24,28},{28,32},{32,36}... | collective-permute-start | bytes 18440 | tf_op jit(solution)/shard_map/ppermute | solution.py:18
  114.1 5.9 %collective-permute-start.18 = (f32[12,3,1,64]{3,2,1,0:T(1,128)S(1)}, f32[12,3,1,64]{3,2,1,0:T(1,128)S(1)}, u32[]{:S(2)}, u32[]{:S(2)}) collective-permute-start(f32[12,3,1,64]{3,2,1,0:T(1,128)S(1)} %get-tuple-element.102), channel_id=1, source_target_pairs={{0,1},{1,2},{2,3},{4,5},{5,6},{6,7},{8,9},{9,10},{10,11},{12,13},{... | collective-permute-start | bytes 27656 | tf_op jit(solution)/shard_map/ppermute | solution.py:18
  115.4 6.0 %collective-permute-start.19 = (f32[12,3,1,64]{3,2,1,0:T(1,128)S(1)}, f32[12,3,1,64]{3,2,1,0:T(1,128)S(1)}, u32[]{:S(2)}, u32[]{:S(2)}) collective-permute-start(f32[12,3,1,64]{3,2,1,0:T(1,128)S(1)} %get-tuple-element.103), channel_id=1, source_target_pairs={{1,0},{2,1},{3,2},{5,4},{6,5},{7,6},{9,8},{10,9},{11,10},{13,12},{... | collective-permute-start | bytes 27656 | tf_op jit(solution)/shard_map/ppermute | solution.py:21
  124.3 7.3 %collective-permute-start.21 = (f32[12,1,4,128]{3,2,1,0:T(4,128)S(1)}, f32[12,1,4,128]{3,2,1,0:T(4,128)S(1)}, u32[]{:S(2)}, u32[]{:S(2)}) collective-permute-start(f32[12,1,4,128]{3,2,1,0:T(4,128)S(1)} %get-tuple-element.82), channel_id=1, source_target_pairs={{0,4},{4,8},{8,12},{12,16},{16,20},{20,24},{24,28},{28,32},{32,36}... | collective-permute-start | bytes 73736 | tf_op jit(solution)/shard_map/ppermute | solution.py:18
  131.6 5.7 %collective-permute-start.22 = (f32[12,4,1,128]{3,2,1,0:T(1,128)S(1)}, f32[12,4,1,128]{3,2,1,0:T(1,128)S(1)}, u32[]{:S(2)}, u32[]{:S(2)}) collective-permute-start(f32[12,4,1,128]{3,2,1,0:T(1,128)S(1)} %get-tuple-element.51), channel_id=1, source_target_pairs={{1,0},{2,1},{3,2},{5,4},{6,5},{7,6},{9,8},{10,9},{11,10},{13,12},{... | collective-permute-start | bytes 73736 | tf_op jit(solution)/shard_map/ppermute | solution.py:21
  135.9 5.7 %collective-permute-start.23 = (f32[12,4,1,128]{3,2,1,0:T(1,128)S(1)}, f32[12,4,1,128]{3,2,1,0:T(1,128)S(1)}, u32[]{:S(2)}, u32[]{:S(2)}) collective-permute-start(f32[12,4,1,128]{3,2,1,0:T(1,128)S(1)} %get-tuple-element.50), channel_id=1, source_target_pairs={{0,1},{1,2},{2,3},{4,5},{5,6},{6,7},{8,9},{9,10},{10,11},{12,13},{... | collective-permute-start | bytes 73736 | tf_op jit(solution)/shard_map/ppermute | solution.py:18
  145.1 7.3 %collective-permute-start.25 = (f32[12,1,4,128]{3,2,1,0:T(4,128)S(1)}, f32[12,1,4,128]{3,2,1,0:T(4,128)S(1)}, u32[]{:S(2)}, u32[]{:S(2)}) collective-permute-start(f32[12,1,4,128]{3,2,1,0:T(4,128)S(1)} %get-tuple-element.80), channel_id=1, source_target_pairs={{0,4},{4,8},{8,12},{12,16},{16,20},{20,24},{24,28},{28,32},{32,36}... | collective-permute-start | bytes 73736 | tf_op jit(solution)/shard_map/ppermute | solution.py:18
  154.7 5.7 %collective-permute-start.27 = (f32[12,4,1,128]{3,2,1,0:T(1,128)S(1)}, f32[12,4,1,128]{3,2,1,0:T(1,128)S(1)}, u32[]{:S(2)}, u32[]{:S(2)}) collective-permute-start(f32[12,4,1,128]{3,2,1,0:T(1,128)S(1)} %get-tuple-element.48), channel_id=1, source_target_pairs={{0,1},{1,2},{2,3},{4,5},{5,6},{6,7},{8,9},{9,10},{10,11},{12,13},{... | collective-permute-start | bytes 73736 | tf_op jit(solution)/shard_map/ppermute | solution.py:18
  163.1 7.3 %collective-permute-start.29 = (f32[12,1,4,128]{3,2,1,0:T(4,128)S(1)}, f32[12,1,4,128]{3,2,1,0:T(4,128)S(1)}, u32[]{:S(2)}, u32[]{:S(2)}) collective-permute-start(f32[12,1,4,128]{3,2,1,0:T(4,128)S(1)} %get-tuple-element.78), channel_id=1, source_target_pairs={{0,4},{4,8},{8,12},{12,16},{16,20},{20,24},{24,28},{28,32},{32,36}... | collective-permute-start | bytes 73736 | tf_op jit(solution)/shard_map/ppermute | solution.py:18
  172.3 5.7 %collective-permute-start.31 = (f32[12,4,1,128]{3,2,1,0:T(1,128)S(1)}, f32[12,4,1,128]{3,2,1,0:T(1,128)S(1)}, u32[]{:S(2)}, u32[]{:S(2)}) collective-permute-start(f32[12,4,1,128]{3,2,1,0:T(1,128)S(1)} %get-tuple-element.46), channel_id=1, source_target_pairs={{0,1},{1,2},{2,3},{4,5},{5,6},{6,7},{8,9},{9,10},{10,11},{12,13},{... | collective-permute-start | bytes 73736 | tf_op jit(solution)/shard_map/ppermute | solution.py:18
  178.6 7.7 %collective-permute-start.32 = (f32[12,1,4,128]{3,2,1,0:T(4,128)S(1)}, f32[12,1,4,128]{3,2,1,0:T(4,128)S(1)}, u32[]{:S(2)}, u32[]{:S(2)}) collective-permute-start(f32[12,1,4,128]{3,2,1,0:T(4,128)S(1)} %get-tuple-element.76), channel_id=1, source_target_pairs={{0,4},{4,8},{8,12},{12,16},{16,20},{20,24},{24,28},{28,32},{32,36}... | collective-permute-start | bytes 73736 | tf_op jit(solution)/shard_map/ppermute | solution.py:18
  180.5 7.3 %collective-permute-start.33 = (f32[12,1,4,128]{3,2,1,0:T(4,128)S(1)}, f32[12,1,4,128]{3,2,1,0:T(4,128)S(1)}, u32[]{:S(2)}, u32[]{:S(2)}) collective-permute-start(f32[12,1,4,128]{3,2,1,0:T(4,128)S(1)} %get-tuple-element.77), channel_id=1, source_target_pairs={{4,0},{8,4},{12,8},{16,12},{20,16},{24,20},{28,24},{32,28},{36,32}... | collective-permute-start | bytes 73736 | tf_op jit(solution)/shard_map/ppermute | solution.py:21
  187.8 6.1 %collective-permute-start.34 = (f32[12,4,1,128]{3,2,1,0:T(1,128)S(1)}, f32[12,4,1,128]{3,2,1,0:T(1,128)S(1)}, u32[]{:S(2)}, u32[]{:S(2)}) collective-permute-start(f32[12,4,1,128]{3,2,1,0:T(1,128)S(1)} %get-tuple-element.44), channel_id=1, source_target_pairs={{0,1},{1,2},{2,3},{4,5},{5,6},{6,7},{8,9},{9,10},{10,11},{12,13},{... | collective-permute-start | bytes 73736 | tf_op jit(solution)/shard_map/ppermute | solution.py:18
  189.1 6.1 %collective-permute-start.35 = (f32[12,4,1,128]{3,2,1,0:T(1,128)S(1)}, f32[12,4,1,128]{3,2,1,0:T(1,128)S(1)}, u32[]{:S(2)}, u32[]{:S(2)}) collective-permute-start(f32[12,4,1,128]{3,2,1,0:T(1,128)S(1)} %get-tuple-element.45), channel_id=1, source_target_pairs={{1,0},{2,1},{3,2},{5,4},{6,5},{7,6},{9,8},{10,9},{11,10},{13,12},{... | collective-permute-start | bytes 73736 | tf_op jit(solution)/shard_map/ppermute | solution.py:21
  203.8 7.3 %collective-permute-start.36 = (f32[12,1,2,64]{3,1,2,0:T(1,128)S(1)}, f32[12,1,2,64]{3,1,2,0:T(1,128)S(1)}, u32[]{:S(2)}, u32[]{:S(2)}) collective-permute-start(f32[12,1,2,64]{3,1,2,0:T(1,128)S(1)} %get-tuple-element.18), channel_id=1, source_target_pairs={{4,0},{8,4},{12,8},{16,12},{20,16},{24,20},{28,24},{32,28},{36,32}... | collective-permute-start | bytes 18440 | tf_op jit(solution)/shard_map/ppermute | solution.py:21
  208.4 7.1 %collective-permute-start.37 = (f32[12,1,2,64]{3,1,2,0:T(1,128)S(1)}, f32[12,1,2,64]{3,1,2,0:T(1,128)S(1)}, u32[]{:S(2)}, u32[]{:S(2)}) collective-permute-start(f32[12,1,2,64]{3,1,2,0:T(1,128)S(1)} %get-tuple-element.18), channel_id=1, source_target_pairs={{0,4},{4,8},{8,12},{12,16},{16,20},{20,24},{24,28},{28,32},{32,36}... | collective-permute-start | bytes 18440 | tf_op jit(solution)/shard_map/ppermute | solution.py:18
  215.6 5.6 %collective-permute-start.38 = (f32[12,3,1,64]{3,1,2,0:T(4,128)S(1)}, f32[12,3,1,64]{3,1,2,0:T(4,128)S(1)}, u32[]{:S(2)}, u32[]{:S(2)}) collective-permute-start(f32[12,3,1,64]{3,1,2,0:T(4,128)S(1)} %get-tuple-element.75), channel_id=1, source_target_pairs={{1,0},{2,1},{3,2},{5,4},{6,5},{7,6},{9,8},{10,9},{11,10},{13,12},{... | collective-permute-start | bytes 27656 | tf_op jit(solution)/shard_map/ppermute | solution.py:21
  219.6 5.7 %collective-permute-start.39 = (f32[12,3,1,64]{3,1,2,0:T(4,128)S(1)}, f32[12,3,1,64]{3,1,2,0:T(4,128)S(1)}, u32[]{:S(2)}, u32[]{:S(2)}) collective-permute-start(f32[12,3,1,64]{3,1,2,0:T(4,128)S(1)} %get-tuple-element.74), channel_id=1, source_target_pairs={{0,1},{1,2},{2,3},{4,5},{5,6},{6,7},{8,9},{9,10},{10,11},{12,13},{... | collective-permute-start | bytes 27656 | tf_op jit(solution)/shard_map/ppermute | solution.py:18
  226.7 5.1 %collective-permute-start.40 = (f32[12,1,2,64]{3,1,2,0:T(1,128)S(1)}, f32[12,1,2,64]{3,1,2,0:T(1,128)S(1)}, u32[]{:S(2)}, u32[]{:S(2)}) collective-permute-start(f32[12,1,2,64]{3,1,2,0:T(1,128)S(1)} %get-tuple-element.14), channel_id=1, source_target_pairs={{4,0},{8,4},{12,8},{16,12},{20,16},{24,20},{28,24},{32,28},{36,32}... | collective-permute-start | bytes 18440 | tf_op jit(solution)/shard_map/ppermute | solution.py:21
  228.7 7.1 %collective-permute-start.41 = (f32[12,1,2,64]{3,1,2,0:T(1,128)S(1)}, f32[12,1,2,64]{3,1,2,0:T(1,128)S(1)}, u32[]{:S(2)}, u32[]{:S(2)}) collective-permute-start(f32[12,1,2,64]{3,1,2,0:T(1,128)S(1)} %get-tuple-element.14), channel_id=1, source_target_pairs={{0,4},{4,8},{8,12},{12,16},{16,20},{20,24},{24,28},{28,32},{32,36}... | collective-permute-start | bytes 18440 | tf_op jit(solution)/shard_map/ppermute | solution.py:18
  238.1 5.7 %collective-permute-start.43 = (f32[12,3,1,64]{3,1,2,0:T(4,128)S(1)}, f32[12,3,1,64]{3,1,2,0:T(4,128)S(1)}, u32[]{:S(2)}, u32[]{:S(2)}) collective-permute-start(f32[12,3,1,64]{3,1,2,0:T(4,128)S(1)} %get-tuple-element.70), channel_id=1, source_target_pairs={{0,1},{1,2},{2,3},{4,5},{5,6},{6,7},{8,9},{9,10},{10,11},{12,13},{... | collective-permute-start | bytes 27656 | tf_op jit(solution)/shard_map/ppermute | solution.py:18
  245.3 7.7 %collective-permute-start.44 = (f32[12,1,2,64]{3,1,2,0:T(1,128)S(1)}, f32[12,1,2,64]{3,1,2,0:T(1,128)S(1)}, u32[]{:S(2)}, u32[]{:S(2)}) collective-permute-start(f32[12,1,2,64]{3,1,2,0:T(1,128)S(1)} %add_add_fusion.3), channel_id=1, source_target_pairs={{0,4},{4,8},{8,12},{12,16},{16,20},{20,24},{24,28},{28,32},{32,36}... | collective-permute-start | bytes 18440 | tf_op jit(solution)/shard_map/ppermute | solution.py:18
  247.2 7.1 %collective-permute-start.45 = (f32[12,1,2,64]{3,1,2,0:T(1,128)S(1)}, f32[12,1,2,64]{3,1,2,0:T(1,128)S(1)}, u32[]{:S(2)}, u32[]{:S(2)}) collective-permute-start(f32[12,1,2,64]{3,1,2,0:T(1,128)S(1)} %add_add_fusion.3), channel_id=1, source_target_pairs={{4,0},{8,4},{12,8},{16,12},{20,16},{24,20},{28,24},{32,28},{36,32}... | collective-permute-start | bytes 18440 | tf_op jit(solution)/shard_map/ppermute | solution.py:21
  254.4 5.9 %collective-permute-start.46 = (f32[12,3,1,64]{3,2,1,0:T(1,128)S(1)}, f32[12,3,1,64]{3,2,1,0:T(1,128)S(1)}, u32[]{:S(2)}, u32[]{:S(2)}) collective-permute-start(f32[12,3,1,64]{3,2,1,0:T(1,128)S(1)} %get-tuple-element.100), channel_id=1, source_target_pairs={{0,1},{1,2},{2,3},{4,5},{5,6},{6,7},{8,9},{9,10},{10,11},{12,13},{... | collective-permute-start | bytes 27656 | tf_op jit(solution)/shard_map/ppermute | solution.py:18
  255.7 6.0 %collective-permute-start.47 = (f32[12,3,1,64]{3,2,1,0:T(1,128)S(1)}, f32[12,3,1,64]{3,2,1,0:T(1,128)S(1)}, u32[]{:S(2)}, u32[]{:S(2)}) collective-permute-start(f32[12,3,1,64]{3,2,1,0:T(1,128)S(1)} %get-tuple-element.101), channel_id=1, source_target_pairs={{1,0},{2,1},{3,2},{5,4},{6,5},{7,6},{9,8},{10,9},{11,10},{13,12},{... | collective-permute-start | bytes 27656 | tf_op jit(solution)/shard_map/ppermute | solution.py:21
  262.7 6.5 %collective-permute-start.48 = (f32[12,1,4,128]{3,2,1,0:T(4,128)S(1)}, f32[12,1,4,128]{3,2,1,0:T(4,128)S(1)}, u32[]{:S(2)}, u32[]{:S(2)}) collective-permute-start(f32[12,1,4,128]{3,2,1,0:T(4,128)S(1)} %get-tuple-element.63), channel_id=1, source_target_pairs={{4,0},{8,4},{12,8},{16,12},{20,16},{24,20},{28,24},{32,28},{36,32}... | collective-permute-start | bytes 73736 | tf_op jit(solution)/shard_map/ppermute | solution.py:21
  267.4 7.3 %collective-permute-start.49 = (f32[12,1,4,128]{3,2,1,0:T(4,128)S(1)}, f32[12,1,4,128]{3,2,1,0:T(4,128)S(1)}, u32[]{:S(2)}, u32[]{:S(2)}) collective-permute-start(f32[12,1,4,128]{3,2,1,0:T(4,128)S(1)} %get-tuple-element.62), channel_id=1, source_target_pairs={{0,4},{4,8},{8,12},{12,16},{16,20},{20,24},{24,28},{28,32},{32,36}... | collective-permute-start | bytes 73736 | tf_op jit(solution)/shard_map/ppermute | solution.py:18
  274.7 5.4 %collective-permute-start.50 = (f32[12,4,1,128]{3,2,1,0:T(1,128)S(1)}, f32[12,4,1,128]{3,2,1,0:T(1,128)S(1)}, u32[]{:S(2)}, u32[]{:S(2)}) collective-permute-start(f32[12,4,1,128]{3,2,1,0:T(1,128)S(1)} %get-tuple-element.43), channel_id=1, source_target_pairs={{1,0},{2,1},{3,2},{5,4},{6,5},{7,6},{9,8},{10,9},{11,10},{13,12},{... | collective-permute-start | bytes 73736 | tf_op jit(solution)/shard_map/ppermute | solution.py:21
  278.6 5.7 %collective-permute-start.51 = (f32[12,4,1,128]{3,2,1,0:T(1,128)S(1)}, f32[12,4,1,128]{3,2,1,0:T(1,128)S(1)}, u32[]{:S(2)}, u32[]{:S(2)}) collective-permute-start(f32[12,4,1,128]{3,2,1,0:T(1,128)S(1)} %get-tuple-element.42), channel_id=1, source_target_pairs={{0,1},{1,2},{2,3},{4,5},{5,6},{6,7},{8,9},{9,10},{10,11},{12,13},{... | collective-permute-start | bytes 73736 | tf_op jit(solution)/shard_map/ppermute | solution.py:18
  285.0 4.3 %collective-permute-start.52 = (f32[12,1,4,128]{3,2,1,0:T(4,128)S(1)}, f32[12,1,4,128]{3,2,1,0:T(4,128)S(1)}, u32[]{:S(2)}, u32[]{:S(2)}) collective-permute-start(f32[12,1,4,128]{3,2,1,0:T(4,128)S(1)} %get-tuple-element.61), channel_id=1, source_target_pairs={{4,0},{8,4},{12,8},{16,12},{20,16},{24,20},{28,24},{32,28},{36,32}... | collective-permute-start | bytes 73736 | tf_op jit(solution)/shard_map/ppermute | solution.py:21
  287.0 7.3 %collective-permute-start.53 = (f32[12,1,4,128]{3,2,1,0:T(4,128)S(1)}, f32[12,1,4,128]{3,2,1,0:T(4,128)S(1)}, u32[]{:S(2)}, u32[]{:S(2)}) collective-permute-start(f32[12,1,4,128]{3,2,1,0:T(4,128)S(1)} %get-tuple-element.60), channel_id=1, source_target_pairs={{0,4},{4,8},{8,12},{12,16},{16,20},{20,24},{24,28},{28,32},{32,36}... | collective-permute-start | bytes 73736 | tf_op jit(solution)/shard_map/ppermute | solution.py:18
  296.5 5.7 %collective-permute-start.55 = (f32[12,4,1,128]{3,2,1,0:T(1,128)S(1)}, f32[12,4,1,128]{3,2,1,0:T(1,128)S(1)}, u32[]{:S(2)}, u32[]{:S(2)}) collective-permute-start(f32[12,4,1,128]{3,2,1,0:T(1,128)S(1)} %get-tuple-element.40), channel_id=1, source_target_pairs={{0,1},{1,2},{2,3},{4,5},{5,6},{6,7},{8,9},{9,10},{10,11},{12,13},{... | collective-permute-start | bytes 73736 | tf_op jit(solution)/shard_map/ppermute | solution.py:18
  (13 other events, 61.6 us)
where the time goes:
time: 305 us; the launch traced here: 303 us
  starting transfers between devices  159 us (52%)
  waiting for transfers between devices  101 us (33%)
  local copies, waits for them, and re-layouts  21 us (7%)
  other arithmetic  19.7 us (6%)
    ppermute x28, starting transfers between devices, with_halo(): lax.ppermute(lax.slice_in_dim(block, 0, width, axis=dim), axis, backward)  111 us
    ppermute x28, waiting for transfers between devices, with_halo(): lax.ppermute(lax.slice_in_dim(block, block.shape[dim] - width, None, axis...  91.2 us
    ppermute x28, starting transfers between devices, with_halo(): lax.ppermute(lax.slice_in_dim(block, block.shape[dim] - width, None, axis...  48.4 us
    slice x8, local copies, waits for them, and re-layouts, squeeze_dim(): lax.slice_in_dim(padded, offset, offset + 2 * length - 1, 2, axis)  15 us
    ppermute x28, waiting for transfers between devices, with_halo(): lax.ppermute(lax.slice_in_dim(block, 0, width, axis=dim), axis, backward)  9.99 us
  transfers between devices with their start and end apart: 56, of which 28 were waited for; matrix products, arithmetic and copies ran while one was open for 2% of the time, Pallas kernels for 0%

commit v1 on v0

v1 whole, which is shorter than its diff:
```python
import functools

import jax
import jax.numpy as jnp
from jax import lax
from jax.experimental import pallas as pl
from jax.experimental.pallas import tpu as pltpu
from jax.sharding import Mesh
from jax.sharding import PartitionSpec as P

COMP = 12
HALF = 6
F32 = jnp.float32
BF16 = jnp.bfloat16
X_AXES = ("xg", "xc", "core")
TILE = (8, 128)
CHANNELS = 11
CENTRE = 3
VMEM_LIMIT = 32 * 1024 * 1024


def rows(shape=TILE):
    return lax.broadcasted_iota(jnp.int32, shape, 0)


def lanes(shape=TILE):
    return lax.broadcasted_iota(jnp.int32, shape, 1)


def up(x, by):
    return pltpu.roll(x, 8 - by, 0)


def down(x, by):
    return pltpu.roll(x, by, 0)


def pick(cond, a, b):
    return jnp.where(cond, a, b)


def hat(diff):
    inner = jnp.logical_or(diff == 0, diff == 1)
    outer = jnp.logical_or(diff == -1, diff == 2)
    return jnp.where(inner, 3.0, jnp.where(outer, 1.0, 0.0)).astype(F32)


def split(x, parts):
    pieces = []
    for _ in range(parts):
        piece = x.astype(BF16)
        pieces.append(piece)
        x = x - piece.astype(F32)
    return pieces


def dot(a, b):
    return jnp.dot(a, b, preferred_element_type=F32)


def dot_right(x, weights, parts=3):
    total = None
    for piece in split(x, parts):
        term = dot(piece, weights)
        total = term if total is None else total + term
    return total


def dot_left(weights, x, parts=3):
    total = None
    for piece in split(x, parts):
        term = dot(weights, piece)
        total = term if total is None else total + term
    return total


def fine_mask_of(act_ref):
    brick = lanes() // 32
    out = jnp.zeros(TILE, F32)
    for b in range(4):
        out = jnp.where(brick == b, act_ref[b].astype(F32), out)
    return out


def packed_mask_of(act_ref):
    brick = (lanes() % 64) // 16
    out = jnp.zeros(TILE, F32)
    for b in range(4):
        out = jnp.where(brick == b, act_ref[b].astype(F32), out)
    return out


def load(ref):
    return [ref[c] for c in range(COMP)]


def block_product(blocks_ref, vec):
    out = []
    for c in range(COMP):
        acc = None
        for d in range(0, COMP, 2):
            pair = blocks_ref[pl.ds((c * COMP + d) * 8, 16), :].astype(F32)
            term = pair[:8] * vec[d] + pair[8:] * vec[d + 1]
            acc = term if acc is None else acc + term
        out.append(acc)
    return out


def smooth(smoother_ref, mask, resid):
    prod = block_product(smoother_ref, resid)
    return [mask * a + (1.0 - mask) * r for a, r in zip(prod, resid)]


def neighbours(mv, hx, hz):
    z = rows() % 4
    lane = lanes()
    total = down(mv, 4) + hx + hz
    total = total + jnp.where(z > 0, down(mv, 1), 0.0) + jnp.where(z < 3, up(mv, 1), 0.0)
    total = total + jnp.where(lane > 0, pltpu.roll(mv, 1, 1), 0.0)
    return total + jnp.where(lane < 127, pltpu.roll(mv, 127, 1), 0.0)


def operator(reaction_ref, diff_ref, mask, vec, hx, hz):
    prod = block_product(reaction_ref, vec)
    out = []
    for c in range(COMP):
        v = vec[c]
        inner = prod[c] + diff_ref[c] * (6.0 * v - neighbours(mask * v, hx[c], hz[c]))
        out.append(mask * inner + (1.0 - mask) * v)
    return out


def write_faces(sc_ref, mask, vec, face_ref, swap_ref):
    core, zd = sc_ref[0], sc_ref[1]
    s = rows()
    low_half = s < 4
    z = s % 4
    mv = [mask * v for v in vec]
    first = core == 0
    for j in range(HALF):
        a, b = mv[j], mv[j + HALF]
        to_high = jnp.where(low_half, down(a, 4), b)
        to_low = jnp.where(low_half, a, down(b, 4))
        in_chip = pick(first, to_high, to_low)
        swap_ref[j] = pick(first, to_low, to_high)
        z_up = jnp.where(z == 0, up(a, 3), jnp.where(z == 1, up(b, 2), 0.0))
        z_down = jnp.where(z == 3, down(a, 3), jnp.where(z == 2, down(b, 2), 0.0))
        for other in range(4):
            along = pick(other > zd, z_up, z_down)
            face_ref[other, j] = pick(first, along, in_chip)
            face_ref[4 + other, j] = pick(first, in_chip, along)


def read_faces(sc_ref, face_ref, swap_ref):
    core, zd = sc_ref[0], sc_ref[1]
    s = rows()
    low_half = s < 4
    z = s % 4
    first = core == 0
    chip_at = (1 - core) * 4 + zd
    low_at = core * 4 + jnp.maximum(zd - 1, 0)
    high_at = core * 4 + jnp.minimum(zd + 1, 3)
    has_low = jnp.logical_and(z == 0, zd > 0)
    has_high = jnp.logical_and(z == 3, zd < 3)
    hx, hz = [None] * COMP, [None] * COMP
    for j in range(HALF):
        chip = face_ref[chip_at, j]
        cross = swap_ref[j]
        low = pick(first, cross, chip)
        high = pick(first, chip, cross)
        hx[j] = jnp.where(low_half, low, down(high, 4))
        hx[j + HALF] = jnp.where(low_half, down(low, 4), high)
        zl = face_ref[low_at, j]
        zh = face_ref[high_at, j]
        hz[j] = jnp.where(has_low, zl, jnp.where(has_high, zh, 0.0))
        hz[j + HALF] = jnp.where(has_low, up(zl, 1), jnp.where(has_high, down(zh, 1), 0.0))
    return hx, hz


def contributions(resid):
    l, o = rows((128, 128)), lanes((128, 128))
    low = jnp.where(o < 64, hat(l - 2 * o), 0.0).astype(BF16)
    high = jnp.where(o >= 64, hat(l - 2 * (o - 64)), 0.0).astype(BF16)
    a = jnp.concatenate(resid[:HALF], axis=0)
    b = jnp.concatenate(resid[HALF:], axis=0)
    along_y = (dot_right(a, low) + dot_right(b, high)) * 0.125
    tiles = [along_y[8 * j : 8 * j + 8] for j in range(HALF)]
    stacked = jnp.concatenate(
        [jnp.concatenate(tiles[:3], axis=1), jnp.concatenate(tiles[3:], axis=1)], axis=0
    )
    o, k = rows((24, 16)), lanes((24, 16))
    x, group, zr = o // 8, (o % 8) // 4, o % 4
    xi, zi = (k % 8) // 4, k % 4
    weights = hat(xi - 2 * (x - 1)) * hat(zi - 2 * (zr - 1))
    weights = jnp.where(group == k // 8, weights, 0.0).astype(BF16)
    result = dot_left(weights, stacked) * (1.0 / 64.0)
    out = []
    for jj in range(3):
        for x in range(3):
            out.append(result[8 * x : 8 * x + 8, 128 * jj : 128 * jj + 128])
    return out


def packed_blocks(smoother_ref, reaction_ref, act_ref, sums_ref):
    l, o = rows((128, 128)), lanes((128, 128))
    weights = jnp.where(l // 32 == o % 4, 1.0 / 256.0, 0.0).astype(BF16)
    zero = jnp.zeros((16, 128), F32)
    for a, ref in enumerate((smoother_ref, reaction_ref)):
        for n in range(0, COMP * COMP, 2):
            pair = ref[pl.ds(n * 8, 16), :].astype(F32)
            sums_ref[a, pl.ds(n, 1), :] = jnp.sum(pair[:8], axis=0, keepdims=True)
            sums_ref[a, pl.ds(n + 1, 1), :] = jnp.sum(pair[8:], axis=0, keepdims=True)
        sums_ref[a, pl.ds(144, 16), :] = zero
        sums_ref[a] = dot_right(sums_ref[a], weights)
    s, lane = rows((16, 128)), lanes((16, 128))
    out = zero
    for k in range(8):
        for a in range(2):
            for half in range(2):
                part = sums_ref[a, pl.ds(72 * half + 9 * k, 16), :]
                out = jnp.where(lane // 4 == 4 * k + 2 * a + half, part, out)
    coarse = jnp.broadcast_to(packed_mask_of(act_ref)[:1], (16, 128))
    fine = jnp.broadcast_to(fine_mask_of(act_ref)[:1], (16, 128))
    return jnp.where(s < 9, out, jnp.where(s == 9, coarse, jnp.where(s == 10, fine, 0.0)))


def expand_channel(get_row):
    owner = rows() // 2
    out = jnp.broadcast_to(get_row(0), TILE)
    for zd in range(1, 4):
        out = jnp.where(owner == zd, jnp.broadcast_to(get_row(zd), TILE), out)
    return out


def coarse_product(bx_ref, which, w, vec):
    left = lanes() < 64
    both = [None] * COMP
    for j in range(HALF):
        turned = pltpu.roll(vec[j], 64, 1)
        both[j] = jnp.where(left, vec[j], turned)
        both[j + HALF] = jnp.where(left, turned, vec[j])
    out = []
    for j in range(HALF):
        acc = None
        for d in range(COMP):
            term = bx_ref[w, j * COMP + d, which] * both[d]
            acc = term if acc is None else acc + term
        out.append(acc)
    return out


def coarse_smooth(bx_ref, mask, w, resid):
    prod = coarse_product(bx_ref, 0, w, resid)
    return [mask * a + (1.0 - mask) * r for a, r in zip(prod, resid)]


def expand_blocks(win_ref, bx_ref):
    flat = jnp.concatenate([win_ref[w, r] for w in range(7) for r in range(9)], axis=0)
    pieces = split(flat, 2)
    l, o = rows((128, 256)), lanes((128, 256))
    target = (o // 128) * 8 + ((o % 128) // 64) * 4 + (o % 64) // 16
    for k in range(8):
        weights = jnp.where(l == 16 * k + target, 1.0, 0.0).astype(BF16)
        out = dot(pieces[0], weights) + dot(pieces[1], weights)
        for w in range(7):
            for r in range(9):
                tile = out[(w * 9 + r) * 8 : (w * 9 + r) * 8 + 8]
                bx_ref[w, 9 * k + r, 0] = tile[:, :128]
                bx_ref[w, 9 * k + r, 1] = tile[:, 128:]


def solve_coarse(sc_ref, diff_ref, rhs, win_ref, bx_ref):
    s, lane = rows(), lanes()
    left = lane < 64
    inner_lane = lane % 64
    coeffs = [
        0.25 * jnp.where(left, jnp.full(TILE, diff_ref[j], F32), jnp.full(TILE, diff_ref[j + HALF], F32))
        for j in range(HALF)
    ]
    masks = [win_ref[w, 9] for w in range(7)]
    b = [rhs(w) for w in range(7)]
    v = [coarse_smooth(bx_ref, masks[w], w, b[w]) for w in range(7)]
    for edge in (1, 2):
        mv = [[masks[w] * t for t in v[w]] if v[w] is not None else None for w in range(7)]
        new = [None] * 7
        for w in range(edge, 7 - edge):
            prod = coarse_product(bx_ref, 1, w, v[w])
            resid = []
            for j in range(HALF):
                t = mv[w][j]
                total = mv[w - 1][j] + mv[w + 1][j]
                total = total + jnp.where(s > 0, down(t, 1), 0.0) + jnp.where(s < 7, up(t, 1), 0.0)
                total = total + jnp.where(inner_lane > 0, pltpu.roll(t, 1, 1), 0.0)
                total = total + jnp.where(inner_lane < 63, pltpu.roll(t, 127, 1), 0.0)
                inner = prod[j] + coeffs[j] * (6.0 * v[w][j] - total)
                resid.append(b[w][j] - (masks[w] * inner + (1.0 - masks[w]) * v[w][j]))
            step = coarse_smooth(bx_ref, masks[w], w, resid)
            new[w] = [x + y for x, y in zip(v[w], step)]
        v = new
    return v[2:5]


def prolong(sc_ref, q):
    zd = sc_ref[1]
    o, k = rows((24, 24)), lanes((24, 24))
    group, s = o // 8, o % 8
    z = s % 4
    fx = jnp.where(group == 1, jnp.where(s < 4, -1, 2), s // 4)
    fz = jnp.where(group == 2, jnp.where(z == 0, -1, 4), z) + 4 * zd
    weights = hat(fx - 2 * (k // 8 - 1)) * hat(fz - 2 * (k % 8))
    unused = jnp.logical_and(group == 2, jnp.logical_or(z == 1, z == 2))
    weights = jnp.where(unused, 0.0, weights * 0.0625).astype(BF16)
    stacked = jnp.concatenate([jnp.concatenate(row, axis=1) for row in q], axis=0)
    xz = dot_left(weights, stacked)
    tall = jnp.concatenate([xz[:, 128 * j : 128 * j + 128] for j in range(HALF)], axis=0)
    a, f = rows((128, 256)), lanes((128, 256))
    along = hat(f % 128 - 2 * (a % 64)) * 0.25
    along = jnp.where(a // 64 == f // 128, along, 0.0).astype(BF16)
    fine = dot_right(tall, along)
    groups = []
    for g in range(3):
        tiles = [fine[24 * j + 8 * g : 24 * j + 8 * g + 8] for j in range(HALF)]
        groups.append([t[:, :128] for t in tiles] + [t[:, 128:] for t in tiles])
    return groups


def outside_masks(sc_ref, win_ref):
    zd = sc_ref[1]
    s = rows()
    z = s % 4
    turn = lax.rem(8 - 2 * zd, 8)
    low_x = pltpu.roll(win_ref[CENTRE - 1, 10], turn, 0)[:1]
    high_x = pltpu.roll(win_ref[CENTRE + 1, 10], turn, 0)[:1]
    own = pltpu.roll(win_ref[CENTRE, 10], turn, 0)
    low_z, high_z = own[7:8], own[2:3]
    mask_x = jnp.where(s < 4, jnp.broadcast_to(low_x, TILE), jnp.broadcast_to(high_x, TILE))
    mask_z = jnp.where(
        jnp.logical_and(z == 0, zd > 0),
        jnp.broadcast_to(low_z, TILE),
        jnp.where(jnp.logical_and(z == 3, zd < 3), jnp.broadcast_to(high_z, TILE), 0.0),
    )
    return mask_x, mask_z


def first_kernel(sc_ref, act_ref, src_ref, smoother_ref, u_ref, face_ref, swap_ref):
    mask = fine_mask_of(act_ref)
    u = smooth(smoother_ref, mask, load(src_ref))
    for c in range(COMP):
        u_ref[c] = u[c]
    write_faces(sc_ref, mask, u, face_ref, swap_ref)


def residual(sc_ref, act_ref, diff_ref, src_ref, reaction_ref, u_ref, face_ref, swap_ref):
    mask = fine_mask_of(act_ref)
    u = load(u_ref)
    hx, hz = read_faces(sc_ref, face_ref, swap_ref)
    au = operator(reaction_ref, diff_ref, mask, u, hx, hz)
    return mask, u, [src_ref[c] - au[c] for c in range(COMP)]


def send_kernel(
    with_blocks, sc_ref, act_ref, diff_ref, src_ref, reaction_ref, u_ref, face_ref, swap_ref, *rest
):
    if with_blocks:
        smoother_ref, r_ref, out_ref, sums_ref = rest
    else:
        r_ref, out_ref = rest
    _, _, resid = residual(sc_ref, act_ref, diff_ref, src_ref, reaction_ref, u_ref, face_ref, swap_ref)
    for c in range(COMP):
        r_ref[c] = resid[c]
    tiles = contributions(resid)
    if with_blocks:
        packed = packed_blocks(smoother_ref, reaction_ref, act_ref, sums_ref)
        tiles = tiles + [packed[:8], packed[8:]]
    for n, tile in enumerate(tiles):
        for target in range(16):
            out_ref[target, n] = tile


def gather_kernel(with_blocks, sc_ref, recv_ref, own_ref, far_ref, near_ref):
    right = sc_ref[2] // 2
    s = rows()
    low_half = s < 4
    for j in range(6):
        for jj in range(3):
            parts = []
            for zd in range(4):
                total = None
                for q in range(4):
                    x = j - q
                    if 0 <= x <= 2:
                        tile = recv_ref[q * 4 + zd, jj * 3 + x]
                        total = tile if total is None else total + tile
                parts.append(total)
            m0, m1, m2, m3 = parts
            even = (jnp.where(low_half, m0, down(m2, 4)), jnp.where(low_half, down(m0, 4), m2))
            odd = (jnp.where(low_half, m1, down(m3, 4)), jnp.where(low_half, down(m1, 4), m3))
            for n in range(2):
                own_ref[j, jj + 3 * n] = jnp.where(s < 7, up(even[n], 1), 0.0) + jnp.where(
                    s > 0, down(odd[n], 1), 0.0
                )
    for f in range(4):
        for j in range(HALF):
            far_ref[f * 6 + j] = own_ref[2 * right + f, j]
    for f in range(2):
        for j in range(HALF):
            near_ref[f * 6 + j] = own_ref[4 * right + f, j]
    if with_blocks:
        for e in range(3):
            for zd in range(4):
                for t in range(2):
                    far_ref[24 + e * 8 + zd * 2 + t] = recv_ref[(e + right) * 4 + zd, 9 + t]
        for zd in range(4):
            for t in range(2):
                near_ref[12 + zd * 2 + t] = recv_ref[3 * right * 4 + zd, 9 + t]


def fill_window(sc_ref, recv_ref, far_ref, near_ref, all_ref, win_ref):
    p = sc_ref[2]
    right = p // 2
    zero = jnp.zeros(TILE, F32)
    for n in range(16):
        for r in range(CHANNELS):
            all_ref[n, r] = zero
    for q in range(4):
        for r in range(CHANNELS):
            at = pl.ds(r % 8, 1)
            all_ref[q - p + 7, r] = expand_channel(lambda zd: recv_ref[q * 4 + zd, 9 + r // 8, at, :])
    base = 4 - p + 7 * right
    for e in range(3):
        for r in range(CHANNELS):
            at = pl.ds(r % 8, 1)
            all_ref[e + base, r] = expand_channel(lambda zd: far_ref[24 + e * 8 + zd * 2 + r // 8, at, :])
    place = 11 - p - 5 * right
    for r in range(CHANNELS):
        at = pl.ds(r % 8, 1)
        all_ref[place, r] = expand_channel(lambda zd: near_ref[12 + zd * 2 + r // 8, at, :])
    for w in range(7):
        for r in range(CHANNELS):
            win_ref[w, r] = all_ref[w + 4, r]


def correct_kernel(
    with_blocks,
    sc_ref,
    act_ref,
    diff_ref,
    reaction_ref,
    smoother_ref,
    u_ref,
    r_ref,
    own_ref,
    far_ref,
    near_ref,
    *rest,
):
    if with_blocks:
        recv_ref, new_ref, face_ref, swap_ref, win_ref, rhs_ref, bx_ref, all_ref = rest
        fill_window(sc_ref, recv_ref, far_ref, near_ref, all_ref, win_ref)
    else:
        win_ref, new_ref, face_ref, swap_ref, rhs_ref, bx_ref = rest
    p, brick, bricks = sc_ref[2], sc_ref[3], sc_ref[4]
    right = p // 2
    zero = jnp.zeros(TILE, F32)
    for n in range(16):
        for j in range(HALF):
            rhs_ref[n, j] = zero
    for n in range(6):
        for j in range(HALF):
            rhs_ref[n - p + 6, j] = own_ref[n, j]
    for f in range(4):
        at = f + 4 - p + 6 * right
        for j in range(HALF):
            rhs_ref[at, j] = rhs_ref[at, j] + far_ref[f * 6 + j]
    for f in range(2):
        at = f + 10 - p - 4 * right
        for j in range(HALF):
            rhs_ref[at, j] = rhs_ref[at, j] + near_ref[f * 6 + j]

    def rhs(w):
        place = brick + (w - CENTRE)
        inside = jnp.logical_and(place >= 0, place < bricks)
        return [pick(inside, rhs_ref[w + 4, j], 0.0) for j in range(HALF)]

    expand_blocks(win_ref, bx_ref)
    q = solve_coarse(sc_ref, diff_ref, rhs, win_ref, bx_ref)
    inside, hx, hz = prolong(sc_ref, q)
    mask_x, mask_z = outside_masks(sc_ref, win_ref)
    hx = [mask_x * t for t in hx]
    hz = [mask_z * t for t in hz]
    mask = fine_mask_of(act_ref)
    change = operator(reaction_ref, diff_ref, mask, inside, hx, hz)
    resid = [r_ref[c] - change[c] for c in range(COMP)]
    step = smooth(smoother_ref, mask, resid)
    new = [u_ref[c] + inside[c] + step[c] for c in range(COMP)]
    for c in range(COMP):
        new_ref[c] = new[c]
    write_faces(sc_ref, mask, new, face_ref, swap_ref)


def sweep_kernel(
    sc_ref, act_ref, diff_ref, src_ref, reaction_ref, u_ref, face_ref, swap_ref, smoother_ref,
    new_ref, face_out, swap_out,
):
    mask, u, resid = residual(
        sc_ref, act_ref, diff_ref, src_ref, reaction_ref, u_ref, face_ref, swap_ref
    )
    step = smooth(smoother_ref, mask, resid)
    new = [a + b for a, b in zip(u, step)]
    for c in range(COMP):
        new_ref[c] = new[c]
    write_faces(sc_ref, mask, new, face_out, swap_out)


def last_kernel(
    sc_ref, act_ref, diff_ref, src_ref, reaction_ref, u_ref, face_ref, swap_ref, r_ref
):
    _, _, resid = residual(
        sc_ref, act_ref, diff_ref, src_ref, reaction_ref, u_ref, face_ref, swap_ref
    )
    for c in range(COMP):
        r_ref[c] = resid[c]


SMEM_SPEC = pl.BlockSpec(memory_space=pltpu.SMEM)
VMEM_SPEC = pl.BlockSpec(memory_space=pltpu.VMEM)


def call(kernel, name, scalars, arrays, outs, scratch=()):
    return pl.pallas_call(
        kernel,
        name=name,
        in_specs=[SMEM_SPEC] * len(scalars) + [VMEM_SPEC] * len(arrays),
        out_specs=[VMEM_SPEC] * len(outs),
        out_shape=[jax.ShapeDtypeStruct(shape, F32) for shape in outs],
        scratch_shapes=[pltpu.VMEM(shape, F32) for shape in scratch],
        compiler_params=pltpu.CompilerParams(vmem_limit_bytes=VMEM_LIMIT),
    )(*scalars, *arrays)


VEC = (COMP, 8, 128)
FACE = (8, HALF, 8, 128)
SWAP = (HALF, 8, 128)


def local(bricks, source, reaction, smoother, diffusion, active):
    core = lax.axis_index("core")
    zd = lax.axis_index("gz")
    brick = lax.axis_index(X_AXES)
    scalars = jnp.stack(
        [core, zd, brick % 4, brick, jnp.int32(bricks), core, core, core]
    ).astype(jnp.int32)
    act = active.reshape(4)
    src = source.reshape(VEC)
    react = reaction.reshape(COMP * COMP * 8, 128)
    smoo = smoother.reshape(COMP * COMP * 8, 128)
    groups = bricks // 4

    pairs = [(i, i + 1) for i in range(1, bricks - 1, 2)]
    swap_pairs = pairs + [(b, a) for a, b in pairs]
    far_pairs, near_pairs = [], []
    for i in range(bricks):
        g, p = divmod(i, 4)
        step = 1 if p >= 2 else -1
        if 0 <= g + step < groups:
            far_pairs.append((i, 4 * (g + step) + 3 - p))
            near_pairs.append((i, i + 4 * step))

    def faces(face, swap):
        swap = lax.ppermute(swap, X_AXES, swap_pairs)
        face = lax.all_to_all(face, ("core", "gz"), 0, 0)
        return face, swap

    def to_coarse(message, with_blocks):
        recv = lax.all_to_all(message, ("xc", "core", "gz"), 0, 0)
        far_rows, near_rows = (48, 20) if with_blocks else (24, 12)
        own, far, near = call(
            functools.partial(gather_kernel, with_blocks),
            "gather",
            [scalars],
            [recv],
            [(6, HALF, 8, 128), (far_rows, 8, 128), (near_rows, 8, 128)],
        )
        far = lax.ppermute(far, X_AXES, far_pairs)
        near = lax.ppermute(near, X_AXES, near_pairs)
        return recv, own, far, near

    small = [scalars, act, diffusion]
    u, face, swap = call(first_kernel, "first", [scalars, act], [src, smoo], [VEC, FACE, SWAP])
    face, swap = faces(face, swap)
    resid, message = call(
        functools.partial(send_kernel, True),
        "send",
        small,
        [src, react, u, face, swap, smoo],
        [VEC, (16, 11, 8, 128)],
        [(2, 160, 128)],
    )
    recv, own, far, near = to_coarse(message, True)
    rhs_shape, bx_shape = (16, HALF, 8, 128), (7, 72, 2, 8, 128)
    u, face, swap, window = call(
        functools.partial(correct_kernel, True),
        "correct",
        small,
        [react, smoo, u, resid, own, far, near, recv],
        [VEC, FACE, SWAP, (7, CHANNELS, 8, 128)],
        [rhs_shape, bx_shape, (16, CHANNELS, 8, 128)],
    )
    face, swap = faces(face, swap)
    u, face, swap = call(
        sweep_kernel, "sweep", small, [src, react, u, face, swap, smoo], [VEC, FACE, SWAP]
    )
    face, swap = faces(face, swap)
    resid, message = call(
        functools.partial(send_kernel, False),
        "send",
        small,
        [src, react, u, face, swap],
        [VEC, (16, 9, 8, 128)],
    )
    recv, own, far, near = to_coarse(message, False)
    u, face, swap = call(
        functools.partial(correct_kernel, False),
        "correct",
        small,
        [react, smoo, u, resid, own, far, near, window],
        [VEC, FACE, SWAP],
        [rhs_shape, bx_shape],
    )
    face, swap = faces(face, swap)
    (resid,) = call(last_kernel, "last", small, [src, react, u, face, swap], [VEC])
    return u.reshape(source.shape), resid.reshape(source.shape)


def solution(mesh):
    bricks = mesh.shape["bricks"]
    gz = mesh.shape["gz"]
    inner = Mesh(mesh.devices.reshape(bricks // 4, 2, 2, gz), X_AXES + ("gz",))
    in_specs = (
        P(None, X_AXES, "gz", None),
        P(None, None, X_AXES, "gz", None),
        P(None, None, X_AXES, "gz", None),
        P(),
        P(X_AXES, "gz", None),
    )
    out_specs = (P(None, X_AXES, "gz", None), P(None, X_AXES, "gz", None))
    return jax.shard_map(
        functools.partial(local, bricks),
        mesh=inner,
        in_specs=in_specs,
        out_specs=out_specs,
        check_vma=False,
    )
```

time: 305 us -> 135 us (0.44)
  the two profiles are of different devices: /device:TPU:30 before, /device:TPU:14 now
where the time goes in v1:
time: 135 us; the launch traced here: 134 us
  starting transfers between devices  65.3 us (48%)
  blocking collectives  30.8 us (23%)
  waiting for transfers between devices  19.8 us (15%)
  Pallas kernels  15.1 us (11%)
  local copies, waits for them, and re-layouts  2.39 us (2%)
    all_to_all x2, blocking collectives, to_coarse(): recv = lax.all_to_all(message, ('xc', 'core', 'gz'), 0, 0)  30.8 us
    ppermute x4, starting transfers between devices, faces(): swap = lax.ppermute(swap, X_AXES, swap_pairs)  30.5 us
    all_to_all x4, starting transfers between devices, faces(): face = lax.all_to_all(face, ('core', 'gz'), 0, 0)  19.4 us
    pallas_call x9, Pallas kernels, call(): pl.pallas_call(kernel, name=name, in_specs=[SMEM_SPEC] * len(scalars) + [...  15.1 us
    ppermute x4, waiting for transfers between devices, faces(): swap = lax.ppermute(swap, X_AXES, swap_pairs)  11.4 us
    ppermute x2, starting transfers between devices, to_coarse(): far = lax.ppermute(far, X_AXES, far_pairs)  9.56 us
    ppermute x2, waiting for transfers between devices, to_coarse(): near = lax.ppermute(near, X_AXES, near_pairs)  8.34 us
    ppermute x2, starting transfers between devices, to_coarse(): near = lax.ppermute(near, X_AXES, near_pairs)  5.84 us
  transfers between devices with their start and end apart: 12, of which 6 were waited for; matrix products, arithmetic and copies ran while one was open for 0% of the time, Pallas kernels for 0%

profile of v1, /device:TPU:14, one launch (start us, length us, event | category | flops | bytes accessed | tf_op | source)
XLA Modules:
  0.0 134.2 jit_solution(4497845466085671878)
XLA Ops:
  0.6 0.0 copy-start.3
  0.7 0.1 stack.22.sc_ref
  0.7 0.0 copy-start.5
  0.7 0.7 copy-done.3
  1.4 0.0 copy-done.5
  1.4 0.0 copy-start.1
  1.4 1.0 copy-done.1
  2.4 0.0 copy-start
  2.4 0.0 copy-start.2
  2.4 1.3 first.1
  3.7 4.9 %all-to-all-start = ((f32[8,6,8,128]{3,2,1,0:T(8,128)}), f32[8,6,8,128]{3,2,1,0:T(8,128)S(1)}, u32[]{:S(2)}, u32[]{:S(2)}) async-start(f32[8,6,8,128]{3,2,1,0:T(8,128)} %get-tuple-element.26), calls=%async_computation | async-start | bytes 393216 | tf_op jit(solution)/shard_map/all_to_all | solution.py:571
  8.6 18.7 %collective-permute-start = (f32[6,8,128]{2,1,0:T(8,128)S(1)}, f32[6,8,128]{2,1,0:T(8,128)S(1)}, u32[]{:S(2)}, u32[]{:S(2)}) collective-permute-start(f32[6,8,128]{2,1,0:T(8,128)S(1)} %get-tuple-element.27), channel_id=1, source_target_pairs={{4,8},{12,16},{20,24},{28,32},{36,40},{44,48},{52,56},{60,64},{68,... | collective-permute-start | bytes 73736 | tf_op jit(solution)/shard_map/ppermute | solution.py:570
  27.3 1.5 %collective-permute-done.swap_ref = f32[6,8,128]{2,1,0:T(8,128)S(1)} collective-permute-done((f32[6,8,128]{2,1,0:T(8,128)S(1)}, f32[6,8,128]{2,1,0:T(8,128)S(1)}, u32[]{:S(2)}, u32[]{:S(2)}) %collective-permute-start) | collective-permute-done | bytes 24608 | tf_op jit(solution)/shard_map/ppermute | solution.py:570
  28.8 0.0 all-to-all-done.face_ref
  28.8 0.0 copy-done
  28.8 0.0 copy-done.2
  28.8 0.6 copy-done.6
  29.5 1.4 %send.2 = (f32[12,8,128]{2,1,0:T(8,128)S(1)}, f32[16,11,8,128]{3,2,1,0:T(8,128)S(1)}) custom-call(s32[8]{0:T(128)S(1)} %stack.22.sc_ref, s32[4]{0:T(128)S(1)} %bitcast.28, f32[12]{0:T(128)S(1)} %copy-done.6, f32[12,8,128]{2,1,0:T(8,128)S(1)} %bitcast.22, bf16[1152,128]{1,0:T(8,128)(2,1)S(1)} %bitcast.10, f32[12,8,128]{2,1,0:T(8,128)S(1)} %get-tuple-element.25.u_ref, ...), custom_call_target="tpu_custom_call" | custom-call | tf_op jit(solution)/shard_map/send/pallas_call | solution.py:530
  30.9 16.0 %all_to_all.30.recv_ref.rest_0_ = f32[16,11,8,128]{3,2,1,0:T(8,128)S(1)} all-to-all(f32[16,11,8,128]{3,2,1,0:T(8,128)S(1)} %get-tuple-element.29), channel_id=1, replica_groups=mesh['xg'=64,'xc'=2,'core'=2,'gz'=4] {'xc','core','gz'}, dimensions={0} | all-to-all | bytes 1441792 | tf_op jit(solution)/shard_map/all_to_all | solution.py:575
  46.9 0.6 gather.2
  47.5 5.7 %collective-permute-start.1 = (f32[48,8,128]{2,1,0:T(8,128)S(1)}, f32[48,8,128]{2,1,0:T(8,128)S(1)}, u32[]{:S(2)}, u32[]{:S(2)}) collective-permute-start(f32[48,8,128]{2,1,0:T(8,128)S(1)} %get-tuple-element.31), channel_id=1, source_target_pairs={{8,20},{12,16},{16,12},{20,8},{24,36},{28,32},{32,28},{36,24},{40,... | collective-permute-start | bytes 589832 | tf_op jit(solution)/shard_map/ppermute | solution.py:584
  53.2 2.9 %collective-permute-start.2 = (f32[20,8,128]{2,1,0:T(8,128)S(1)}, f32[20,8,128]{2,1,0:T(8,128)S(1)}, u32[]{:S(2)}, u32[]{:S(2)}) collective-permute-start(f32[20,8,128]{2,1,0:T(8,128)S(1)} %get-tuple-element.32), channel_id=1, source_target_pairs={{8,24},{12,28},{16,0},{20,4},{24,40},{28,44},{32,16},{36,20},{40,5... | collective-permute-start | bytes 245768 | tf_op jit(solution)/shard_map/ppermute | solution.py:585
  56.1 4.4 %collective-permute-done.2.near_ref = f32[20,8,128]{2,1,0:T(8,128)S(1)} collective-permute-done((f32[20,8,128]{2,1,0:T(8,128)S(1)}, f32[20,8,128]{2,1,0:T(8,128)S(1)}, u32[]{:S(2)}, u32[]{:S(2)}) %collective-permute-start.2) | collective-permute-done | bytes 81952 | tf_op jit(solution)/shard_map/ppermute | solution.py:585
  60.5 0.0 collective-permute-done.1.far_ref
  60.6 3.8 %correct.2 = (f32[12,8,128]{2,1,0:T(8,128)S(1)}, f32[8,6,8,128]{3,2,1,0:T(8,128)}, f32[6,8,128]{2,1,0:T(8,128)S(1)}, f32[7,11,8,128]{3,2,1,0:T(8,128)S(1)}) custom-call(s32[8]{0:T(128)S(1)} %stack.22.sc_ref, s32[4]{0:T(128)S(1)} %bitcast.29, f32[12]{0:T(128)S(1)} %copy-done.6, bf16[1152,128]{1,0:T(8,128)(2,1)S(1)} %bitcast.11, ...), custom_call_target="tpu_custom_call" | custom-call | tf_op jit(solution)/shard_map/correct/pallas_call | solution.py:530
  64.3 4.8 %all-to-all-start.2 = ((f32[8,6,8,128]{3,2,1,0:T(8,128)}), f32[8,6,8,128]{3,2,1,0:T(8,128)S(1)}, u32[]{:S(2)}, u32[]{:S(2)}) async-start(f32[8,6,8,128]{3,2,1,0:T(8,128)} %get-tuple-element.34), calls=%async_computation.2 | async-start | bytes 393216 | tf_op jit(solution)/shard_map/all_to_all | solution.py:571
  69.1 4.2 %collective-permute-start.3 = (f32[6,8,128]{2,1,0:T(8,128)S(1)}, f32[6,8,128]{2,1,0:T(8,128)S(1)}, u32[]{:S(2)}, u32[]{:S(2)}) collective-permute-start(f32[6,8,128]{2,1,0:T(8,128)S(1)} %get-tuple-element.35), channel_id=1, source_target_pairs={{4,8},{12,16},{20,24},{28,32},{36,40},{44,48},{52,56},{60,64},{68,... | collective-permute-start | bytes 73736 | tf_op jit(solution)/shard_map/ppermute | solution.py:570
  73.4 3.0 %collective-permute-done.3.swap_ref = f32[6,8,128]{2,1,0:T(8,128)S(1)} collective-permute-done((f32[6,8,128]{2,1,0:T(8,128)S(1)}, f32[6,8,128]{2,1,0:T(8,128)S(1)}, u32[]{:S(2)}, u32[]{:S(2)}) %collective-permute-start.3) | collective-permute-done | bytes 24608 | tf_op jit(solution)/shard_map/ppermute | solution.py:570
  76.4 0.0 all-to-all-done.2.face_ref
  76.4 1.4 %sweep.1 = (f32[12,8,128]{2,1,0:T(8,128)S(1)}, f32[8,6,8,128]{3,2,1,0:T(8,128)}, f32[6,8,128]{2,1,0:T(8,128)S(1)}) custom-call(s32[8]{0:T(128)S(1)} %stack.22.sc_ref, s32[4]{0:T(128)S(1)} %bitcast.30, f32[12]{0:T(128)S(1)} %copy-done.6, f32[12,8,128]{2,1,0:T(8,128)S(1)} %bitcast.23, bf16[1152,128]{1,0:T(8,128)(2,1)S(1)} %bitcast.12, ...), custom_call_target="tpu_custom_call" | custom-call | tf_op jit(solution)/shard_map/sweep/pallas_call | solution.py:530
  77.8 4.8 %all-to-all-start.3 = ((f32[8,6,8,128]{3,2,1,0:T(8,128)}), f32[8,6,8,128]{3,2,1,0:T(8,128)S(1)}, u32[]{:S(2)}, u32[]{:S(2)}) async-start(f32[8,6,8,128]{3,2,1,0:T(8,128)} %get-tuple-element.37), calls=%async_computation.3 | async-start | bytes 393216 | tf_op jit(solution)/shard_map/all_to_all | solution.py:571
  82.6 4.0 %collective-permute-start.4 = (f32[6,8,128]{2,1,0:T(8,128)S(1)}, f32[6,8,128]{2,1,0:T(8,128)S(1)}, u32[]{:S(2)}, u32[]{:S(2)}) collective-permute-start(f32[6,8,128]{2,1,0:T(8,128)S(1)} %get-tuple-element.38), channel_id=1, source_target_pairs={{4,8},{12,16},{20,24},{28,32},{36,40},{44,48},{52,56},{60,64},{68,... | collective-permute-start | bytes 73736 | tf_op jit(solution)/shard_map/ppermute | solution.py:570
  86.6 3.2 %collective-permute-done.4.swap_ref = f32[6,8,128]{2,1,0:T(8,128)S(1)} collective-permute-done((f32[6,8,128]{2,1,0:T(8,128)S(1)}, f32[6,8,128]{2,1,0:T(8,128)S(1)}, u32[]{:S(2)}, u32[]{:S(2)}) %collective-permute-start.4) | collective-permute-done | bytes 24608 | tf_op jit(solution)/shard_map/ppermute | solution.py:570
  89.9 0.0 all-to-all-done.3.face_ref
  89.9 1.1 send.3
  90.9 14.8 %all_to_all.31.recv_ref = f32[16,9,8,128]{3,2,1,0:T(8,128)S(1)} all-to-all(f32[16,9,8,128]{3,2,1,0:T(8,128)S(1)} %get-tuple-element.40), channel_id=1, replica_groups=mesh['xg'=64,'xc'=2,'core'=2,'gz'=4] {'xc','core','gz'}, dimensions={0} | all-to-all | bytes 1179648 | tf_op jit(solution)/shard_map/all_to_all | solution.py:575
  105.7 0.6 gather.3
  106.3 3.9 %collective-permute-start.5 = (f32[24,8,128]{2,1,0:T(8,128)S(1)}, f32[24,8,128]{2,1,0:T(8,128)S(1)}, u32[]{:S(2)}, u32[]{:S(2)}) collective-permute-start(f32[24,8,128]{2,1,0:T(8,128)S(1)} %get-tuple-element.42), channel_id=1, source_target_pairs={{8,20},{12,16},{16,12},{20,8},{24,36},{28,32},{32,28},{36,24},{40,... | collective-permute-start | bytes 294920 | tf_op jit(solution)/shard_map/ppermute | solution.py:584
  110.2 3.0 %collective-permute-start.6 = (f32[12,8,128]{2,1,0:T(8,128)S(1)}, f32[12,8,128]{2,1,0:T(8,128)S(1)}, u32[]{:S(2)}, u32[]{:S(2)}) collective-permute-start(f32[12,8,128]{2,1,0:T(8,128)S(1)} %get-tuple-element.43), channel_id=1, source_target_pairs={{8,24},{12,28},{16,0},{20,4},{24,40},{28,44},{32,16},{36,20},{40,5... | collective-permute-start | bytes 147464 | tf_op jit(solution)/shard_map/ppermute | solution.py:585
  113.2 3.9 %collective-permute-done.6.near_ref = f32[12,8,128]{2,1,0:T(8,128)S(1)} collective-permute-done((f32[12,8,128]{2,1,0:T(8,128)S(1)}, f32[12,8,128]{2,1,0:T(8,128)S(1)}, u32[]{:S(2)}, u32[]{:S(2)}) %collective-permute-start.6) | collective-permute-done | bytes 49184 | tf_op jit(solution)/shard_map/ppermute | solution.py:585
  117.1 0.0 collective-permute-done.5.far_ref
  117.1 3.7 %correct.3 = (f32[12,8,128]{2,1,0:T(8,128)}, f32[8,6,8,128]{3,2,1,0:T(8,128)}, f32[6,8,128]{2,1,0:T(8,128)S(1)}) custom-call(s32[8]{0:T(128)S(1)} %stack.22.sc_ref, s32[4]{0:T(128)S(1)} %bitcast.32, f32[12]{0:T(128)S(1)} %copy-done.6, bf16[1152,128]{1,0:T(8,128)(2,1)S(1)} %bitcast.14, bf16[1152,128]{1,0:T(8,128)(2,1)S(1)} %bitcast.20, ...), custom_call_target="tpu_custom_call" | custom-call | tf_op jit(solution)/shard_map/correct/pallas_call | solution.py:530
  120.7 4.9 %all-to-all-start.5 = ((f32[8,6,8,128]{3,2,1,0:T(8,128)}), f32[8,6,8,128]{3,2,1,0:T(8,128)S(1)}, u32[]{:S(2)}, u32[]{:S(2)}) async-start(f32[8,6,8,128]{3,2,1,0:T(8,128)} %get-tuple-element.46), calls=%async_computation.5 | async-start | bytes 393216 | tf_op jit(solution)/shard_map/all_to_all | solution.py:571
  125.6 3.6 %collective-permute-start.7 = (f32[6,8,128]{2,1,0:T(8,128)S(1)}, f32[6,8,128]{2,1,0:T(8,128)S(1)}, u32[]{:S(2)}, u32[]{:S(2)}) collective-permute-start(f32[6,8,128]{2,1,0:T(8,128)S(1)} %get-tuple-element.47), channel_id=1, source_target_pairs={{4,8},{12,16},{20,24},{28,32},{36,40},{44,48},{52,56},{60,64},{68,... | collective-permute-start | bytes 73736 | tf_op jit(solution)/shard_map/ppermute | solution.py:570
  129.2 3.7 %collective-permute-done.7.swap_ref = f32[6,8,128]{2,1,0:T(8,128)S(1)} collective-permute-done((f32[6,8,128]{2,1,0:T(8,128)S(1)}, f32[6,8,128]{2,1,0:T(8,128)S(1)}, u32[]{:S(2)}, u32[]{:S(2)}) %collective-permute-start.7) | collective-permute-done | bytes 24608 | tf_op jit(solution)/shard_map/ppermute | solution.py:570
  132.9 0.0 all-to-all-done.5.face_ref
  132.9 0.0 copy-done.4
  132.9 1.3 last.1
  (2 shorter events, 0.0 us)
Async XLA Ops:
  0.6 0.8 copy-start.3
  0.7 0.7 copy-start.5
  1.4 1.0 copy-start.1
  2.4 26.4 %copy-start = (bf16[12,12,2,4,128]{4,3,2,1,0:T(4,128)(2,1)S(1)}, bf16[12,12,2,4,128]{4,3,2,1,0:T(4,128)(2,1)}, u32[]{:S(2)}) copy-start(bf16[12,12,2,4,128]{4,3,2,1,0:T(4,128)(2,1)} %param.6) | copy-start | bytes 884740
  2.4 26.4 %copy-start.2 = (bf16[12,12,2,4,128]{4,3,2,1,0:T(4,128)(2,1)S(1)}, bf16[12,12,2,4,128]{4,3,2,1,0:T(4,128)(2,1)}, u32[]{:S(2)}) copy-start(bf16[12,12,2,4,128]{4,3,2,1,0:T(4,128)(2,1)} %param.7) | copy-start | bytes 884740
  3.7 25.1 %all-to-all-start = ((f32[8,6,8,128]{3,2,1,0:T(8,128)}), f32[8,6,8,128]{3,2,1,0:T(8,128)S(1)}, u32[]{:S(2)}, u32[]{:S(2)}) async-start(f32[8,6,8,128]{3,2,1,0:T(8,128)} %get-tuple-element.26), calls=%async_computation | async-start | bytes 393216 | tf_op jit(solution)/shard_map/all_to_all | solution.py:571
  8.6 20.2 %collective-permute-start = (f32[6,8,128]{2,1,0:T(8,128)S(1)}, f32[6,8,128]{2,1,0:T(8,128)S(1)}, u32[]{:S(2)}, u32[]{:S(2)}) collective-permute-start(f32[6,8,128]{2,1,0:T(8,128)S(1)} %get-tuple-element.27), channel_id=1, source_target_pairs={{4,8},{12,16},{20,24},{28,32},{36,40},{44,48},{52,56},{60,64},{68,... | collective-permute-start | bytes 73736 | tf_op jit(solution)/shard_map/ppermute | solution.py:570
  28.8 0.7 copy-start.6
  47.5 13.0 %collective-permute-start.1 = (f32[48,8,128]{2,1,0:T(8,128)S(1)}, f32[48,8,128]{2,1,0:T(8,128)S(1)}, u32[]{:S(2)}, u32[]{:S(2)}) collective-permute-start(f32[48,8,128]{2,1,0:T(8,128)S(1)} %get-tuple-element.31), channel_id=1, source_target_pairs={{8,20},{12,16},{16,12},{20,8},{24,36},{28,32},{32,28},{36,24},{40,... | collective-permute-start | bytes 589832 | tf_op jit(solution)/shard_map/ppermute | solution.py:584
  53.2 7.3 %collective-permute-start.2 = (f32[20,8,128]{2,1,0:T(8,128)S(1)}, f32[20,8,128]{2,1,0:T(8,128)S(1)}, u32[]{:S(2)}, u32[]{:S(2)}) collective-permute-start(f32[20,8,128]{2,1,0:T(8,128)S(1)} %get-tuple-element.32), channel_id=1, source_target_pairs={{8,24},{12,28},{16,0},{20,4},{24,40},{28,44},{32,16},{36,20},{40,5... | collective-permute-start | bytes 245768 | tf_op jit(solution)/shard_map/ppermute | solution.py:585
  64.3 12.0 %all-to-all-start.2 = ((f32[8,6,8,128]{3,2,1,0:T(8,128)}), f32[8,6,8,128]{3,2,1,0:T(8,128)S(1)}, u32[]{:S(2)}, u32[]{:S(2)}) async-start(f32[8,6,8,128]{3,2,1,0:T(8,128)} %get-tuple-element.34), calls=%async_computation.2 | async-start | bytes 393216 | tf_op jit(solution)/shard_map/all_to_all | solution.py:571
  69.1 7.2 %collective-permute-start.3 = (f32[6,8,128]{2,1,0:T(8,128)S(1)}, f32[6,8,128]{2,1,0:T(8,128)S(1)}, u32[]{:S(2)}, u32[]{:S(2)}) collective-permute-start(f32[6,8,128]{2,1,0:T(8,128)S(1)} %get-tuple-element.35), channel_id=1, source_target_pairs={{4,8},{12,16},{20,24},{28,32},{36,40},{44,48},{52,56},{60,64},{68,... | collective-permute-start | bytes 73736 | tf_op jit(solution)/shard_map/ppermute | solution.py:570
  77.8 12.1 %all-to-all-start.3 = ((f32[8,6,8,128]{3,2,1,0:T(8,128)}), f32[8,6,8,128]{3,2,1,0:T(8,128)S(1)}, u32[]{:S(2)}, u32[]{:S(2)}) async-start(f32[8,6,8,128]{3,2,1,0:T(8,128)} %get-tuple-element.37), calls=%async_computation.3 | async-start | bytes 393216 | tf_op jit(solution)/shard_map/all_to_all | solution.py:571
  82.6 7.2 %collective-permute-start.4 = (f32[6,8,128]{2,1,0:T(8,128)S(1)}, f32[6,8,128]{2,1,0:T(8,128)S(1)}, u32[]{:S(2)}, u32[]{:S(2)}) collective-permute-start(f32[6,8,128]{2,1,0:T(8,128)S(1)} %get-tuple-element.38), channel_id=1, source_target_pairs={{4,8},{12,16},{20,24},{28,32},{36,40},{44,48},{52,56},{60,64},{68,... | collective-permute-start | bytes 73736 | tf_op jit(solution)/shard_map/ppermute | solution.py:570
  106.3 10.8 %collective-permute-start.5 = (f32[24,8,128]{2,1,0:T(8,128)S(1)}, f32[24,8,128]{2,1,0:T(8,128)S(1)}, u32[]{:S(2)}, u32[]{:S(2)}) collective-permute-start(f32[24,8,128]{2,1,0:T(8,128)S(1)} %get-tuple-element.42), channel_id=1, source_target_pairs={{8,20},{12,16},{16,12},{20,8},{24,36},{28,32},{32,28},{36,24},{40,... | collective-permute-start | bytes 294920 | tf_op jit(solution)/shard_map/ppermute | solution.py:584
  110.2 6.9 %collective-permute-start.6 = (f32[12,8,128]{2,1,0:T(8,128)S(1)}, f32[12,8,128]{2,1,0:T(8,128)S(1)}, u32[]{:S(2)}, u32[]{:S(2)}) collective-permute-start(f32[12,8,128]{2,1,0:T(8,128)S(1)} %get-tuple-element.43), channel_id=1, source_target_pairs={{8,24},{12,28},{16,0},{20,4},{24,40},{28,44},{32,16},{36,20},{40,5... | collective-permute-start | bytes 147464 | tf_op jit(solution)/shard_map/ppermute | solution.py:585
  120.7 12.1 %copy-start.4 = (f32[12,8,128]{2,1,0:T(8,128)S(1)}, f32[12,8,128]{2,1,0:T(8,128)}, u32[]{:S(2)}) copy-start(f32[12,8,128]{2,1,0:T(8,128)} %get-tuple-element.45.u_ref) | copy-start | bytes 147460
  120.7 12.1 %all-to-all-start.5 = ((f32[8,6,8,128]{3,2,1,0:T(8,128)}), f32[8,6,8,128]{3,2,1,0:T(8,128)S(1)}, u32[]{:S(2)}, u32[]{:S(2)}) async-start(f32[8,6,8,128]{3,2,1,0:T(8,128)} %get-tuple-element.46), calls=%async_computation.5 | async-start | bytes 393216 | tf_op jit(solution)/shard_map/all_to_all | solution.py:571
  125.6 7.2 %collective-permute-start.7 = (f32[6,8,128]{2,1,0:T(8,128)S(1)}, f32[6,8,128]{2,1,0:T(8,128)S(1)}, u32[]{:S(2)}, u32[]{:S(2)}) collective-permute-start(f32[6,8,128]{2,1,0:T(8,128)S(1)} %get-tuple-element.47), channel_id=1, source_target_pairs={{4,8},{12,16},{20,24},{28,32},{36,40},{44,48},{52,56},{60,64},{68,... | collective-permute-start | bytes 73736 | tf_op jit(solution)/shard_map/ppermute | solution.py:570

commit v2 on v1

v2 whole, which is shorter than its diff:
```python
import functools

import jax
import jax.numpy as jnp
from jax import lax
from jax.experimental import pallas as pl
from jax.experimental.pallas import tpu as pltpu
from jax.sharding import Mesh
from jax.sharding import PartitionSpec as P

COMP = 12
HALF = 6
F32 = jnp.float32
BF16 = jnp.bfloat16
X_AXES = ("xg", "xc", "core")
TILE = (8, 128)
CHANNELS = 11
BRICK_TILES = 6
CENTRE = 3
VMEM_LIMIT = 16 * 1024 * 1024


def rows(shape=TILE):
    return lax.broadcasted_iota(jnp.int32, shape, 0)


def lanes(shape=TILE):
    return lax.broadcasted_iota(jnp.int32, shape, 1)


def up(x, by):
    return pltpu.roll(x, 8 - by, 0)


def down(x, by):
    return pltpu.roll(x, by, 0)


def pick(cond, a, b):
    return jnp.where(cond, a, b)


def hat(diff):
    inner = jnp.logical_or(diff == 0, diff == 1)
    outer = jnp.logical_or(diff == -1, diff == 2)
    return jnp.where(inner, 3.0, jnp.where(outer, 1.0, 0.0)).astype(F32)


def split(x, parts):
    pieces = []
    for _ in range(parts):
        piece = x.astype(BF16)
        pieces.append(piece)
        x = x - piece.astype(F32)
    return pieces


def dot(a, b):
    return jnp.dot(a, b, preferred_element_type=F32)


def dot_right(x, weights, parts=3):
    total = None
    for piece in split(x, parts):
        term = dot(piece, weights)
        total = term if total is None else total + term
    return total


def dot_left(weights, x, parts=3):
    total = None
    for piece in split(x, parts):
        term = dot(weights, piece)
        total = term if total is None else total + term
    return total


def fine_mask_of(sc_ref):
    brick = lanes() // 32
    out = jnp.zeros(TILE, F32)
    for b in range(4):
        out = jnp.where(brick == b, sc_ref[8 + b].astype(F32), out)
    return out


def packed_mask_of(sc_ref):
    brick = (lanes() % 64) // 16
    out = jnp.zeros(TILE, F32)
    for b in range(4):
        out = jnp.where(brick == b, sc_ref[8 + b].astype(F32), out)
    return out


def load(ref):
    return [ref[c] for c in range(COMP)]


def block_product(blocks_ref, vec):
    out = []
    for c in range(COMP):
        acc = None
        for d in range(0, COMP, 2):
            pair = blocks_ref[pl.ds((c * COMP + d) * 8, 16), :].astype(F32)
            term = pair[:8] * vec[d] + pair[8:] * vec[d + 1]
            acc = term if acc is None else acc + term
        out.append(acc)
    return out


def smooth(smoother_ref, mask, resid):
    prod = block_product(smoother_ref, resid)
    return [mask * a + (1.0 - mask) * r for a, r in zip(prod, resid)]


def neighbours(mv, hx, hz):
    z = rows() % 4
    lane = lanes()
    total = down(mv, 4) + hx + hz
    total = total + jnp.where(z > 0, down(mv, 1), 0.0) + jnp.where(z < 3, up(mv, 1), 0.0)
    total = total + jnp.where(lane > 0, pltpu.roll(mv, 1, 1), 0.0)
    return total + jnp.where(lane < 127, pltpu.roll(mv, 127, 1), 0.0)


def operator(reaction_ref, diff_ref, mask, vec, hx, hz):
    prod = block_product(reaction_ref, vec)
    out = []
    for c in range(COMP):
        v = vec[c]
        inner = prod[c] + diff_ref[c] * (6.0 * v - neighbours(mask * v, hx[c], hz[c]))
        out.append(mask * inner + (1.0 - mask) * v)
    return out


def x_messages(vec):
    low_half = rows() < 4
    to_high, to_low = [], []
    for j in range(HALF):
        a, b = vec[j], vec[j + HALF]
        to_high.append(jnp.where(low_half, down(a, 4), b))
        to_low.append(jnp.where(low_half, a, down(b, 4)))
    return to_high, to_low


def x_halo(low, high):
    low_half = rows() < 4
    first = [jnp.where(low_half, a, down(b, 4)) for a, b in zip(low, high)]
    second = [jnp.where(low_half, down(a, 4), b) for a, b in zip(low, high)]
    return first + second


def z_messages(vec):
    z = rows() % 4
    to_high, to_low = [], []
    for c in range(3):
        up_tile, down_tile = up(vec[c], 3), vec[c]
        for k in range(1, 4):
            t = vec[c + 3 * k]
            up_tile = jnp.where(z == k, up(t, 3 - k) if k < 3 else t, up_tile)
            down_tile = jnp.where(z == k, down(t, k), down_tile)
        to_high.append(up_tile)
        to_low.append(down_tile)
    return to_high, to_low


def z_halo(zd, low, high):
    z = rows() % 4
    has_low = jnp.logical_and(z == 0, zd > 0)
    has_high = jnp.logical_and(z == 3, zd < 3)
    out = []
    for c in range(COMP):
        k, at = c // 3, c % 3
        a = up(low[at], k) if k else low[at]
        b = down(high[at], 3 - k) if k < 3 else high[at]
        out.append(jnp.where(has_low, a, jnp.where(has_high, b, 0.0)))
    return out


def write_faces(sc_ref, mask, vec, face_ref, swap_ref):
    core, zd = sc_ref[0], sc_ref[1]
    first = core == 0
    mv = [mask * v for v in vec]
    x_high, x_low = x_messages(mv)
    z_high, z_low = z_messages(mv)
    for j in range(HALF):
        in_chip = pick(first, x_high[j], x_low[j])
        swap_ref[j] = pick(first, x_low[j], x_high[j])
        for other in range(4):
            along = pick(other > zd, z_high[j % 3], z_low[j % 3])
            face_ref[other, j] = pick(first, along, in_chip)
            face_ref[4 + other, j] = pick(first, in_chip, along)


def read_faces(sc_ref, face_ref, swap_ref):
    core, zd = sc_ref[0], sc_ref[1]
    first = core == 0
    chip_at = (1 - core) * 4 + zd
    low_at = core * 4 + jnp.maximum(zd - 1, 0)
    high_at = core * 4 + jnp.minimum(zd + 1, 3)
    low, high = [], []
    for j in range(HALF):
        chip, cross = face_ref[chip_at, j], swap_ref[j]
        low.append(pick(first, cross, chip))
        high.append(pick(first, chip, cross))
    hz = z_halo(zd, [face_ref[low_at, c] for c in range(3)], [face_ref[high_at, c] for c in range(3)])
    return x_halo(low, high), hz


def write_layers(sc_ref, mask, vec, resid, chip_ref, cross_ref):
    first = sc_ref[0] == 0
    r_high, r_low = x_messages(resid)
    v_high, v_low = x_messages([mask * v for v in vec])
    for n, (high, low) in enumerate(zip(r_high + v_high + [mask], r_low + v_low + [mask])):
        chip_ref[n] = pick(first, high, low)
        cross_ref[n] = pick(first, low, high)


def restrict(own, beside, above):
    kinds = [own, beside] + ([above] if above is not None else [])
    depth = 8 * len(kinds)
    l, o = rows((128, 128)), lanes((128, 128))
    low = jnp.where(o < 64, hat(l - 2 * o), 0.0).astype(BF16)
    high = jnp.where(o >= 64, hat(l - 2 * (o - 64)), 0.0).astype(BF16)
    a = jnp.concatenate([kind[j] for j in range(HALF) for kind in kinds], axis=0)
    b = jnp.concatenate([kind[j + HALF] for j in range(HALF) for kind in kinds], axis=0)
    along_y = (dot_right(a, low) + dot_right(b, high)) * 0.125
    blocks = [along_y[depth * j : depth * j + depth] for j in range(HALF)]
    stacked = jnp.concatenate(
        [jnp.concatenate(blocks[:3], axis=1), jnp.concatenate(blocks[3:], axis=1)], axis=0
    )
    o, k = rows((8, 2 * depth)), lanes((8, 2 * depth))
    kind, s = (k % depth) // 8, k % 8
    z = s % 4
    outer_x = jnp.where(s < 4, -1, 2)
    in_own = jnp.logical_or(z == 0, z == 3)
    x = jnp.where(kind == 0, s // 4, jnp.where(kind == 1, outer_x, jnp.where(in_own, s // 4, outer_x)))
    fine_z = jnp.where(kind == 2, jnp.where(z < 2, -1, 4), z)
    weights = hat(x) * hat(fine_z - 2 * (o % 4 - 1))
    weights = jnp.where(o // 4 == k // depth, weights, 0.0).astype(BF16)
    result = dot_left(weights, stacked) * (1.0 / 64.0)
    return [result[:, 128 * jj : 128 * jj + 128] for jj in range(3)]


def packed_blocks(smoother_ref, reaction_ref, sc_ref, sums_ref):
    l, o = rows((128, 128)), lanes((128, 128))
    weights = jnp.where(l // 32 == o % 4, 1.0 / 256.0, 0.0).astype(BF16)
    zero = jnp.zeros((16, 128), F32)
    for a, ref in enumerate((smoother_ref, reaction_ref)):
        for n in range(0, COMP * COMP, 2):
            pair = ref[pl.ds(n * 8, 16), :].astype(F32)
            sums_ref[a, pl.ds(n, 1), :] = jnp.sum(pair[:8], axis=0, keepdims=True)
            sums_ref[a, pl.ds(n + 1, 1), :] = jnp.sum(pair[8:], axis=0, keepdims=True)
        sums_ref[a, pl.ds(144, 16), :] = zero
        sums_ref[a] = dot_right(sums_ref[a], weights)
    s, lane = rows((16, 128)), lanes((16, 128))
    out = zero
    for k in range(8):
        for a in range(2):
            for half in range(2):
                part = sums_ref[a, pl.ds(72 * half + 9 * k, 16), :]
                out = jnp.where(lane // 4 == 4 * k + 2 * a + half, part, out)
    coarse = jnp.broadcast_to(packed_mask_of(sc_ref)[:1], (16, 128))
    fine = jnp.broadcast_to(fine_mask_of(sc_ref)[:1], (16, 128))
    return jnp.where(s < 9, out, jnp.where(s == 9, coarse, jnp.where(s == 10, fine, 0.0)))


def expand_channel(get_row):
    owner = rows() // 2
    out = jnp.broadcast_to(get_row(0), TILE)
    for zd in range(1, 4):
        out = jnp.where(owner == zd, jnp.broadcast_to(get_row(zd), TILE), out)
    return out


def slots_of(p):
    right = p // 2
    out = []
    for w in range(7):
        x = p - CENTRE + w
        before = jnp.where(right == 0, x + 7, 7)
        after = jnp.where(right == 1, x, 7)
        out.append(jnp.where(x < 0, before, jnp.where(x > 3, after, x)))
    return out


def coarse_product(bx_ref, which, slot, vec):
    left = lanes() < 64
    both = [None] * COMP
    for j in range(HALF):
        turned = pltpu.roll(vec[j], 64, 1)
        both[j] = jnp.where(left, vec[j], turned)
        both[j + HALF] = jnp.where(left, turned, vec[j])
    out = []
    for j in range(HALF):
        acc = None
        for d in range(COMP):
            term = bx_ref[slot, j * COMP + d, which] * both[d]
            acc = term if acc is None else acc + term
        out.append(acc)
    return out


def coarse_smooth(bx_ref, mask, slot, resid):
    prod = coarse_product(bx_ref, 0, slot, resid)
    return [mask * a + (1.0 - mask) * r for a, r in zip(prod, resid)]


def expand_blocks(win_ref, bx_ref, slots):
    flat = jnp.concatenate([win_ref[n, r] for n in slots for r in range(9)], axis=0)
    pieces = jnp.concatenate(split(flat, 2), axis=1)
    l, o = rows((256, 256)) % 128, lanes((256, 256))
    target = (o // 128) * 8 + ((o % 128) // 64) * 4 + (o % 64) // 16
    for k in range(8):
        weights = jnp.where(l == 16 * k + target, 1.0, 0.0).astype(BF16)
        out = dot(pieces, weights)
        for i, n in enumerate(slots):
            for r in range(9):
                tile = out[(i * 9 + r) * 8 : (i * 9 + r) * 8 + 8]
                bx_ref[n, 9 * k + r, 0] = tile[:, :128]
                bx_ref[n, 9 * k + r, 1] = tile[:, 128:]


def solve_coarse(diff_ref, rhs, slots, win_ref, bx_ref):
    s, lane = rows(), lanes()
    left = lane < 64
    inner_lane = lane % 64
    coeffs = [
        0.25 * jnp.where(left, jnp.full(TILE, diff_ref[j], F32), jnp.full(TILE, diff_ref[j + HALF], F32))
        for j in range(HALF)
    ]
    masks = [win_ref[slots[w], 9] for w in range(7)]
    b = [rhs(w) for w in range(7)]
    v = [coarse_smooth(bx_ref, masks[w], slots[w], b[w]) for w in range(7)]
    for edge in (1, 2):
        mv = [[masks[w] * t for t in v[w]] if v[w] is not None else None for w in range(7)]
        new = [None] * 7
        for w in range(edge, 7 - edge):
            prod = coarse_product(bx_ref, 1, slots[w], v[w])
            resid = []
            for j in range(HALF):
                t = mv[w][j]
                total = mv[w - 1][j] + mv[w + 1][j]
                total = total + jnp.where(s > 0, down(t, 1), 0.0) + jnp.where(s < 7, up(t, 1), 0.0)
                total = total + jnp.where(inner_lane > 0, pltpu.roll(t, 1, 1), 0.0)
                total = total + jnp.where(inner_lane < 63, pltpu.roll(t, 127, 1), 0.0)
                inner = prod[j] + coeffs[j] * (6.0 * v[w][j] - total)
                resid.append(b[w][j] - (masks[w] * inner + (1.0 - masks[w]) * v[w][j]))
            step = coarse_smooth(bx_ref, masks[w], slots[w], resid)
            new[w] = [x + y for x, y in zip(v[w], step)]
        v = new
    return v[2:5]


def prolong(sc_ref, q):
    zd = sc_ref[1]
    o, k = rows((24, 24)), lanes((24, 24))
    group, s = o // 8, o % 8
    z = s % 4
    fx = jnp.where(group == 1, jnp.where(s < 4, -1, 2), s // 4)
    fz = jnp.where(group == 2, jnp.where(z == 0, -1, 4), z) + 4 * zd
    weights = hat(fx - 2 * (k // 8 - 1)) * hat(fz - 2 * (k % 8))
    unused = jnp.logical_and(group == 2, jnp.logical_or(z == 1, z == 2))
    weights = jnp.where(unused, 0.0, weights * 0.0625).astype(BF16)
    stacked = jnp.concatenate([jnp.concatenate(row, axis=1) for row in q], axis=0)
    xz = dot_left(weights, stacked)
    tall = jnp.concatenate([xz[:, 128 * j : 128 * j + 128] for j in range(HALF)], axis=0)
    a, f = rows((128, 256)), lanes((128, 256))
    along = hat(f % 128 - 2 * (a % 64)) * 0.25
    along = jnp.where(a // 64 == f // 128, along, 0.0).astype(BF16)
    fine = dot_right(tall, along)
    groups = []
    for g in range(3):
        tiles = [fine[24 * j + 8 * g : 24 * j + 8 * g + 8] for j in range(HALF)]
        groups.append([t[:, :128] for t in tiles] + [t[:, 128:] for t in tiles])
    return groups


def masks_around(zd, tile):
    own = pltpu.roll(tile, lax.rem(8 - 2 * zd, 8), 0)
    return own[7:8], own[:1], own[2:3]


def outside_masks(zd, tiles):
    s = rows()
    z = s % 4
    _, low_x, _ = masks_around(zd, tiles[0])
    low_z, _, high_z = masks_around(zd, tiles[1])
    _, high_x, _ = masks_around(zd, tiles[2])
    mask_x = jnp.where(s < 4, jnp.broadcast_to(low_x, TILE), jnp.broadcast_to(high_x, TILE))
    mask_z = jnp.where(
        jnp.logical_and(z == 0, zd > 0),
        jnp.broadcast_to(low_z, TILE),
        jnp.where(jnp.logical_and(z == 3, zd < 3), jnp.broadcast_to(high_z, TILE), 0.0),
    )
    return mask_x, mask_z


def layer_masks(zd, tiles):
    s = rows()
    z = s % 4
    around = [masks_around(zd, tile) for tile in tiles]
    below = [jnp.broadcast_to(a[0], TILE) for a in around]
    above = [jnp.broadcast_to(a[2], TILE) for a in around]
    low = jnp.where(z == 0, below[1], jnp.where(s < 4, below[0], below[2]))
    high = jnp.where(z == 3, above[1], jnp.where(s < 4, above[0], above[2]))
    low = jnp.where(zd > 0, low, 0.0)
    high = jnp.where(zd < 3, high, 0.0)
    return jnp.where(z < 2, low, high)


ZEROS = [0.0] * COMP


def first_kernel(sc_ref, src_ref, smoother_ref, u_ref, z_ref):
    mask = fine_mask_of(sc_ref)
    zd = sc_ref[1]
    u = smooth(smoother_ref, mask, load(src_ref))
    for c in range(COMP):
        u_ref[c] = u[c]
    high, low = z_messages([mask * v for v in u])
    for other in range(4):
        for n in range(3):
            z_ref[other, n] = pick(other > zd, high[n], low[n])


def blocks_kernel(sc_ref, smoother_ref, reaction_ref, out_ref, sums_ref):
    packed = packed_blocks(smoother_ref, reaction_ref, sc_ref, sums_ref)
    out_ref[0] = packed[:8]
    out_ref[1] = packed[8:]


def part_kernel(
    sc_ref, diff_ref, src_ref, reaction_ref, u_ref, z_ref, r_ref, chip_ref, cross_ref
):
    mask = fine_mask_of(sc_ref)
    zd = sc_ref[1]
    u = load(u_ref)
    below, above = jnp.maximum(zd - 1, 0), jnp.minimum(zd + 1, 3)
    hz = z_halo(zd, [z_ref[below, n] for n in range(3)], [z_ref[above, n] for n in range(3)])
    au = operator(reaction_ref, diff_ref, mask, u, ZEROS, hz)
    resid = [src_ref[c] - au[c] for c in range(COMP)]
    for c in range(COMP):
        r_ref[c] = resid[c]
    write_layers(sc_ref, mask, u, resid, chip_ref, cross_ref)


def send_kernel(
    again, sc_ref, diff_ref, u_ref, part_ref, chip_ref, cross_ref, extra_ref, r_ref, out_ref
):
    mask = fine_mask_of(sc_ref)
    zd = sc_ref[1]
    first = sc_ref[0] == 0
    low = [pick(first, cross_ref[n], chip_ref[n]) for n in range(13)]
    high = [pick(first, chip_ref[n], cross_ref[n]) for n in range(13)]
    hr = x_halo(low[:6], high[:6])
    hv = x_halo(low[6:12], high[6:12])
    mask_x = jnp.where(rows() < 4, low[12], high[12])
    mv = [mask * u_ref[c] for c in range(COMP)]
    own = [part_ref[c] + mask * (diff_ref[c] * hv[c]) for c in range(COMP)]
    beside = [hr[c] + mask_x * (diff_ref[c] * mv[c]) for c in range(COMP)]
    for c in range(COMP):
        r_ref[c] = own[c]
    above = None
    if again:
        z = rows() % 4
        inner = jnp.logical_or(z == 0, z == 3)
        edge = layer_masks(zd, [extra_ref[n] for n in range(3)])
        above = []
        for c in range(COMP):
            outer = jnp.where(z == 1, down(hv[c], 1), up(hv[c], 1))
            above.append(edge * (diff_ref[c] * jnp.where(inner, mv[c], outer)))
    tiles = restrict(own, beside, above)
    if not again:
        tiles = tiles + [extra_ref[0], extra_ref[1]]
    for n, tile in enumerate(tiles):
        for target in range(16):
            out_ref[target, n] = tile
    if again:
        z_high, z_low = z_messages(mv)
        for n in range(3):
            for other in range(4):
                tile = pick(other > zd, z_high[n], z_low[n])
                for q in range(4):
                    out_ref[q * 4 + other, 3 + n] = tile


def gather_kernel(with_blocks, sc_ref, recv_ref, own_ref, far_ref, near_ref):
    right = sc_ref[2] // 2
    s = rows()
    low_half = s < 4
    for q in range(4):
        for jj in range(3):
            m0, m1, m2, m3 = [recv_ref[q * 4 + zd, jj] for zd in range(4)]
            even = (jnp.where(low_half, m0, down(m2, 4)), jnp.where(low_half, down(m0, 4), m2))
            odd = (jnp.where(low_half, m1, down(m3, 4)), jnp.where(low_half, down(m1, 4), m3))
            for n in range(2):
                own_ref[q, jj + 3 * n] = jnp.where(s < 7, up(even[n], 1), 0.0) + jnp.where(
                    s > 0, down(odd[n], 1), 0.0
                )
    for e in range(3):
        for j in range(HALF):
            far_ref[e * 6 + j] = own_ref[right + e, j]
    for j in range(HALF):
        near_ref[j] = own_ref[3 * right, j]
    if with_blocks:
        for n in range(BRICK_TILES):
            for e in range(3):
                far_ref[18 + e * BRICK_TILES + n] = brick_tile(recv_ref, right + e, n)
            near_ref[6 + n] = brick_tile(recv_ref, 3 * right, n)


def brick_tile(recv_ref, q, n):
    s = rows()
    out = None
    for at in range(8):
        r = 2 * n + at // 4
        row = recv_ref[q * 4 + at % 4, 3 + r // 8, pl.ds(r % 8, 1), :]
        row = jnp.broadcast_to(row, TILE)
        out = row if out is None else jnp.where(s == at, row, out)
    return out


def fill_own(recv_ref, win_ref):
    for r in range(CHANNELS):
        at, tile = pl.ds(r % 8, 1), r // 8
        for q in range(4):
            win_ref[q, r] = expand_channel(lambda zd: recv_ref[q * 4 + zd, 3 + tile, at, :])


def fill_others(far_ref, near_ref, win_ref):
    for r in range(CHANNELS):
        tile, base = r // 2, 4 * (r % 2)
        for e in range(3):
            win_ref[4 + e, r] = expand_channel(
                lambda zd: far_ref[18 + e * BRICK_TILES + tile, pl.ds(base + zd, 1), :]
            )
        win_ref[7, r] = expand_channel(lambda zd: near_ref[6 + tile, pl.ds(base + zd, 1), :])


def correct_kernel(
    again,
    sc_ref,
    diff_ref,
    reaction_ref,
    smoother_ref,
    u_ref,
    r_ref,
    recv_ref,
    own_ref,
    far_ref,
    near_ref,
    *rest,
):
    zd, p, brick, bricks = sc_ref[1], sc_ref[2], sc_ref[3], sc_ref[4]
    if again:
        win_ref, new_ref, face_ref, swap_ref, rhs_ref, bx_ref = rest
    else:
        new_ref, face_ref, swap_ref, win_ref, around_ref, rhs_ref, bx_ref = rest
        fill_own(recv_ref, win_ref)
        fill_others(far_ref, near_ref, win_ref)
    expand_blocks(win_ref, bx_ref, range(8))
    slots = slots_of(p)
    for j in range(HALF):
        for q in range(4):
            rhs_ref[q, j] = own_ref[q, j]
        for e in range(3):
            rhs_ref[4 + e, j] = far_ref[e * 6 + j]
        rhs_ref[7, j] = near_ref[j]

    def rhs(w):
        place = brick + (w - CENTRE)
        inside = jnp.logical_and(place >= 0, place < bricks)
        return [pick(inside, rhs_ref[slots[w], j], 0.0) for j in range(HALF)]

    q = solve_coarse(diff_ref, rhs, slots, win_ref, bx_ref)
    inside, hx, hz = prolong(sc_ref, q)
    fine_masks = [win_ref[slots[CENTRE + n], 10] for n in (-1, 0, 1)]
    if not again:
        for n in range(3):
            around_ref[n] = fine_masks[n]
    mask_x, mask_z = outside_masks(zd, fine_masks)
    hx = [mask_x * t for t in hx]
    hz = [mask_z * t for t in hz]
    mask = fine_mask_of(sc_ref)
    change = operator(reaction_ref, diff_ref, mask, inside, hx, hz)
    resid = [r_ref[c] - change[c] for c in range(COMP)]
    if again:
        below = p * 4 + jnp.maximum(zd - 1, 0)
        above = p * 4 + jnp.minimum(zd + 1, 3)
        halo = z_halo(
            zd, [recv_ref[below, 3 + n] for n in range(3)], [recv_ref[above, 3 + n] for n in range(3)]
        )
        resid = [r + mask * (diff_ref[c] * h) for c, (r, h) in enumerate(zip(resid, halo))]
    step = smooth(smoother_ref, mask, resid)
    new = [u_ref[c] + inside[c] + step[c] for c in range(COMP)]
    for c in range(COMP):
        new_ref[c] = new[c]
    write_faces(sc_ref, mask, new, face_ref, swap_ref)


def residual(sc_ref, diff_ref, src_ref, reaction_ref, u_ref, face_ref, swap_ref):
    mask = fine_mask_of(sc_ref)
    u = load(u_ref)
    hx, hz = read_faces(sc_ref, face_ref, swap_ref)
    au = operator(reaction_ref, diff_ref, mask, u, hx, hz)
    return mask, u, [src_ref[c] - au[c] for c in range(COMP)]


def sweep_kernel(
    sc_ref, diff_ref, src_ref, reaction_ref, u_ref, face_ref, swap_ref, smoother_ref,
    new_ref, part_ref, chip_ref, cross_ref,
):
    mask, u, resid = residual(
        sc_ref, diff_ref, src_ref, reaction_ref, u_ref, face_ref, swap_ref
    )
    step = smooth(smoother_ref, mask, resid)
    new = [a + b for a, b in zip(u, step)]
    au = operator(reaction_ref, diff_ref, mask, new, ZEROS, ZEROS)
    part = [src_ref[c] - au[c] for c in range(COMP)]
    for c in range(COMP):
        new_ref[c] = new[c]
        part_ref[c] = part[c]
    write_layers(sc_ref, mask, new, part, chip_ref, cross_ref)


def last_kernel(
    sc_ref, diff_ref, src_ref, reaction_ref, u_ref, face_ref, swap_ref, r_ref
):
    _, _, resid = residual(
        sc_ref, diff_ref, src_ref, reaction_ref, u_ref, face_ref, swap_ref
    )
    for c in range(COMP):
        r_ref[c] = resid[c]


SMEM_SPEC = pl.BlockSpec(memory_space=pltpu.SMEM)
VMEM_SPEC = pl.BlockSpec(memory_space=pltpu.VMEM)


def call(kernel, name, scalars, arrays, outs, scratch=()):
    return pl.pallas_call(
        kernel,
        name=name,
        in_specs=[SMEM_SPEC] * len(scalars) + [VMEM_SPEC] * len(arrays),
        out_specs=[VMEM_SPEC] * len(outs),
        out_shape=[jax.ShapeDtypeStruct(shape, F32) for shape in outs],
        scratch_shapes=[pltpu.VMEM(shape, F32) for shape in scratch],
        compiler_params=pltpu.CompilerParams(vmem_limit_bytes=VMEM_LIMIT),
    )(*scalars, *arrays)


VEC = (COMP, 8, 128)
FACE = (8, HALF, 8, 128)
SWAP = (HALF, 8, 128)
LAYER = (13, 8, 128)


def local(bricks, source, reaction, smoother, diffusion, active):
    core = lax.axis_index("core")
    zd = lax.axis_index("gz")
    brick = lax.axis_index(X_AXES)
    scalars = jnp.stack(
        [core, zd, brick % 4, brick, jnp.int32(bricks), core, core, core]
    ).astype(jnp.int32)
    scalars = jnp.concatenate([scalars, active.reshape(4)])
    src = source.reshape(VEC)
    react = reaction.reshape(COMP * COMP * 8, 128)
    smoo = smoother.reshape(COMP * COMP * 8, 128)
    groups = bricks // 4

    chip_pairs = [(i, i ^ 1) for i in range(bricks)]
    pairs = [(i, i + 1) for i in range(1, bricks - 1, 2)]
    swap_pairs = pairs + [(b, a) for a, b in pairs]
    far_pairs, near_pairs = [], []
    for i in range(bricks):
        g, p = divmod(i, 4)
        step = 1 if p >= 2 else -1
        if 0 <= g + step < groups:
            far_pairs.append((i, 4 * (g + step) + 3 - p))
            if p in (1, 2):
                near_pairs.append((i, i + 4 * step))

    def faces(face, swap):
        swap = lax.ppermute(swap, X_AXES, swap_pairs)
        face = lax.all_to_all(face, ("core", "gz"), 0, 0)
        return face, swap

    def layers(chip, cross):
        return lax.ppermute(chip, X_AXES, chip_pairs), lax.ppermute(cross, X_AXES, swap_pairs)

    def to_coarse(message, with_blocks):
        recv = lax.all_to_all(message, ("xc", "core", "gz"), 0, 0)
        far_rows, near_rows = (18 + 3 * BRICK_TILES, 6 + BRICK_TILES) if with_blocks else (18, 6)
        own, far, near = call(
            functools.partial(gather_kernel, with_blocks),
            "gather",
            [scalars],
            [recv],
            [(4, HALF, 8, 128), (far_rows, 8, 128), (near_rows, 8, 128)],
        )
        far = lax.ppermute(far, X_AXES, far_pairs)
        near = lax.ppermute(near, X_AXES, near_pairs)
        return recv, own, far, near

    small = [scalars, diffusion]
    u, edges = call(first_kernel, "first", [scalars], [src, smoo], [VEC, (4, 3, 8, 128)])
    (packed,) = call(blocks_kernel, "blocks", [scalars], [smoo, react], [(2, 8, 128)], [(2, 160, 128)])
    edges = lax.all_to_all(edges, "gz", 0, 0)
    part, chip, cross = call(
        part_kernel, "part", small, [src, react, u, edges], [VEC, LAYER, LAYER]
    )
    chip, cross = layers(chip, cross)
    resid, message = call(
        functools.partial(send_kernel, False),
        "send",
        small,
        [u, part, chip, cross, packed],
        [VEC, (16, 5, 8, 128)],
    )
    recv, own, far, near = to_coarse(message, True)
    rhs_shape, bx_shape, win_shape = (8, HALF, 8, 128), (8, 72, 2, 8, 128), (8, CHANNELS, 8, 128)
    u, face, swap, window, around = call(
        functools.partial(correct_kernel, False),
        "correct",
        small,
        [react, smoo, u, resid, recv, own, far, near],
        [VEC, FACE, SWAP, win_shape, (3, 8, 128)],
        [rhs_shape, bx_shape],
    )
    face, swap = faces(face, swap)
    u, part, chip, cross = call(
        sweep_kernel, "sweep", small, [src, react, u, face, swap, smoo], [VEC, VEC, LAYER, LAYER]
    )
    chip, cross = layers(chip, cross)
    resid, message = call(
        functools.partial(send_kernel, True),
        "send",
        small,
        [u, part, chip, cross, around],
        [VEC, (16, 6, 8, 128)],
    )
    recv, own, far, near = to_coarse(message, False)
    u, face, swap = call(
        functools.partial(correct_kernel, True),
        "correct",
        small,
        [react, smoo, u, resid, recv, own, far, near, window],
        [VEC, FACE, SWAP],
        [rhs_shape, bx_shape],
    )
    face, swap = faces(face, swap)
    (resid,) = call(last_kernel, "last", small, [src, react, u, face, swap], [VEC])
    return u.reshape(source.shape), resid.reshape(source.shape)


def solution(mesh):
    bricks = mesh.shape["bricks"]
    gz = mesh.shape["gz"]
    inner = Mesh(mesh.devices.reshape(bricks // 4, 2, 2, gz), X_AXES + ("gz",))
    in_specs = (
        P(None, X_AXES, "gz", None),
        P(None, None, X_AXES, "gz", None),
        P(None, None, X_AXES, "gz", None),
        P(),
        P(X_AXES, "gz", None),
    )
    out_specs = (P(None, X_AXES, "gz", None), P(None, X_AXES, "gz", None))
    return jax.shard_map(
        functools.partial(local, bricks),
        mesh=inner,
        in_specs=in_specs,
        out_specs=out_specs,
        check_vma=False,
    )
```

time: 135 us -> 127 us (0.941)
  starting transfers between devices: 65.3 us -> 59.1 us
  waiting for transfers between devices: 19.8 us -> 16.2 us
  blocking collectives: 30.8 us -> 32.6 us
    ppermute x0 -> x4, starting transfers between devices: none -> 27.5 us  [the longest x2 23.6 us: layers(): lax.ppermute(cross, X_AXES, swap_pairs)]
    ppermute x4 -> x2, starting transfers between devices: 30.5 us -> 9.12 us  [faces(): swap = lax.ppermute(swap, X_AXES, swap_pairs)]
    all_to_all x0 -> x1, blocking collectives: none -> 8.92 us  [local(): edges = lax.all_to_all(edges, 'gz', 0, 0)]
    ppermute x2, waiting for transfers between devices: 8.34 us -> 0.01 us  [to_coarse(): near = lax.ppermute(near, X_AXES, near_pairs)]
    all_to_all x4 -> x2, starting transfers between devices: 19.4 us -> 11.2 us  [faces(): face = lax.all_to_all(face, ('core', 'gz'), 0, 0)]
    ppermute x2, waiting for transfers between devices: 0.01 us -> 7.18 us  [to_coarse(): far = lax.ppermute(far, X_AXES, far_pairs)]
    all_to_all x2, blocking collectives: 30.8 us -> 23.7 us  [to_coarse(): recv = lax.all_to_all(message, ('xc', 'core', 'gz'), 0, 0)]
    ppermute x4 -> x2, waiting for transfers between devices: 11.4 us -> 5.35 us  [faces(): swap = lax.ppermute(swap, X_AXES, swap_pairs)]
  transfers between devices with their start and end apart: 12 -> 12, of which waited for: 6 -> 6; matrix products, arithmetic and copies ran while one was open for 0% -> 0% of each run, Pallas kernels for 0% -> 1%
where the time goes in v2:
time: 127 us; the launch traced here: 126 us
  starting transfers between devices  59.1 us (47%)
  blocking collectives  32.6 us (26%)
  waiting for transfers between devices  16.2 us (13%)
  Pallas kernels  14.8 us (12%)
  local copies, waits for them, and re-layouts  2.56 us (2%)
    all_to_all x2, blocking collectives, to_coarse(): recv = lax.all_to_all(message, ('xc', 'core', 'gz'), 0, 0)  23.7 us
    ppermute x2, starting transfers between devices, layers(): lax.ppermute(cross, X_AXES, swap_pairs)  23.6 us
    pallas_call x11, Pallas kernels, call(): pl.pallas_call(kernel, name=name, in_specs=[SMEM_SPEC] * len(scalars) + [...  14.8 us
    all_to_all x2, starting transfers between devices, faces(): face = lax.all_to_all(face, ('core', 'gz'), 0, 0)  11.2 us
    ppermute x2, starting transfers between devices, to_coarse(): far = lax.ppermute(far, X_AXES, far_pairs)  9.98 us
    ppermute x2, starting transfers between devices, faces(): swap = lax.ppermute(swap, X_AXES, swap_pairs)  9.12 us
    all_to_all x1, blocking collectives, local(): edges = lax.all_to_all(edges, 'gz', 0, 0)  8.92 us
    ppermute x2, waiting for transfers between devices, to_coarse(): far = lax.ppermute(far, X_AXES, far_pairs)  7.18 us
  transfers between devices with their start and end apart: 12, of which 6 were waited for; matrix products, arithmetic and copies ran while one was open for 0% of the time, Pallas kernels for 1%

profile of v2, /device:TPU:14, one launch (start us, length us, event | category | flops | bytes accessed | tf_op | source)
XLA Modules:
  0.0 126.1 jit_solution(2568726352245620431)
XLA Ops:
  0.6 0.0 copy-start
  0.7 0.8 concatenate.3.sc_ref
  1.4 1.0 copy-done.1
  2.4 0.8 copy-done.3
  3.2 0.6 first.1
  3.8 0.0 copy-start.2
  3.8 8.9 %all_to_all.25.z_ref = f32[4,3,8,128]{3,2,1,0:T(8,128)S(1)} all-to-all(f32[4,3,8,128]{3,2,1,0:T(8,128)S(1)} %get-tuple-element.30), channel_id=1, replica_groups=mesh['xg'=64,'xc'=2,'core'=2,'gz'=4] {'gz'}, dimensions={0} | all-to-all | bytes 98304 | tf_op jit(solution)/shard_map/all_to_all | solution.py:707
  12.8 0.0 copy-done
  12.8 0.0 copy-done.6
  12.8 0.7 part.1
  13.4 1.9 %collective-permute-start = (f32[13,8,128]{2,1,0:T(8,128)S(1)}, f32[13,8,128]{2,1,0:T(8,128)S(1)}, u32[]{:S(2)}, u32[]{:S(2)}) collective-permute-start(f32[13,8,128]{2,1,0:T(8,128)S(1)} %get-tuple-element.32), channel_id=1, source_target_pairs={{0,4},{4,0},{8,12},{12,8},{16,20},{20,16},{24,28},{28,24},{32,36},... | collective-permute-start | bytes 159752 | tf_op jit(solution)/shard_map/ppermute | solution.py:688
  15.4 19.0 %collective-permute-start.1 = (f32[13,8,128]{2,1,0:T(8,128)S(1)}, f32[13,8,128]{2,1,0:T(8,128)S(1)}, u32[]{:S(2)}, u32[]{:S(2)}) collective-permute-start(f32[13,8,128]{2,1,0:T(8,128)S(1)} %get-tuple-element.33), channel_id=1, source_target_pairs={{4,8},{12,16},{20,24},{28,32},{36,40},{44,48},{52,56},{60,64},{68,... | collective-permute-start | bytes 159752 | tf_op jit(solution)/shard_map/ppermute | solution.py:688
  34.4 0.0 copy-done.2
  34.4 1.1 blocks.1.extra_ref
  35.5 0.0 collective-permute-done.chip_ref
  35.5 0.7 collective-permute-done.1.cross_ref
  36.2 0.9 send.2
  37.2 11.2 %all_to_all.26.recv_ref = f32[16,5,8,128]{3,2,1,0:T(8,128)S(1)} all-to-all(f32[16,5,8,128]{3,2,1,0:T(8,128)S(1)} %get-tuple-element.35), channel_id=1, replica_groups=mesh['xg'=64,'xc'=2,'core'=2,'gz'=4] {'xc','core','gz'}, dimensions={0} | all-to-all | bytes 655360 | tf_op jit(solution)/shard_map/all_to_all | solution.py:691
  48.3 0.6 gather.2
  48.9 5.5 %collective-permute-start.2 = (f32[36,8,128]{2,1,0:T(8,128)S(1)}, f32[36,8,128]{2,1,0:T(8,128)S(1)}, u32[]{:S(2)}, u32[]{:S(2)}) collective-permute-start(f32[36,8,128]{2,1,0:T(8,128)S(1)} %get-tuple-element.37), channel_id=1, source_target_pairs={{8,20},{12,16},{16,12},{20,8},{24,36},{28,32},{32,28},{36,24},{40,... | collective-permute-start | bytes 442376 | tf_op jit(solution)/shard_map/ppermute | solution.py:700
  54.4 0.7 collective-permute-start.3
  55.1 0.0 collective-permute-done.3.near_ref
  55.1 3.9 %collective-permute-done.2.far_ref = f32[36,8,128]{2,1,0:T(8,128)S(1)} collective-permute-done((f32[36,8,128]{2,1,0:T(8,128)S(1)}, f32[36,8,128]{2,1,0:T(8,128)S(1)}, u32[]{:S(2)}, u32[]{:S(2)}) %collective-permute-start.2) | collective-permute-done | bytes 147488 | tf_op jit(solution)/shard_map/ppermute | solution.py:700
  59.0 3.6 %correct.2 = (f32[12,8,128]{2,1,0:T(8,128)S(1)}, f32[8,6,8,128]{3,2,1,0:T(8,128)}, f32[6,8,128]{2,1,0:T(8,128)S(1)}, f32[8,11,8,128]{3,2,1,0:T(8,128)S(1)}, f32[3,8,128]{2,1,0:T(8,128)S(1)}) custom-call(s32[12]{0:T(128)S(1)} %concatenate.3.sc_ref, f32[12]{0:T(128)S(1)} %copy-done.6, bf16[1152,128]{1,0:T(8,128)(2,1)S(1)} %bitcast.12, ...), custom_call_target="tpu_custom_call" | custom-call | tf_op jit(solution)/shard_map/correct/pallas_call | solution.py:640
  62.6 5.4 %all-to-all-start.2 = ((f32[8,6,8,128]{3,2,1,0:T(8,128)}), f32[8,6,8,128]{3,2,1,0:T(8,128)S(1)}, u32[]{:S(2)}, u32[]{:S(2)}) async-start(f32[8,6,8,128]{3,2,1,0:T(8,128)} %get-tuple-element.40), calls=%async_computation.2 | async-start | bytes 393216 | tf_op jit(solution)/shard_map/all_to_all | solution.py:684
  68.0 4.6 %collective-permute-start.4 = (f32[6,8,128]{2,1,0:T(8,128)S(1)}, f32[6,8,128]{2,1,0:T(8,128)S(1)}, u32[]{:S(2)}, u32[]{:S(2)}) collective-permute-start(f32[6,8,128]{2,1,0:T(8,128)S(1)} %get-tuple-element.41), channel_id=1, source_target_pairs={{4,8},{12,16},{20,24},{28,32},{36,40},{44,48},{52,56},{60,64},{68,... | collective-permute-start | bytes 73736 | tf_op jit(solution)/shard_map/ppermute | solution.py:683
  72.6 2.7 %collective-permute-done.4.swap_ref = f32[6,8,128]{2,1,0:T(8,128)S(1)} collective-permute-done((f32[6,8,128]{2,1,0:T(8,128)S(1)}, f32[6,8,128]{2,1,0:T(8,128)S(1)}, u32[]{:S(2)}, u32[]{:S(2)}) %collective-permute-start.4) | collective-permute-done | bytes 24608 | tf_op jit(solution)/shard_map/ppermute | solution.py:683
  75.3 0.0 all-to-all-done.2.face_ref
  75.3 0.0 copy-done.4
  75.3 0.8 sweep.1
  76.1 1.9 %collective-permute-start.5 = (f32[13,8,128]{2,1,0:T(8,128)S(1)}, f32[13,8,128]{2,1,0:T(8,128)S(1)}, u32[]{:S(2)}, u32[]{:S(2)}) collective-permute-start(f32[13,8,128]{2,1,0:T(8,128)S(1)} %get-tuple-element.44), channel_id=1, source_target_pairs={{0,4},{4,0},{8,12},{12,8},{16,20},{20,16},{24,28},{28,24},{32,36},... | collective-permute-start | bytes 159752 | tf_op jit(solution)/shard_map/ppermute | solution.py:688
  78.1 4.6 %collective-permute-start.6 = (f32[13,8,128]{2,1,0:T(8,128)S(1)}, f32[13,8,128]{2,1,0:T(8,128)S(1)}, u32[]{:S(2)}, u32[]{:S(2)}) collective-permute-start(f32[13,8,128]{2,1,0:T(8,128)S(1)} %get-tuple-element.45), channel_id=1, source_target_pairs={{4,8},{12,16},{20,24},{28,32},{36,40},{44,48},{52,56},{60,64},{68,... | collective-permute-start | bytes 159752 | tf_op jit(solution)/shard_map/ppermute | solution.py:688
  82.6 0.0 collective-permute-done.5.chip_ref
  82.6 3.0 %collective-permute-done.6.cross_ref = f32[13,8,128]{2,1,0:T(8,128)S(1)} collective-permute-done((f32[13,8,128]{2,1,0:T(8,128)S(1)}, f32[13,8,128]{2,1,0:T(8,128)S(1)}, u32[]{:S(2)}, u32[]{:S(2)}) %collective-permute-start.6) | collective-permute-done | bytes 53280 | tf_op jit(solution)/shard_map/ppermute | solution.py:688
  85.6 1.0 send.3
  86.6 12.5 %all_to_all.27.recv_ref = f32[16,6,8,128]{3,2,1,0:T(8,128)S(1)} all-to-all(f32[16,6,8,128]{3,2,1,0:T(8,128)S(1)} %get-tuple-element.48), channel_id=1, replica_groups=mesh['xg'=64,'xc'=2,'core'=2,'gz'=4] {'xc','core','gz'}, dimensions={0} | all-to-all | bytes 786432 | tf_op jit(solution)/shard_map/all_to_all | solution.py:691
  99.2 0.6 gather.3
  99.7 4.5 %collective-permute-start.7 = (f32[18,8,128]{2,1,0:T(8,128)S(1)}, f32[18,8,128]{2,1,0:T(8,128)S(1)}, u32[]{:S(2)}, u32[]{:S(2)}) collective-permute-start(f32[18,8,128]{2,1,0:T(8,128)S(1)} %get-tuple-element.50), channel_id=1, source_target_pairs={{8,20},{12,16},{16,12},{20,8},{24,36},{28,32},{32,28},{36,24},{40,... | collective-permute-start | bytes 221192 | tf_op jit(solution)/shard_map/ppermute | solution.py:700
  104.3 0.7 collective-permute-start.8
  104.9 0.0 collective-permute-done.8.near_ref
  105.0 3.3 %collective-permute-done.7.far_ref = f32[18,8,128]{2,1,0:T(8,128)S(1)} collective-permute-done((f32[18,8,128]{2,1,0:T(8,128)S(1)}, f32[18,8,128]{2,1,0:T(8,128)S(1)}, u32[]{:S(2)}, u32[]{:S(2)}) %collective-permute-start.7) | collective-permute-done | bytes 73760 | tf_op jit(solution)/shard_map/ppermute | solution.py:700
  108.2 3.6 %correct.3 = (f32[12,8,128]{2,1,0:T(8,128)}, f32[8,6,8,128]{3,2,1,0:T(8,128)}, f32[6,8,128]{2,1,0:T(8,128)S(1)}) custom-call(s32[12]{0:T(128)S(1)} %concatenate.3.sc_ref, f32[12]{0:T(128)S(1)} %copy-done.6, bf16[1152,128]{1,0:T(8,128)(2,1)S(1)} %bitcast.14, bf16[1152,128]{1,0:T(8,128)(2,1)S(1)} %bitcast.20, f32[12,8,128]{2,1,0:T(8,128)S(1)} %get-tuple-element.42.u_ref, ...), custom_call_target="tpu_custom_call" | custom-call | tf_op jit(solution)/shard_map/correct/pallas_call | solution.py:640
  111.8 5.8 %all-to-all-start.4 = ((f32[8,6,8,128]{3,2,1,0:T(8,128)}), f32[8,6,8,128]{3,2,1,0:T(8,128)S(1)}, u32[]{:S(2)}, u32[]{:S(2)}) async-start(f32[8,6,8,128]{3,2,1,0:T(8,128)} %get-tuple-element.54), calls=%async_computation.4 | async-start | bytes 393216 | tf_op jit(solution)/shard_map/all_to_all | solution.py:684
  117.6 4.6 %collective-permute-start.9 = (f32[6,8,128]{2,1,0:T(8,128)S(1)}, f32[6,8,128]{2,1,0:T(8,128)S(1)}, u32[]{:S(2)}, u32[]{:S(2)}) collective-permute-start(f32[6,8,128]{2,1,0:T(8,128)S(1)} %get-tuple-element.55), channel_id=1, source_target_pairs={{4,8},{12,16},{20,24},{28,32},{36,40},{44,48},{52,56},{60,64},{68,... | collective-permute-start | bytes 73736 | tf_op jit(solution)/shard_map/ppermute | solution.py:683
  122.2 2.7 %collective-permute-done.9.swap_ref = f32[6,8,128]{2,1,0:T(8,128)S(1)} collective-permute-done((f32[6,8,128]{2,1,0:T(8,128)S(1)}, f32[6,8,128]{2,1,0:T(8,128)S(1)}, u32[]{:S(2)}, u32[]{:S(2)}) %collective-permute-start.9) | collective-permute-done | bytes 24608 | tf_op jit(solution)/shard_map/ppermute | solution.py:683
  124.8 0.0 all-to-all-done.4.face_ref
  124.8 0.0 copy-done.5
  124.8 1.3 %last.1 = f32[12,8,128]{2,1,0:T(8,128)} custom-call(s32[12]{0:T(128)S(1)} %concatenate.3.sc_ref, f32[12]{0:T(128)S(1)} %copy-done.6, f32[12,8,128]{2,1,0:T(8,128)S(1)} %bitcast.24, bf16[1152,128]{1,0:T(8,128)(2,1)S(1)} %bitcast.15, f32[12,8,128]{2,1,0:T(8,128)S(1)} %copy-done.5, f32[8,6,8,128]{3,2,1,0:T(8,128)S(1)} %all-to-all-done.4.face_ref, ...), custom_call_target="tpu_custom_call" | custom-call | tf_op jit(solution)/shard_map/last/pallas_call | solution.py:640
  (5 shorter events, 0.0 us)
Async XLA Ops:
  0.6 12.1 %copy-start = (bf16[12,12,2,4,128]{4,3,2,1,0:T(4,128)(2,1)S(1)}, bf16[12,12,2,4,128]{4,3,2,1,0:T(4,128)(2,1)}, u32[]{:S(2)}) copy-start(bf16[12,12,2,4,128]{4,3,2,1,0:T(4,128)(2,1)} %param.6) | copy-start | bytes 884740
  1.4 1.0 copy-start.1
  2.4 0.8 copy-start.3
  3.2 9.6 %copy-start.6 = (f32[12]{0:T(128)S(1)}, f32[12]{0:T(128)}, u32[]{:S(2)}) copy-start(f32[12]{0:T(128)} %diff_ref.13) | copy-start | bytes 148
  3.8 30.6 %copy-start.2 = (bf16[12,12,2,4,128]{4,3,2,1,0:T(4,128)(2,1)S(1)}, bf16[12,12,2,4,128]{4,3,2,1,0:T(4,128)(2,1)}, u32[]{:S(2)}) copy-start(bf16[12,12,2,4,128]{4,3,2,1,0:T(4,128)(2,1)} %param.7) | copy-start | bytes 884740
  13.4 22.1 %collective-permute-start = (f32[13,8,128]{2,1,0:T(8,128)S(1)}, f32[13,8,128]{2,1,0:T(8,128)S(1)}, u32[]{:S(2)}, u32[]{:S(2)}) collective-permute-start(f32[13,8,128]{2,1,0:T(8,128)S(1)} %get-tuple-element.32), channel_id=1, source_target_pairs={{0,4},{4,0},{8,12},{12,8},{16,20},{20,16},{24,28},{28,24},{32,36},... | collective-permute-start | bytes 159752 | tf_op jit(solution)/shard_map/ppermute | solution.py:688
  15.4 20.9 %collective-permute-start.1 = (f32[13,8,128]{2,1,0:T(8,128)S(1)}, f32[13,8,128]{2,1,0:T(8,128)S(1)}, u32[]{:S(2)}, u32[]{:S(2)}) collective-permute-start(f32[13,8,128]{2,1,0:T(8,128)S(1)} %get-tuple-element.33), channel_id=1, source_target_pairs={{4,8},{12,16},{20,24},{28,32},{36,40},{44,48},{52,56},{60,64},{68,... | collective-permute-start | bytes 159752 | tf_op jit(solution)/shard_map/ppermute | solution.py:688
  48.9 10.1 %collective-permute-start.2 = (f32[36,8,128]{2,1,0:T(8,128)S(1)}, f32[36,8,128]{2,1,0:T(8,128)S(1)}, u32[]{:S(2)}, u32[]{:S(2)}) collective-permute-start(f32[36,8,128]{2,1,0:T(8,128)S(1)} %get-tuple-element.37), channel_id=1, source_target_pairs={{8,20},{12,16},{16,12},{20,8},{24,36},{28,32},{32,28},{36,24},{40,... | collective-permute-start | bytes 442376 | tf_op jit(solution)/shard_map/ppermute | solution.py:700
  54.4 0.7 collective-permute-start.3
  62.6 12.7 %copy-start.4 = (f32[12,2,4,128]{3,2,1,0:T(4,128)S(1)}, f32[12,2,4,128]{3,2,1,0:T(4,128)}, u32[]{:S(2)}) copy-start(f32[12,2,4,128]{3,2,1,0:T(4,128)} %param.5) | copy-start | bytes 147460
  62.6 12.7 %all-to-all-start.2 = ((f32[8,6,8,128]{3,2,1,0:T(8,128)}), f32[8,6,8,128]{3,2,1,0:T(8,128)S(1)}, u32[]{:S(2)}, u32[]{:S(2)}) async-start(f32[8,6,8,128]{3,2,1,0:T(8,128)} %get-tuple-element.40), calls=%async_computation.2 | async-start | bytes 393216 | tf_op jit(solution)/shard_map/all_to_all | solution.py:684
  68.0 7.2 %collective-permute-start.4 = (f32[6,8,128]{2,1,0:T(8,128)S(1)}, f32[6,8,128]{2,1,0:T(8,128)S(1)}, u32[]{:S(2)}, u32[]{:S(2)}) collective-permute-start(f32[6,8,128]{2,1,0:T(8,128)S(1)} %get-tuple-element.41), channel_id=1, source_target_pairs={{4,8},{12,16},{20,24},{28,32},{36,40},{44,48},{52,56},{60,64},{68,... | collective-permute-start | bytes 73736 | tf_op jit(solution)/shard_map/ppermute | solution.py:683
  76.1 6.5 %collective-permute-start.5 = (f32[13,8,128]{2,1,0:T(8,128)S(1)}, f32[13,8,128]{2,1,0:T(8,128)S(1)}, u32[]{:S(2)}, u32[]{:S(2)}) collective-permute-start(f32[13,8,128]{2,1,0:T(8,128)S(1)} %get-tuple-element.44), channel_id=1, source_target_pairs={{0,4},{4,0},{8,12},{12,8},{16,20},{20,16},{24,28},{28,24},{32,36},... | collective-permute-start | bytes 159752 | tf_op jit(solution)/shard_map/ppermute | solution.py:688
  78.1 7.6 %collective-permute-start.6 = (f32[13,8,128]{2,1,0:T(8,128)S(1)}, f32[13,8,128]{2,1,0:T(8,128)S(1)}, u32[]{:S(2)}, u32[]{:S(2)}) collective-permute-start(f32[13,8,128]{2,1,0:T(8,128)S(1)} %get-tuple-element.45), channel_id=1, source_target_pairs={{4,8},{12,16},{20,24},{28,32},{36,40},{44,48},{52,56},{60,64},{68,... | collective-permute-start | bytes 159752 | tf_op jit(solution)/shard_map/ppermute | solution.py:688
  99.7 8.5 %collective-permute-start.7 = (f32[18,8,128]{2,1,0:T(8,128)S(1)}, f32[18,8,128]{2,1,0:T(8,128)S(1)}, u32[]{:S(2)}, u32[]{:S(2)}) collective-permute-start(f32[18,8,128]{2,1,0:T(8,128)S(1)} %get-tuple-element.50), channel_id=1, source_target_pairs={{8,20},{12,16},{16,12},{20,8},{24,36},{28,32},{32,28},{36,24},{40,... | collective-permute-start | bytes 221192 | tf_op jit(solution)/shard_map/ppermute | solution.py:700
  104.3 0.7 collective-permute-start.8
  111.8 13.1 %copy-start.5 = (f32[12,8,128]{2,1,0:T(8,128)S(1)}, f32[12,8,128]{2,1,0:T(8,128)}, u32[]{:S(2)}) copy-start(f32[12,8,128]{2,1,0:T(8,128)} %get-tuple-element.53.u_ref) | copy-start | bytes 147460
  111.8 13.1 %all-to-all-start.4 = ((f32[8,6,8,128]{3,2,1,0:T(8,128)}), f32[8,6,8,128]{3,2,1,0:T(8,128)S(1)}, u32[]{:S(2)}, u32[]{:S(2)}) async-start(f32[8,6,8,128]{3,2,1,0:T(8,128)} %get-tuple-element.54), calls=%async_computation.4 | async-start | bytes 393216 | tf_op jit(solution)/shard_map/all_to_all | solution.py:684
  117.6 7.2 %collective-permute-start.9 = (f32[6,8,128]{2,1,0:T(8,128)S(1)}, f32[6,8,128]{2,1,0:T(8,128)S(1)}, u32[]{:S(2)}, u32[]{:S(2)}) collective-permute-start(f32[6,8,128]{2,1,0:T(8,128)S(1)} %get-tuple-element.55), channel_id=1, source_target_pairs={{4,8},{12,16},{20,24},{28,32},{36,40},{44,48},{52,56},{60,64},{68,... | collective-permute-start | bytes 73736 | tf_op jit(solution)/shard_map/ppermute | solution.py:683

commit v3 on v2

--- a/solution.py
+++ b/solution.py
@@ -75,19 +75,19 @@
     return total
 
 
-def fine_mask_of(sc_ref):
+def fine_mask_of(here):
     brick = lanes() // 32
     out = jnp.zeros(TILE, F32)
     for b in range(4):
-        out = jnp.where(brick == b, sc_ref[8 + b].astype(F32), out)
-    return out
-
-
-def packed_mask_of(sc_ref):
+        out = jnp.where(brick == b, here[5 + b], out)
+    return out
+
+
+def packed_mask_of(here):
     brick = (lanes() % 64) // 16
     out = jnp.zeros(TILE, F32)
     for b in range(4):
-        out = jnp.where(brick == b, sc_ref[8 + b].astype(F32), out)
+        out = jnp.where(brick == b, here[5 + b], out)
     return out
 
 
@@ -175,8 +175,8 @@
     return out
 
 
-def write_faces(sc_ref, mask, vec, face_ref, swap_ref):
-    core, zd = sc_ref[0], sc_ref[1]
+def write_faces(here, mask, vec, face_ref, swap_ref):
+    core, zd = here[0], here[1]
     first = core == 0
     mv = [mask * v for v in vec]
     x_high, x_low = x_messages(mv)
@@ -190,8 +190,8 @@
             face_ref[4 + other, j] = pick(first, in_chip, along)
 
 
-def read_faces(sc_ref, face_ref, swap_ref):
-    core, zd = sc_ref[0], sc_ref[1]
+def read_faces(here, face_ref, swap_ref):
+    core, zd = here[0], here[1]
     first = core == 0
     chip_at = (1 - core) * 4 + zd
     low_at = core * 4 + jnp.maximum(zd - 1, 0)
@@ -205,8 +205,8 @@
     return x_halo(low, high), hz
 
 
-def write_layers(sc_ref, mask, vec, resid, chip_ref, cross_ref):
-    first = sc_ref[0] == 0
+def write_layers(here, mask, vec, resid, chip_ref, cross_ref):
+    first = here[0] == 0
     r_high, r_low = x_messages(resid)
     v_high, v_low = x_messages([mask * v for v in vec])
     for n, (high, low) in enumerate(zip(r_high + v_high + [mask], r_low + v_low + [mask])):
@@ -240,7 +240,7 @@
     return [result[:, 128 * jj : 128 * jj + 128] for jj in range(3)]
 
 
-def packed_blocks(smoother_ref, reaction_ref, sc_ref, sums_ref):
+def packed_blocks(smoother_ref, reaction_ref, here, sums_ref):
     l, o = rows((128, 128)), lanes((128, 128))
     weights = jnp.where(l // 32 == o % 4, 1.0 / 256.0, 0.0).astype(BF16)
     zero = jnp.zeros((16, 128), F32)
@@ -258,8 +258,8 @@
             for half in range(2):
                 part = sums_ref[a, pl.ds(72 * half + 9 * k, 16), :]
                 out = jnp.where(lane // 4 == 4 * k + 2 * a + half, part, out)
-    coarse = jnp.broadcast_to(packed_mask_of(sc_ref)[:1], (16, 128))
-    fine = jnp.broadcast_to(fine_mask_of(sc_ref)[:1], (16, 128))
+    coarse = jnp.broadcast_to(packed_mask_of(here)[:1], (16, 128))
+    fine = jnp.broadcast_to(fine_mask_of(here)[:1], (16, 128))
     return jnp.where(s < 9, out, jnp.where(s == 9, coarse, jnp.where(s == 10, fine, 0.0)))
 
 
@@ -324,7 +324,7 @@
     left = lane < 64
     inner_lane = lane % 64
     coeffs = [
-        0.25 * jnp.where(left, jnp.full(TILE, diff_ref[j], F32), jnp.full(TILE, diff_ref[j + HALF], F32))
+        0.25 * jnp.where(left, diff_ref[j], diff_ref[j + HALF])
         for j in range(HALF)
     ]
     masks = [win_ref[slots[w], 9] for w in range(7)]
@@ -350,8 +350,8 @@
     return v[2:5]
 
 
-def prolong(sc_ref, q):
-    zd = sc_ref[1]
+def prolong(here, q):
+    zd = here[1]
     o, k = rows((24, 24)), lanes((24, 24))
     group, s = o // 8, o % 8
     z = s % 4
@@ -410,9 +410,9 @@
 ZEROS = [0.0] * COMP
 
 
-def first_kernel(sc_ref, src_ref, smoother_ref, u_ref, z_ref):
-    mask = fine_mask_of(sc_ref)
-    zd = sc_ref[1]
+def first_kernel(here, src_ref, smoother_ref, u_ref, z_ref):
+    mask = fine_mask_of(here)
+    zd = here[1]
     u = smooth(smoother_ref, mask, load(src_ref))
     for c in range(COMP):
         u_ref[c] = u[c]
@@ -422,17 +422,17 @@
             z_ref[other, n] = pick(other > zd, high[n], low[n])
 
 
-def blocks_kernel(sc_ref, smoother_ref, reaction_ref, out_ref, sums_ref):
-    packed = packed_blocks(smoother_ref, reaction_ref, sc_ref, sums_ref)
+def blocks_kernel(here, smoother_ref, reaction_ref, out_ref, sums_ref):
+    packed = packed_blocks(smoother_ref, reaction_ref, here, sums_ref)
     out_ref[0] = packed[:8]
     out_ref[1] = packed[8:]
 
 
 def part_kernel(
-    sc_ref, diff_ref, src_ref, reaction_ref, u_ref, z_ref, r_ref, chip_ref, cross_ref
+    here, diff_ref, src_ref, reaction_ref, u_ref, z_ref, r_ref, chip_ref, cross_ref
 ):
-    mask = fine_mask_of(sc_ref)
-    zd = sc_ref[1]
+    mask = fine_mask_of(here)
+    zd = here[1]
     u = load(u_ref)
     below, above = jnp.maximum(zd - 1, 0), jnp.minimum(zd + 1, 3)
     hz = z_halo(zd, [z_ref[below, n] for n in range(3)], [z_ref[above, n] for n in range(3)])
@@ -440,15 +440,15 @@
     resid = [src_ref[c] - au[c] for c in range(COMP)]
     for c in range(COMP):
         r_ref[c] = resid[c]
-    write_layers(sc_ref, mask, u, resid, chip_ref, cross_ref)
+    write_layers(here, mask, u, resid, chip_ref, cross_ref)
 
 
 def send_kernel(
-    again, sc_ref, diff_ref, u_ref, part_ref, chip_ref, cross_ref, extra_ref, r_ref, out_ref
+    again, here, diff_ref, u_ref, part_ref, chip_ref, cross_ref, extra_ref, r_ref, out_ref
 ):
-    mask = fine_mask_of(sc_ref)
-    zd = sc_ref[1]
-    first = sc_ref[0] == 0
+    mask = fine_mask_of(here)
+    zd = here[1]
+    first = here[0] == 0
     low = [pick(first, cross_ref[n], chip_ref[n]) for n in range(13)]
     high = [pick(first, chip_ref[n], cross_ref[n]) for n in range(13)]
     hr = x_halo(low[:6], high[:6])
@@ -483,8 +483,8 @@
                     out_ref[q * 4 + other, 3 + n] = tile
 
 
-def gather_kernel(with_blocks, sc_ref, recv_ref, own_ref, far_ref, near_ref):
-    right = sc_ref[2] // 2
+def gather_kernel(with_blocks, here, recv_ref, own_ref, far_ref, near_ref):
+    right = here[2] // 2
     s = rows()
     low_half = s < 4
     for q in range(4):
@@ -538,7 +538,7 @@
 
 def correct_kernel(
     again,
-    sc_ref,
+    here,
     diff_ref,
     reaction_ref,
     smoother_ref,
@@ -550,7 +550,7 @@
     near_ref,
     *rest,
 ):
-    zd, p, brick, bricks = sc_ref[1], sc_ref[2], sc_ref[3], sc_ref[4]
+    zd, p, brick, bricks = here[1], here[2], here[3], here[4]
     if again:
         win_ref, new_ref, face_ref, swap_ref, rhs_ref, bx_ref = rest
     else:
@@ -572,7 +572,7 @@
         return [pick(inside, rhs_ref[slots[w], j], 0.0) for j in range(HALF)]
 
     q = solve_coarse(diff_ref, rhs, slots, win_ref, bx_ref)
-    inside, hx, hz = prolong(sc_ref, q)
+    inside, hx, hz = prolong(here, q)
     fine_masks = [win_ref[slots[CENTRE + n], 10] for n in (-1, 0, 1)]
     if not again:
         for n in range(3):
@@ -580,7 +580,7 @@
     mask_x, mask_z = outside_masks(zd, fine_masks)
     hx = [mask_x * t for t in hx]
     hz = [mask_z * t for t in hz]
-    mask = fine_mask_of(sc_ref)
+    mask = fine_mask_of(here)
     change = operator(reaction_ref, diff_ref, mask, inside, hx, hz)
     resid = [r_ref[c] - change[c] for c in range(COMP)]
     if again:
@@ -594,23 +594,23 @@
     new = [u_ref[c] + inside[c] + step[c] for c in range(COMP)]
     for c in range(COMP):
         new_ref[c] = new[c]
-    write_faces(sc_ref, mask, new, face_ref, swap_ref)
-
-
-def residual(sc_ref, diff_ref, src_ref, reaction_ref, u_ref, face_ref, swap_ref):
-    mask = fine_mask_of(sc_ref)
+    write_faces(here, mask, new, face_ref, swap_ref)
+
+
+def residual(here, diff_ref, src_ref, reaction_ref, u_ref, face_ref, swap_ref):
+    mask = fine_mask_of(here)
     u = load(u_ref)
-    hx, hz = read_faces(sc_ref, face_ref, swap_ref)
+    hx, hz = read_faces(here, face_ref, swap_ref)
     au = operator(reaction_ref, diff_ref, mask, u, hx, hz)
     return mask, u, [src_ref[c] - au[c] for c in range(COMP)]
 
 
 def sweep_kernel(
-    sc_ref, diff_ref, src_ref, reaction_ref, u_ref, face_ref, swap_ref, smoother_ref,
+    here, diff_ref, src_ref, reaction_ref, u_ref, face_ref, swap_ref, smoother_ref,
     new_ref, part_ref, chip_ref, cross_ref,
 ):
     mask, u, resid = residual(
-        sc_ref, diff_ref, src_ref, reaction_ref, u_ref, face_ref, swap_ref
+        here, diff_ref, src_ref, reaction_ref, u_ref, face_ref, swap_ref
     )
     step = smooth(smoother_ref, mask, resid)
     new = [a + b for a, b in zip(u, step)]
@@ -619,33 +619,50 @@
     for c in range(COMP):
         new_ref[c] = new[c]
         part_ref[c] = part[c]
-    write_layers(sc_ref, mask, new, part, chip_ref, cross_ref)
+    write_layers(here, mask, new, part, chip_ref, cross_ref)
 
 
 def last_kernel(
-    sc_ref, diff_ref, src_ref, reaction_ref, u_ref, face_ref, swap_ref, r_ref
+    here, diff_ref, src_ref, reaction_ref, u_ref, face_ref, swap_ref, r_ref
 ):
     _, _, resid = residual(
-        sc_ref, diff_ref, src_ref, reaction_ref, u_ref, face_ref, swap_ref
+        here, diff_ref, src_ref, reaction_ref, u_ref, face_ref, swap_ref
     )
     for c in range(COMP):
         r_ref[c] = resid[c]
 
 
-SMEM_SPEC = pl.BlockSpec(memory_space=pltpu.SMEM)
 VMEM_SPEC = pl.BlockSpec(memory_space=pltpu.VMEM)
 
 
-def call(kernel, name, scalars, arrays, outs, scratch=()):
+def place():
+    core = lax.axis_index("core")
+    p = lax.axis_index("xc") * 2 + core
+    brick = lax.axis_index("xg") * 4 + p
+    return [core, lax.axis_index("gz"), p, brick, lax.axis_size("xg") * 4]
+
+
+def spread(row_ref):
+    return [
+        jnp.broadcast_to(row_ref[:, n : n + 1], TILE).astype(F32) for n in range(row_ref.shape[1])
+    ]
+
+
+def call(kernel, name, small, arrays, outs, scratch=()):
+    def body(*refs):
+        tiles = [spread(ref) for ref in refs[: len(small)]]
+        position = place() + (tiles[0] if tiles else [])
+        kernel(position, *tiles[1:], *refs[len(small) :])
+
     return pl.pallas_call(
-        kernel,
+        body,
         name=name,
-        in_specs=[SMEM_SPEC] * len(scalars) + [VMEM_SPEC] * len(arrays),
+        in_specs=[VMEM_SPEC] * (len(small) + len(arrays)),
         out_specs=[VMEM_SPEC] * len(outs),
         out_shape=[jax.ShapeDtypeStruct(shape, F32) for shape in outs],
         scratch_shapes=[pltpu.VMEM(shape, F32) for shape in scratch],
         compiler_params=pltpu.CompilerParams(vmem_limit_bytes=VMEM_LIMIT),
-    )(*scalars, *arrays)
+    )(*small, *arrays)
 
 
 VEC = (COMP, 8, 128)
@@ -655,13 +672,8 @@
 
 
 def local(bricks, source, reaction, smoother, diffusion, active):
-    core = lax.axis_index("core")
-    zd = lax.axis_index("gz")
-    brick = lax.axis_index(X_AXES)
-    scalars = jnp.stack(
-        [core, zd, brick % 4, brick, jnp.int32(bricks), core, core, core]
-    ).astype(jnp.int32)
-    scalars = jnp.concatenate([scalars, active.reshape(4)])
+    act = active.reshape(1, 4)
+    small = [act, diffusion.reshape(1, COMP)]
     src = source.reshape(VEC)
     react = reaction.reshape(COMP * COMP * 8, 128)
     smoo = smoother.reshape(COMP * COMP * 8, 128)
@@ -693,7 +705,7 @@
         own, far, near = call(
             functools.partial(gather_kernel, with_blocks),
             "gather",
-            [scalars],
+            [],
             [recv],
             [(4, HALF, 8, 128), (far_rows, 8, 128), (near_rows, 8, 128)],
         )
@@ -701,9 +713,8 @@
         near = lax.ppermute(near, X_AXES, near_pairs)
         return recv, own, far, near
 
-    small = [scalars, diffusion]
-    u, edges = call(first_kernel, "first", [scalars], [src, smoo], [VEC, (4, 3, 8, 128)])
-    (packed,) = call(blocks_kernel, "blocks", [scalars], [smoo, react], [(2, 8, 128)], [(2, 160, 128)])
+    u, edges = call(first_kernel, "first", [act], [src, smoo], [VEC, (4, 3, 8, 128)])
+    (packed,) = call(blocks_kernel, "blocks", [act], [smoo, react], [(2, 8, 128)], [(2, 160, 128)])
     edges = lax.all_to_all(edges, "gz", 0, 0)
     part, chip, cross = call(
         part_kernel, "part", small, [src, react, u, edges], [VEC, LAYER, LAYER]

time: 127 us -> 122 us (0.961)
  Pallas kernels: 14.8 us -> 9.03 us
    pallas_call x11, Pallas kernels: 14.8 us -> 9.03 us  [call(): pl.pallas_call(body, name=name, in_specs=[VMEM_SPEC] * (len(small) + len(...]
  transfers between devices with their start and end apart: 12 -> 12, of which waited for: 6 -> 6; matrix products, arithmetic and copies ran while one was open for 0% -> 0% of each run, Pallas kernels for 1% -> 0%
where the time goes in v3:
time: 122 us; the launch traced here: 121 us
  starting transfers between devices  59.2 us (49%)
  blocking collectives  32.6 us (27%)
  waiting for transfers between devices  16.8 us (14%)
  Pallas kernels  9.03 us (7%)
  local copies, waits for them, and re-layouts  2.48 us (2%)
    all_to_all x2, blocking collectives, to_coarse(): recv = lax.all_to_all(message, ('xc', 'core', 'gz'), 0, 0)  23.7 us
    ppermute x2, starting transfers between devices, layers(): lax.ppermute(cross, X_AXES, swap_pairs)  23.6 us
    all_to_all x2, starting transfers between devices, faces(): face = lax.all_to_all(face, ('core', 'gz'), 0, 0)  11.2 us
    ppermute x2, starting transfers between devices, to_coarse(): far = lax.ppermute(far, X_AXES, far_pairs)  9.97 us
    ppermute x2, starting transfers between devices, faces(): swap = lax.ppermute(swap, X_AXES, swap_pairs)  9.26 us
    pallas_call x11, Pallas kernels, call(): pl.pallas_call(body, name=name, in_specs=[VMEM_SPEC] * (len(small) + len(...  9.03 us
    all_to_all x1, blocking collectives, local(): edges = lax.all_to_all(edges, 'gz', 0, 0)  8.92 us
    ppermute x2, waiting for transfers between devices, to_coarse(): far = lax.ppermute(far, X_AXES, far_pairs)  7.19 us
  transfers between devices with their start and end apart: 12, of which 6 were waited for; matrix products, arithmetic and copies ran while one was open for 0% of the time, Pallas kernels for 0%

profile of v3, /device:TPU:14, one launch (start us, length us, event | category | flops | bytes accessed | tf_op | source)
XLA Modules:
  0.0 121.0 jit_solution(16591804390093764110)
XLA Ops:
  0.6 0.0 copy-start
  0.6 0.0 copy-start.1
  0.7 1.0 copy-done.1
  1.6 0.8 copy-done.3
  2.4 0.7 copy-done.6
  3.1 0.1 first.1
  3.2 0.0 copy-start.2
  3.2 8.9 %all_to_all.25.refs_5_ = f32[4,3,8,128]{3,2,1,0:T(8,128)S(1)} all-to-all(f32[4,3,8,128]{3,2,1,0:T(8,128)S(1)} %get-tuple-element.30), channel_id=1, replica_groups=mesh['xg'=64,'xc'=2,'core'=2,'gz'=4] {'gz'}, dimensions={0} | all-to-all | bytes 98304 | tf_op jit(solution)/shard_map/all_to_all | solution.py:718
  12.1 0.0 copy-done
  12.1 0.0 copy-done.8
  12.1 0.2 part.1
  12.3 1.9 %collective-permute-start = (f32[13,8,128]{2,1,0:T(8,128)S(1)}, f32[13,8,128]{2,1,0:T(8,128)S(1)}, u32[]{:S(2)}, u32[]{:S(2)}) collective-permute-start(f32[13,8,128]{2,1,0:T(8,128)S(1)} %get-tuple-element.32), channel_id=1, source_target_pairs={{0,4},{4,0},{8,12},{12,8},{16,20},{20,16},{24,28},{28,24},{32,36},... | collective-permute-start | bytes 159752 | tf_op jit(solution)/shard_map/ppermute | solution.py:700
  14.3 19.0 %collective-permute-start.1 = (f32[13,8,128]{2,1,0:T(8,128)S(1)}, f32[13,8,128]{2,1,0:T(8,128)S(1)}, u32[]{:S(2)}, u32[]{:S(2)}) collective-permute-start(f32[13,8,128]{2,1,0:T(8,128)S(1)} %get-tuple-element.33), channel_id=1, source_target_pairs={{4,8},{12,16},{20,24},{28,32},{36,40},{44,48},{52,56},{60,64},{68,... | collective-permute-start | bytes 159752 | tf_op jit(solution)/shard_map/ppermute | solution.py:700
  33.3 0.0 copy-done.2
  33.3 0.5 blocks.1.refs_6_
  33.8 0.0 collective-permute-done.refs_4_
  33.9 1.3 %collective-permute-done.1.refs_5_ = f32[13,8,128]{2,1,0:T(8,128)S(1)} collective-permute-done((f32[13,8,128]{2,1,0:T(8,128)S(1)}, f32[13,8,128]{2,1,0:T(8,128)S(1)}, u32[]{:S(2)}, u32[]{:S(2)}) %collective-permute-start.1) | collective-permute-done | bytes 53280 | tf_op jit(solution)/shard_map/ppermute | solution.py:700
  35.1 0.4 send.2
  35.6 11.2 %all_to_all.26.refs_0_.refs_6_ = f32[16,5,8,128]{3,2,1,0:T(8,128)S(1)} all-to-all(f32[16,5,8,128]{3,2,1,0:T(8,128)S(1)} %get-tuple-element.35), channel_id=1, replica_groups=mesh['xg'=64,'xc'=2,'core'=2,'gz'=4] {'xc','core','gz'}, dimensions={0} | all-to-all | bytes 655360 | tf_op jit(solution)/shard_map/all_to_all | solution.py:703
  46.7 0.1 gather.2
  46.8 5.5 %collective-permute-start.2 = (f32[36,8,128]{2,1,0:T(8,128)S(1)}, f32[36,8,128]{2,1,0:T(8,128)S(1)}, u32[]{:S(2)}, u32[]{:S(2)}) collective-permute-start(f32[36,8,128]{2,1,0:T(8,128)S(1)} %get-tuple-element.37), channel_id=1, source_target_pairs={{8,20},{12,16},{16,12},{20,8},{24,36},{28,32},{32,28},{36,24},{40,... | collective-permute-start | bytes 442376 | tf_op jit(solution)/shard_map/ppermute | solution.py:712
  52.3 0.7 collective-permute-start.3
  52.9 0.0 collective-permute-done.3.refs_9_
  52.9 3.9 %collective-permute-done.2.refs_8_ = f32[36,8,128]{2,1,0:T(8,128)S(1)} collective-permute-done((f32[36,8,128]{2,1,0:T(8,128)S(1)}, f32[36,8,128]{2,1,0:T(8,128)S(1)}, u32[]{:S(2)}, u32[]{:S(2)}) %collective-permute-start.2) | collective-permute-done | bytes 147488 | tf_op jit(solution)/shard_map/ppermute | solution.py:712
  56.9 3.0 %correct.2 = (f32[12,8,128]{2,1,0:T(8,128)S(1)}, f32[8,6,8,128]{3,2,1,0:T(8,128)}, f32[6,8,128]{2,1,0:T(8,128)S(1)}, f32[8,11,8,128]{3,2,1,0:T(8,128)S(1)}, f32[3,8,128]{2,1,0:T(8,128)S(1)}) custom-call(s32[1,4]{1,0:T(1,128)S(1)} %bitcast.27, f32[1,12]{1,0:T(1,128)S(1)} %bitcast.34, bf16[1152,128]{1,0:T(8,128)(2,1)S(1)} %bitcast.9, ...), custom_call_target="tpu_custom_call" | custom-call | tf_op jit(solution)/shard_map/correct/pallas_call | solution.py:657
  59.9 5.4 %all-to-all-start.2 = ((f32[8,6,8,128]{3,2,1,0:T(8,128)}), f32[8,6,8,128]{3,2,1,0:T(8,128)S(1)}, u32[]{:S(2)}, u32[]{:S(2)}) async-start(f32[8,6,8,128]{3,2,1,0:T(8,128)} %get-tuple-element.40), calls=%async_computation.2 | async-start | bytes 393216 | tf_op jit(solution)/shard_map/all_to_all | solution.py:696
  65.3 4.7 %collective-permute-start.4 = (f32[6,8,128]{2,1,0:T(8,128)S(1)}, f32[6,8,128]{2,1,0:T(8,128)S(1)}, u32[]{:S(2)}, u32[]{:S(2)}) collective-permute-start(f32[6,8,128]{2,1,0:T(8,128)S(1)} %get-tuple-element.41), channel_id=1, source_target_pairs={{4,8},{12,16},{20,24},{28,32},{36,40},{44,48},{52,56},{60,64},{68,... | collective-permute-start | bytes 73736 | tf_op jit(solution)/shard_map/ppermute | solution.py:695
  70.0 2.7 %collective-permute-done.4.refs_6_ = f32[6,8,128]{2,1,0:T(8,128)S(1)} collective-permute-done((f32[6,8,128]{2,1,0:T(8,128)S(1)}, f32[6,8,128]{2,1,0:T(8,128)S(1)}, u32[]{:S(2)}, u32[]{:S(2)}) %collective-permute-start.4) | collective-permute-done | bytes 24608 | tf_op jit(solution)/shard_map/ppermute | solution.py:695
  72.7 0.0 all-to-all-done.2.refs_5_
  72.7 0.0 copy-done.4
  72.7 0.0 copy-done.7
  72.7 0.4 sweep.1
  73.1 1.9 %collective-permute-start.5 = (f32[13,8,128]{2,1,0:T(8,128)S(1)}, f32[13,8,128]{2,1,0:T(8,128)S(1)}, u32[]{:S(2)}, u32[]{:S(2)}) collective-permute-start(f32[13,8,128]{2,1,0:T(8,128)S(1)} %get-tuple-element.44), channel_id=1, source_target_pairs={{0,4},{4,0},{8,12},{12,8},{16,20},{20,16},{24,28},{28,24},{32,36},... | collective-permute-start | bytes 159752 | tf_op jit(solution)/shard_map/ppermute | solution.py:700
  75.0 4.6 %collective-permute-start.6 = (f32[13,8,128]{2,1,0:T(8,128)S(1)}, f32[13,8,128]{2,1,0:T(8,128)S(1)}, u32[]{:S(2)}, u32[]{:S(2)}) collective-permute-start(f32[13,8,128]{2,1,0:T(8,128)S(1)} %get-tuple-element.45), channel_id=1, source_target_pairs={{4,8},{12,16},{20,24},{28,32},{36,40},{44,48},{52,56},{60,64},{68,... | collective-permute-start | bytes 159752 | tf_op jit(solution)/shard_map/ppermute | solution.py:700
  79.6 0.0 collective-permute-done.5.refs_4_
  79.6 3.0 %collective-permute-done.6.refs_5_ = f32[13,8,128]{2,1,0:T(8,128)S(1)} collective-permute-done((f32[13,8,128]{2,1,0:T(8,128)S(1)}, f32[13,8,128]{2,1,0:T(8,128)S(1)}, u32[]{:S(2)}, u32[]{:S(2)}) %collective-permute-start.6) | collective-permute-done | bytes 53280 | tf_op jit(solution)/shard_map/ppermute | solution.py:700
  82.6 0.5 send.3
  83.1 12.5 %all_to_all.27.refs_0_.refs_6_ = f32[16,6,8,128]{3,2,1,0:T(8,128)S(1)} all-to-all(f32[16,6,8,128]{3,2,1,0:T(8,128)S(1)} %get-tuple-element.48), channel_id=1, replica_groups=mesh['xg'=64,'xc'=2,'core'=2,'gz'=4] {'xc','core','gz'}, dimensions={0} | all-to-all | bytes 786432 | tf_op jit(solution)/shard_map/all_to_all | solution.py:703
  95.7 4.5 %collective-permute-start.7 = (f32[18,8,128]{2,1,0:T(8,128)S(1)}, f32[18,8,128]{2,1,0:T(8,128)S(1)}, u32[]{:S(2)}, u32[]{:S(2)}) collective-permute-start(f32[18,8,128]{2,1,0:T(8,128)S(1)} %get-tuple-element.50), channel_id=1, source_target_pairs={{8,20},{12,16},{16,12},{20,8},{24,36},{28,32},{32,28},{36,24},{40,... | collective-permute-start | bytes 221192 | tf_op jit(solution)/shard_map/ppermute | solution.py:712
  100.2 0.7 collective-permute-start.8
  100.8 0.0 collective-permute-done.8.refs_9_
  100.9 3.3 %collective-permute-done.7.refs_8_ = f32[18,8,128]{2,1,0:T(8,128)S(1)} collective-permute-done((f32[18,8,128]{2,1,0:T(8,128)S(1)}, f32[18,8,128]{2,1,0:T(8,128)S(1)}, u32[]{:S(2)}, u32[]{:S(2)}) %collective-permute-start.7) | collective-permute-done | bytes 73760 | tf_op jit(solution)/shard_map/ppermute | solution.py:712
  104.1 3.0 %correct.3 = (f32[12,8,128]{2,1,0:T(8,128)}, f32[8,6,8,128]{3,2,1,0:T(8,128)}, f32[6,8,128]{2,1,0:T(8,128)S(1)}) custom-call(s32[1,4]{1,0:T(1,128)S(1)} %bitcast.30, f32[1,12]{1,0:T(1,128)S(1)} %bitcast.37, bf16[1152,128]{1,0:T(8,128)(2,1)S(1)} %bitcast.11, bf16[1152,128]{1,0:T(8,128)(2,1)S(1)} %bitcast.17, ...), custom_call_target="tpu_custom_call" | custom-call | tf_op jit(solution)/shard_map/correct/pallas_call | solution.py:657
  107.1 5.8 %all-to-all-start.4 = ((f32[8,6,8,128]{3,2,1,0:T(8,128)}), f32[8,6,8,128]{3,2,1,0:T(8,128)S(1)}, u32[]{:S(2)}, u32[]{:S(2)}) async-start(f32[8,6,8,128]{3,2,1,0:T(8,128)} %get-tuple-element.54), calls=%async_computation.4 | async-start | bytes 393216 | tf_op jit(solution)/shard_map/all_to_all | solution.py:696
  112.9 4.6 %collective-permute-start.9 = (f32[6,8,128]{2,1,0:T(8,128)S(1)}, f32[6,8,128]{2,1,0:T(8,128)S(1)}, u32[]{:S(2)}, u32[]{:S(2)}) collective-permute-start(f32[6,8,128]{2,1,0:T(8,128)S(1)} %get-tuple-element.55), channel_id=1, source_target_pairs={{4,8},{12,16},{20,24},{28,32},{36,40},{44,48},{52,56},{60,64},{68,... | collective-permute-start | bytes 73736 | tf_op jit(solution)/shard_map/ppermute | solution.py:695
  117.5 2.7 %collective-permute-done.9.refs_6_ = f32[6,8,128]{2,1,0:T(8,128)S(1)} collective-permute-done((f32[6,8,128]{2,1,0:T(8,128)S(1)}, f32[6,8,128]{2,1,0:T(8,128)S(1)}, u32[]{:S(2)}, u32[]{:S(2)}) %collective-permute-start.9) | collective-permute-done | bytes 24608 | tf_op jit(solution)/shard_map/ppermute | solution.py:695
  120.2 0.0 all-to-all-done.4.refs_5_
  120.2 0.8 last.1
  (8 shorter events, 0.1 us)
Async XLA Ops:
  0.6 11.5 %copy-start = (bf16[12,12,2,4,128]{4,3,2,1,0:T(4,128)(2,1)S(1)}, bf16[12,12,2,4,128]{4,3,2,1,0:T(4,128)(2,1)}, u32[]{:S(2)}) copy-start(bf16[12,12,2,4,128]{4,3,2,1,0:T(4,128)(2,1)} %param.6) | copy-start | bytes 884740
  0.6 1.0 copy-start.1
  1.6 0.8 copy-start.3
  2.4 0.7 copy-start.6
  3.1 9.0 %copy-start.8 = (f32[12]{0:T(128)S(1)}, f32[12]{0:T(128)}, u32[]{:S(2)}) copy-start(f32[12]{0:T(128)} %param.8) | copy-start | bytes 148
  3.2 30.1 %copy-start.2 = (bf16[12,12,2,4,128]{4,3,2,1,0:T(4,128)(2,1)S(1)}, bf16[12,12,2,4,128]{4,3,2,1,0:T(4,128)(2,1)}, u32[]{:S(2)}) copy-start(bf16[12,12,2,4,128]{4,3,2,1,0:T(4,128)(2,1)} %param.7) | copy-start | bytes 884740
  12.3 21.5 %collective-permute-start = (f32[13,8,128]{2,1,0:T(8,128)S(1)}, f32[13,8,128]{2,1,0:T(8,128)S(1)}, u32[]{:S(2)}, u32[]{:S(2)}) collective-permute-start(f32[13,8,128]{2,1,0:T(8,128)S(1)} %get-tuple-element.32), channel_id=1, source_target_pairs={{0,4},{4,0},{8,12},{12,8},{16,20},{20,16},{24,28},{28,24},{32,36},... | collective-permute-start | bytes 159752 | tf_op jit(solution)/shard_map/ppermute | solution.py:700
  14.3 20.9 %collective-permute-start.1 = (f32[13,8,128]{2,1,0:T(8,128)S(1)}, f32[13,8,128]{2,1,0:T(8,128)S(1)}, u32[]{:S(2)}, u32[]{:S(2)}) collective-permute-start(f32[13,8,128]{2,1,0:T(8,128)S(1)} %get-tuple-element.33), channel_id=1, source_target_pairs={{4,8},{12,16},{20,24},{28,32},{36,40},{44,48},{52,56},{60,64},{68,... | collective-permute-start | bytes 159752 | tf_op jit(solution)/shard_map/ppermute | solution.py:700
  46.8 10.1 %collective-permute-start.2 = (f32[36,8,128]{2,1,0:T(8,128)S(1)}, f32[36,8,128]{2,1,0:T(8,128)S(1)}, u32[]{:S(2)}, u32[]{:S(2)}) collective-permute-start(f32[36,8,128]{2,1,0:T(8,128)S(1)} %get-tuple-element.37), channel_id=1, source_target_pairs={{8,20},{12,16},{16,12},{20,8},{24,36},{28,32},{32,28},{36,24},{40,... | collective-permute-start | bytes 442376 | tf_op jit(solution)/shard_map/ppermute | solution.py:712
  52.3 0.7 collective-permute-start.3
  59.9 12.8 %copy-start.4 = (f32[12,2,4,128]{3,2,1,0:T(4,128)S(1)}, f32[12,2,4,128]{3,2,1,0:T(4,128)}, u32[]{:S(2)}) copy-start(f32[12,2,4,128]{3,2,1,0:T(4,128)} %param.5) | copy-start | bytes 147460
  59.9 12.8 %all-to-all-start.2 = ((f32[8,6,8,128]{3,2,1,0:T(8,128)}), f32[8,6,8,128]{3,2,1,0:T(8,128)S(1)}, u32[]{:S(2)}, u32[]{:S(2)}) async-start(f32[8,6,8,128]{3,2,1,0:T(8,128)} %get-tuple-element.40), calls=%async_computation.2 | async-start | bytes 393216 | tf_op jit(solution)/shard_map/all_to_all | solution.py:696
  65.3 7.4 %copy-start.7 = (s32[1,1,4]{2,1,0:T(1,128)S(1)}, s32[1,1,4]{2,1,0:T(1,128)}, u32[]{:S(2)}) copy-start(s32[1,1,4]{2,1,0:T(1,128)} %param.9) | copy-start | bytes 52
  65.3 7.4 %collective-permute-start.4 = (f32[6,8,128]{2,1,0:T(8,128)S(1)}, f32[6,8,128]{2,1,0:T(8,128)S(1)}, u32[]{:S(2)}, u32[]{:S(2)}) collective-permute-start(f32[6,8,128]{2,1,0:T(8,128)S(1)} %get-tuple-element.41), channel_id=1, source_target_pairs={{4,8},{12,16},{20,24},{28,32},{36,40},{44,48},{52,56},{60,64},{68,... | collective-permute-start | bytes 73736 | tf_op jit(solution)/shard_map/ppermute | solution.py:695
  73.1 6.5 %collective-permute-start.5 = (f32[13,8,128]{2,1,0:T(8,128)S(1)}, f32[13,8,128]{2,1,0:T(8,128)S(1)}, u32[]{:S(2)}, u32[]{:S(2)}) collective-permute-start(f32[13,8,128]{2,1,0:T(8,128)S(1)} %get-tuple-element.44), channel_id=1, source_target_pairs={{0,4},{4,0},{8,12},{12,8},{16,20},{20,16},{24,28},{28,24},{32,36},... | collective-permute-start | bytes 159752 | tf_op jit(solution)/shard_map/ppermute | solution.py:700
  75.0 7.6 %collective-permute-start.6 = (f32[13,8,128]{2,1,0:T(8,128)S(1)}, f32[13,8,128]{2,1,0:T(8,128)S(1)}, u32[]{:S(2)}, u32[]{:S(2)}) collective-permute-start(f32[13,8,128]{2,1,0:T(8,128)S(1)} %get-tuple-element.45), channel_id=1, source_target_pairs={{4,8},{12,16},{20,24},{28,32},{36,40},{44,48},{52,56},{60,64},{68,... | collective-permute-start | bytes 159752 | tf_op jit(solution)/shard_map/ppermute | solution.py:700
  95.7 8.5 %collective-permute-start.7 = (f32[18,8,128]{2,1,0:T(8,128)S(1)}, f32[18,8,128]{2,1,0:T(8,128)S(1)}, u32[]{:S(2)}, u32[]{:S(2)}) collective-permute-start(f32[18,8,128]{2,1,0:T(8,128)S(1)} %get-tuple-element.50), channel_id=1, source_target_pairs={{8,20},{12,16},{16,12},{20,8},{24,36},{28,32},{32,28},{36,24},{40,... | collective-permute-start | bytes 221192 | tf_op jit(solution)/shard_map/ppermute | solution.py:712
  100.2 0.7 collective-permute-start.8
  107.1 13.1 %copy-start.5 = (f32[12,8,128]{2,1,0:T(8,128)S(1)}, f32[12,8,128]{2,1,0:T(8,128)}, u32[]{:S(2)}) copy-start(f32[12,8,128]{2,1,0:T(8,128)} %get-tuple-element.53.refs_4_) | copy-start | bytes 147460
  107.1 13.1 %all-to-all-start.4 = ((f32[8,6,8,128]{3,2,1,0:T(8,128)}), f32[8,6,8,128]{3,2,1,0:T(8,128)S(1)}, u32[]{:S(2)}, u32[]{:S(2)}) async-start(f32[8,6,8,128]{3,2,1,0:T(8,128)} %get-tuple-element.54), calls=%async_computation.4 | async-start | bytes 393216 | tf_op jit(solution)/shard_map/all_to_all | solution.py:696
  112.9 7.2 %collective-permute-start.9 = (f32[6,8,128]{2,1,0:T(8,128)S(1)}, f32[6,8,128]{2,1,0:T(8,128)S(1)}, u32[]{:S(2)}, u32[]{:S(2)}) collective-permute-start(f32[6,8,128]{2,1,0:T(8,128)S(1)} %get-tuple-element.55), channel_id=1, source_target_pairs={{4,8},{12,16},{20,24},{28,32},{36,40},{44,48},{52,56},{60,64},{68,... | collective-permute-start | bytes 73736 | tf_op jit(solution)/shard_map/ppermute | solution.py:695

commit v4 on v3

--- a/solution.py
+++ b/solution.py
@@ -60,19 +60,11 @@
 
 
 def dot_right(x, weights, parts=3):
-    total = None
-    for piece in split(x, parts):
-        term = dot(piece, weights)
-        total = term if total is None else total + term
-    return total
+    return dot(jnp.concatenate(split(x, parts), axis=1), jnp.concatenate([weights] * parts, axis=0))
 
 
 def dot_left(weights, x, parts=3):
-    total = None
-    for piece in split(x, parts):
-        term = dot(weights, piece)
-        total = term if total is None else total + term
-    return total
+    return dot(jnp.concatenate([weights] * parts, axis=1), jnp.concatenate(split(x, parts), axis=0))
 
 
 def fine_mask_of(here):
@@ -688,8 +680,8 @@
         step = 1 if p >= 2 else -1
         if 0 <= g + step < groups:
             far_pairs.append((i, 4 * (g + step) + 3 - p))
-            if p in (1, 2):
-                near_pairs.append((i, i + 4 * step))
+            if p in (0, 3):
+                near_pairs.append((i, i + 3 * step))
 
     def faces(face, swap):
         swap = lax.ppermute(swap, X_AXES, swap_pairs)

time: 122 us -> 122 us (level)
  starting transfers between devices: 59.2 us -> 60.6 us
    ppermute x2, waiting for transfers between devices: 7.19 us -> 1.16 us  [to_coarse(): far = lax.ppermute(far, X_AXES, far_pairs)]
    ppermute x2, waiting for transfers between devices: 0.01 us -> 3.51 us  [to_coarse(): near = lax.ppermute(near, X_AXES, near_pairs)]
    ppermute x2, starting transfers between devices: 1.33 us -> 4.43 us  [to_coarse(): near = lax.ppermute(near, X_AXES, near_pairs)]
  transfers between devices with their start and end apart: 12 -> 12, of which waited for: 6 -> 8; matrix products, arithmetic and copies ran while one was open for 0% -> 0% of each run, Pallas kernels for 0% -> 0%
where the time goes in v4:
time: 122 us; the launch traced here: 121 us
  starting transfers between devices  60.6 us (50%)
  blocking collectives  32.6 us (27%)
  waiting for transfers between devices  16 us (13%)
  Pallas kernels  8.8 us (7%)
  local copies, waits for them, and re-layouts  2.48 us (2%)
    all_to_all x2, blocking collectives, to_coarse(): recv = lax.all_to_all(message, ('xc', 'core', 'gz'), 0, 0)  23.7 us
    ppermute x2, starting transfers between devices, layers(): lax.ppermute(cross, X_AXES, swap_pairs)  23 us
    all_to_all x2, starting transfers between devices, faces(): face = lax.all_to_all(face, ('core', 'gz'), 0, 0)  11.8 us
    ppermute x2, starting transfers between devices, to_coarse(): far = lax.ppermute(far, X_AXES, far_pairs)  9.4 us
    all_to_all x1, blocking collectives, local(): edges = lax.all_to_all(edges, 'gz', 0, 0)  8.92 us
    pallas_call x11, Pallas kernels, call(): pl.pallas_call(body, name=name, in_specs=[VMEM_SPEC] * (len(small) + len(...  8.8 us
    ppermute x2, starting transfers between devices, faces(): swap = lax.ppermute(swap, X_AXES, swap_pairs)  8.11 us
    ppermute x2, waiting for transfers between devices, faces(): swap = lax.ppermute(swap, X_AXES, swap_pairs)  6.5 us
  transfers between devices with their start and end apart: 12, of which 8 were waited for; matrix products, arithmetic and copies ran while one was open for 0% of the time, Pallas kernels for 0%

profile of v4, /device:TPU:14, one launch (start us, length us, event | category | flops | bytes accessed | tf_op | source)
XLA Modules:
  0.0 121.4 jit_solution(9094881764073010199)
XLA Ops:
  0.6 0.0 copy-start
  0.6 0.0 copy-start.1
  0.7 1.0 copy-done.1
  1.6 0.8 copy-done.3
  2.4 0.7 copy-done.6
  3.1 0.1 first.1
  3.2 0.0 copy-start.2
  3.2 8.9 %all_to_all.25.refs_5_ = f32[4,3,8,128]{3,2,1,0:T(8,128)S(1)} all-to-all(f32[4,3,8,128]{3,2,1,0:T(8,128)S(1)} %get-tuple-element.30), channel_id=1, replica_groups=mesh['xg'=64,'xc'=2,'core'=2,'gz'=4] {'gz'}, dimensions={0} | all-to-all | bytes 98304 | tf_op jit(solution)/shard_map/all_to_all | solution.py:710
  12.1 0.0 copy-done
  12.1 0.0 copy-done.8
  12.1 0.2 part.1
  12.3 1.9 %collective-permute-start = (f32[13,8,128]{2,1,0:T(8,128)S(1)}, f32[13,8,128]{2,1,0:T(8,128)S(1)}, u32[]{:S(2)}, u32[]{:S(2)}) collective-permute-start(f32[13,8,128]{2,1,0:T(8,128)S(1)} %get-tuple-element.32), channel_id=1, source_target_pairs={{0,4},{4,0},{8,12},{12,8},{16,20},{20,16},{24,28},{28,24},{32,36},... | collective-permute-start | bytes 159752 | tf_op jit(solution)/shard_map/ppermute | solution.py:692
  14.3 19.0 %collective-permute-start.1 = (f32[13,8,128]{2,1,0:T(8,128)S(1)}, f32[13,8,128]{2,1,0:T(8,128)S(1)}, u32[]{:S(2)}, u32[]{:S(2)}) collective-permute-start(f32[13,8,128]{2,1,0:T(8,128)S(1)} %get-tuple-element.33), channel_id=1, source_target_pairs={{4,8},{12,16},{20,24},{28,32},{36,40},{44,48},{52,56},{60,64},{68,... | collective-permute-start | bytes 159752 | tf_op jit(solution)/shard_map/ppermute | solution.py:692
  33.3 0.0 copy-done.2
  33.3 0.5 blocks.1.refs_6_
  33.8 0.0 collective-permute-done.refs_4_
  33.8 1.3 %collective-permute-done.1.refs_5_ = f32[13,8,128]{2,1,0:T(8,128)S(1)} collective-permute-done((f32[13,8,128]{2,1,0:T(8,128)S(1)}, f32[13,8,128]{2,1,0:T(8,128)S(1)}, u32[]{:S(2)}, u32[]{:S(2)}) %collective-permute-start.1) | collective-permute-done | bytes 53280 | tf_op jit(solution)/shard_map/ppermute | solution.py:692
  35.1 0.4 send.2
  35.5 11.2 %all_to_all.26.refs_0_.refs_6_ = f32[16,5,8,128]{3,2,1,0:T(8,128)S(1)} all-to-all(f32[16,5,8,128]{3,2,1,0:T(8,128)S(1)} %get-tuple-element.35), channel_id=1, replica_groups=mesh['xg'=64,'xc'=2,'core'=2,'gz'=4] {'xc','core','gz'}, dimensions={0} | all-to-all | bytes 655360 | tf_op jit(solution)/shard_map/all_to_all | solution.py:695
  46.7 0.1 gather.2
  46.8 5.5 %collective-permute-start.2 = (f32[36,8,128]{2,1,0:T(8,128)S(1)}, f32[36,8,128]{2,1,0:T(8,128)S(1)}, u32[]{:S(2)}, u32[]{:S(2)}) collective-permute-start(f32[36,8,128]{2,1,0:T(8,128)S(1)} %get-tuple-element.37), channel_id=1, source_target_pairs={{8,20},{12,16},{16,12},{20,8},{24,36},{28,32},{32,28},{36,24},{40,... | collective-permute-start | bytes 442376 | tf_op jit(solution)/shard_map/ppermute | solution.py:704
  52.2 2.2 %collective-permute-start.3 = (f32[12,8,128]{2,1,0:T(8,128)S(1)}, f32[12,8,128]{2,1,0:T(8,128)S(1)}, u32[]{:S(2)}, u32[]{:S(2)}) collective-permute-start(f32[12,8,128]{2,1,0:T(8,128)S(1)} %get-tuple-element.38), channel_id=1, source_target_pairs={{12,24},{16,4},{28,40},{32,20},{44,56},{48,36},{60,72},{64,52},{76... | collective-permute-start | bytes 147464 | tf_op jit(solution)/shard_map/ppermute | solution.py:705
  54.5 2.0 %collective-permute-done.3.refs_9_ = f32[12,8,128]{2,1,0:T(8,128)S(1)} collective-permute-done((f32[12,8,128]{2,1,0:T(8,128)S(1)}, f32[12,8,128]{2,1,0:T(8,128)S(1)}, u32[]{:S(2)}, u32[]{:S(2)}) %collective-permute-start.3) | collective-permute-done | bytes 49184 | tf_op jit(solution)/shard_map/ppermute | solution.py:705
  56.5 0.3 collective-permute-done.2.refs_8_
  56.8 3.0 %correct.2 = (f32[12,8,128]{2,1,0:T(8,128)S(1)}, f32[8,6,8,128]{3,2,1,0:T(8,128)}, f32[6,8,128]{2,1,0:T(8,128)S(1)}, f32[8,11,8,128]{3,2,1,0:T(8,128)S(1)}, f32[3,8,128]{2,1,0:T(8,128)S(1)}) custom-call(s32[1,4]{1,0:T(1,128)S(1)} %bitcast.27, f32[1,12]{1,0:T(1,128)S(1)} %bitcast.34, bf16[1152,128]{1,0:T(8,128)(2,1)S(1)} %bitcast.9, ...), custom_call_target="tpu_custom_call" | custom-call | tf_op jit(solution)/shard_map/correct/pallas_call | solution.py:649
  59.8 6.0 %all-to-all-start.2 = ((f32[8,6,8,128]{3,2,1,0:T(8,128)}), f32[8,6,8,128]{3,2,1,0:T(8,128)S(1)}, u32[]{:S(2)}, u32[]{:S(2)}) async-start(f32[8,6,8,128]{3,2,1,0:T(8,128)} %get-tuple-element.40), calls=%async_computation.2 | async-start | bytes 393216 | tf_op jit(solution)/shard_map/all_to_all | solution.py:688
  65.8 4.1 %collective-permute-start.4 = (f32[6,8,128]{2,1,0:T(8,128)S(1)}, f32[6,8,128]{2,1,0:T(8,128)S(1)}, u32[]{:S(2)}, u32[]{:S(2)}) collective-permute-start(f32[6,8,128]{2,1,0:T(8,128)S(1)} %get-tuple-element.41), channel_id=1, source_target_pairs={{4,8},{12,16},{20,24},{28,32},{36,40},{44,48},{52,56},{60,64},{68,... | collective-permute-start | bytes 73736 | tf_op jit(solution)/shard_map/ppermute | solution.py:687
  70.0 3.3 %collective-permute-done.4.refs_6_ = f32[6,8,128]{2,1,0:T(8,128)S(1)} collective-permute-done((f32[6,8,128]{2,1,0:T(8,128)S(1)}, f32[6,8,128]{2,1,0:T(8,128)S(1)}, u32[]{:S(2)}, u32[]{:S(2)}) %collective-permute-start.4) | collective-permute-done | bytes 24608 | tf_op jit(solution)/shard_map/ppermute | solution.py:687
  73.2 0.0 all-to-all-done.2.refs_5_
  73.2 0.0 copy-done.7
  73.2 0.4 sweep.1
  73.6 1.9 %collective-permute-start.5 = (f32[13,8,128]{2,1,0:T(8,128)S(1)}, f32[13,8,128]{2,1,0:T(8,128)S(1)}, u32[]{:S(2)}, u32[]{:S(2)}) collective-permute-start(f32[13,8,128]{2,1,0:T(8,128)S(1)} %get-tuple-element.44), channel_id=1, source_target_pairs={{0,4},{4,0},{8,12},{12,8},{16,20},{20,16},{24,28},{28,24},{32,36},... | collective-permute-start | bytes 159752 | tf_op jit(solution)/shard_map/ppermute | solution.py:692
  75.5 4.0 %collective-permute-start.6 = (f32[13,8,128]{2,1,0:T(8,128)S(1)}, f32[13,8,128]{2,1,0:T(8,128)S(1)}, u32[]{:S(2)}, u32[]{:S(2)}) collective-permute-start(f32[13,8,128]{2,1,0:T(8,128)S(1)} %get-tuple-element.45), channel_id=1, source_target_pairs={{4,8},{12,16},{20,24},{28,32},{36,40},{44,48},{52,56},{60,64},{68,... | collective-permute-start | bytes 159752 | tf_op jit(solution)/shard_map/ppermute | solution.py:692
  79.5 0.0 collective-permute-done.5.refs_4_
  79.5 3.6 %collective-permute-done.6.refs_5_ = f32[13,8,128]{2,1,0:T(8,128)S(1)} collective-permute-done((f32[13,8,128]{2,1,0:T(8,128)S(1)}, f32[13,8,128]{2,1,0:T(8,128)S(1)}, u32[]{:S(2)}, u32[]{:S(2)}) %collective-permute-start.6) | collective-permute-done | bytes 53280 | tf_op jit(solution)/shard_map/ppermute | solution.py:692
  83.1 0.4 send.3
  83.5 12.5 %all_to_all.27.refs_0_.refs_6_ = f32[16,6,8,128]{3,2,1,0:T(8,128)S(1)} all-to-all(f32[16,6,8,128]{3,2,1,0:T(8,128)S(1)} %get-tuple-element.48), channel_id=1, replica_groups=mesh['xg'=64,'xc'=2,'core'=2,'gz'=4] {'xc','core','gz'}, dimensions={0} | all-to-all | bytes 786432 | tf_op jit(solution)/shard_map/all_to_all | solution.py:695
  96.1 3.9 %collective-permute-start.7 = (f32[18,8,128]{2,1,0:T(8,128)S(1)}, f32[18,8,128]{2,1,0:T(8,128)S(1)}, u32[]{:S(2)}, u32[]{:S(2)}) collective-permute-start(f32[18,8,128]{2,1,0:T(8,128)S(1)} %get-tuple-element.50), channel_id=1, source_target_pairs={{8,20},{12,16},{16,12},{20,8},{24,36},{28,32},{32,28},{36,24},{40,... | collective-permute-start | bytes 221192 | tf_op jit(solution)/shard_map/ppermute | solution.py:704
  100.0 2.2 %collective-permute-start.8 = (f32[6,8,128]{2,1,0:T(8,128)S(1)}, f32[6,8,128]{2,1,0:T(8,128)S(1)}, u32[]{:S(2)}, u32[]{:S(2)}) collective-permute-start(f32[6,8,128]{2,1,0:T(8,128)S(1)} %get-tuple-element.51), channel_id=1, source_target_pairs={{12,24},{16,4},{28,40},{32,20},{44,56},{48,36},{60,72},{64,52},{76... | collective-permute-start | bytes 73736 | tf_op jit(solution)/shard_map/ppermute | solution.py:705
  102.2 1.5 %collective-permute-done.8.refs_9_ = f32[6,8,128]{2,1,0:T(8,128)S(1)} collective-permute-done((f32[6,8,128]{2,1,0:T(8,128)S(1)}, f32[6,8,128]{2,1,0:T(8,128)S(1)}, u32[]{:S(2)}, u32[]{:S(2)}) %collective-permute-start.8) | collective-permute-done | bytes 24608 | tf_op jit(solution)/shard_map/ppermute | solution.py:705
  103.7 0.8 collective-permute-done.7.refs_8_
  104.6 2.9 %correct.3 = (f32[12,8,128]{2,1,0:T(8,128)}, f32[8,6,8,128]{3,2,1,0:T(8,128)}, f32[6,8,128]{2,1,0:T(8,128)S(1)}) custom-call(s32[1,4]{1,0:T(1,128)S(1)} %bitcast.30, f32[1,12]{1,0:T(1,128)S(1)} %bitcast.37, bf16[1152,128]{1,0:T(8,128)(2,1)S(1)} %bitcast.11, bf16[1152,128]{1,0:T(8,128)(2,1)S(1)} %bitcast.17, ...), custom_call_target="tpu_custom_call" | custom-call | tf_op jit(solution)/shard_map/correct/pallas_call | solution.py:649
  107.5 5.8 %all-to-all-start.4 = ((f32[8,6,8,128]{3,2,1,0:T(8,128)}), f32[8,6,8,128]{3,2,1,0:T(8,128)S(1)}, u32[]{:S(2)}, u32[]{:S(2)}) async-start(f32[8,6,8,128]{3,2,1,0:T(8,128)} %get-tuple-element.54), calls=%async_computation.4 | async-start | bytes 393216 | tf_op jit(solution)/shard_map/all_to_all | solution.py:688
  113.3 4.0 %collective-permute-start.9 = (f32[6,8,128]{2,1,0:T(8,128)S(1)}, f32[6,8,128]{2,1,0:T(8,128)S(1)}, u32[]{:S(2)}, u32[]{:S(2)}) collective-permute-start(f32[6,8,128]{2,1,0:T(8,128)S(1)} %get-tuple-element.55), channel_id=1, source_target_pairs={{4,8},{12,16},{20,24},{28,32},{36,40},{44,48},{52,56},{60,64},{68,... | collective-permute-start | bytes 73736 | tf_op jit(solution)/shard_map/ppermute | solution.py:687
  117.3 3.2 %collective-permute-done.9.refs_6_ = f32[6,8,128]{2,1,0:T(8,128)S(1)} collective-permute-done((f32[6,8,128]{2,1,0:T(8,128)S(1)}, f32[6,8,128]{2,1,0:T(8,128)S(1)}, u32[]{:S(2)}, u32[]{:S(2)}) %collective-permute-start.9) | collective-permute-done | bytes 24608 | tf_op jit(solution)/shard_map/ppermute | solution.py:687
  120.6 0.0 all-to-all-done.4.refs_5_
  120.6 0.0 copy-done.5
  120.6 0.8 last.1
  (8 shorter events, 0.1 us)
Async XLA Ops:
  0.6 11.5 %copy-start = (bf16[12,12,2,4,128]{4,3,2,1,0:T(4,128)(2,1)S(1)}, bf16[12,12,2,4,128]{4,3,2,1,0:T(4,128)(2,1)}, u32[]{:S(2)}) copy-start(bf16[12,12,2,4,128]{4,3,2,1,0:T(4,128)(2,1)} %param.6) | copy-start | bytes 884740
  0.6 1.0 copy-start.1
  1.6 0.8 copy-start.3
  2.4 0.7 copy-start.6
  3.1 9.0 %copy-start.8 = (f32[12]{0:T(128)S(1)}, f32[12]{0:T(128)}, u32[]{:S(2)}) copy-start(f32[12]{0:T(128)} %param.8) | copy-start | bytes 148
  3.2 30.1 %copy-start.2 = (bf16[12,12,2,4,128]{4,3,2,1,0:T(4,128)(2,1)S(1)}, bf16[12,12,2,4,128]{4,3,2,1,0:T(4,128)(2,1)}, u32[]{:S(2)}) copy-start(bf16[12,12,2,4,128]{4,3,2,1,0:T(4,128)(2,1)} %param.7) | copy-start | bytes 884740
  12.3 21.5 %collective-permute-start = (f32[13,8,128]{2,1,0:T(8,128)S(1)}, f32[13,8,128]{2,1,0:T(8,128)S(1)}, u32[]{:S(2)}, u32[]{:S(2)}) collective-permute-start(f32[13,8,128]{2,1,0:T(8,128)S(1)} %get-tuple-element.32), channel_id=1, source_target_pairs={{0,4},{4,0},{8,12},{12,8},{16,20},{20,16},{24,28},{28,24},{32,36},... | collective-permute-start | bytes 159752 | tf_op jit(solution)/shard_map/ppermute | solution.py:692
  14.3 20.9 %collective-permute-start.1 = (f32[13,8,128]{2,1,0:T(8,128)S(1)}, f32[13,8,128]{2,1,0:T(8,128)S(1)}, u32[]{:S(2)}, u32[]{:S(2)}) collective-permute-start(f32[13,8,128]{2,1,0:T(8,128)S(1)} %get-tuple-element.33), channel_id=1, source_target_pairs={{4,8},{12,16},{20,24},{28,32},{36,40},{44,48},{52,56},{60,64},{68,... | collective-permute-start | bytes 159752 | tf_op jit(solution)/shard_map/ppermute | solution.py:692
  46.8 10.1 %collective-permute-start.2 = (f32[36,8,128]{2,1,0:T(8,128)S(1)}, f32[36,8,128]{2,1,0:T(8,128)S(1)}, u32[]{:S(2)}, u32[]{:S(2)}) collective-permute-start(f32[36,8,128]{2,1,0:T(8,128)S(1)} %get-tuple-element.37), channel_id=1, source_target_pairs={{8,20},{12,16},{16,12},{20,8},{24,36},{28,32},{32,28},{36,24},{40,... | collective-permute-start | bytes 442376 | tf_op jit(solution)/shard_map/ppermute | solution.py:704
  52.2 4.3 %collective-permute-start.3 = (f32[12,8,128]{2,1,0:T(8,128)S(1)}, f32[12,8,128]{2,1,0:T(8,128)S(1)}, u32[]{:S(2)}, u32[]{:S(2)}) collective-permute-start(f32[12,8,128]{2,1,0:T(8,128)S(1)} %get-tuple-element.38), channel_id=1, source_target_pairs={{12,24},{16,4},{28,40},{32,20},{44,56},{48,36},{60,72},{64,52},{76... | collective-permute-start | bytes 147464 | tf_op jit(solution)/shard_map/ppermute | solution.py:705
  59.8 13.4 %copy-start.4 = (f32[12,2,4,128]{3,2,1,0:T(4,128)S(1)}, f32[12,2,4,128]{3,2,1,0:T(4,128)}, u32[]{:S(2)}) copy-start(f32[12,2,4,128]{3,2,1,0:T(4,128)} %param.5) | copy-start | bytes 147460
  59.8 13.4 %all-to-all-start.2 = ((f32[8,6,8,128]{3,2,1,0:T(8,128)}), f32[8,6,8,128]{3,2,1,0:T(8,128)S(1)}, u32[]{:S(2)}, u32[]{:S(2)}) async-start(f32[8,6,8,128]{3,2,1,0:T(8,128)} %get-tuple-element.40), calls=%async_computation.2 | async-start | bytes 393216 | tf_op jit(solution)/shard_map/all_to_all | solution.py:688
  65.8 7.4 %copy-start.7 = (s32[1,1,4]{2,1,0:T(1,128)S(1)}, s32[1,1,4]{2,1,0:T(1,128)}, u32[]{:S(2)}) copy-start(s32[1,1,4]{2,1,0:T(1,128)} %param.9) | copy-start | bytes 52
  65.8 7.4 %collective-permute-start.4 = (f32[6,8,128]{2,1,0:T(8,128)S(1)}, f32[6,8,128]{2,1,0:T(8,128)S(1)}, u32[]{:S(2)}, u32[]{:S(2)}) collective-permute-start(f32[6,8,128]{2,1,0:T(8,128)S(1)} %get-tuple-element.41), channel_id=1, source_target_pairs={{4,8},{12,16},{20,24},{28,32},{36,40},{44,48},{52,56},{60,64},{68,... | collective-permute-start | bytes 73736 | tf_op jit(solution)/shard_map/ppermute | solution.py:687
  73.6 5.9 %collective-permute-start.5 = (f32[13,8,128]{2,1,0:T(8,128)S(1)}, f32[13,8,128]{2,1,0:T(8,128)S(1)}, u32[]{:S(2)}, u32[]{:S(2)}) collective-permute-start(f32[13,8,128]{2,1,0:T(8,128)S(1)} %get-tuple-element.44), channel_id=1, source_target_pairs={{0,4},{4,0},{8,12},{12,8},{16,20},{20,16},{24,28},{28,24},{32,36},... | collective-permute-start | bytes 159752 | tf_op jit(solution)/shard_map/ppermute | solution.py:692
  75.5 7.6 %collective-permute-start.6 = (f32[13,8,128]{2,1,0:T(8,128)S(1)}, f32[13,8,128]{2,1,0:T(8,128)S(1)}, u32[]{:S(2)}, u32[]{:S(2)}) collective-permute-start(f32[13,8,128]{2,1,0:T(8,128)S(1)} %get-tuple-element.45), channel_id=1, source_target_pairs={{4,8},{12,16},{20,24},{28,32},{36,40},{44,48},{52,56},{60,64},{68,... | collective-permute-start | bytes 159752 | tf_op jit(solution)/shard_map/ppermute | solution.py:692
  96.1 8.5 %collective-permute-start.7 = (f32[18,8,128]{2,1,0:T(8,128)S(1)}, f32[18,8,128]{2,1,0:T(8,128)S(1)}, u32[]{:S(2)}, u32[]{:S(2)}) collective-permute-start(f32[18,8,128]{2,1,0:T(8,128)S(1)} %get-tuple-element.50), channel_id=1, source_target_pairs={{8,20},{12,16},{16,12},{20,8},{24,36},{28,32},{32,28},{36,24},{40,... | collective-permute-start | bytes 221192 | tf_op jit(solution)/shard_map/ppermute | solution.py:704
  100.0 3.7 %collective-permute-start.8 = (f32[6,8,128]{2,1,0:T(8,128)S(1)}, f32[6,8,128]{2,1,0:T(8,128)S(1)}, u32[]{:S(2)}, u32[]{:S(2)}) collective-permute-start(f32[6,8,128]{2,1,0:T(8,128)S(1)} %get-tuple-element.51), channel_id=1, source_target_pairs={{12,24},{16,4},{28,40},{32,20},{44,56},{48,36},{60,72},{64,52},{76... | collective-permute-start | bytes 73736 | tf_op jit(solution)/shard_map/ppermute | solution.py:705
  107.5 13.1 %copy-start.5 = (f32[12,8,128]{2,1,0:T(8,128)S(1)}, f32[12,8,128]{2,1,0:T(8,128)}, u32[]{:S(2)}) copy-start(f32[12,8,128]{2,1,0:T(8,128)} %get-tuple-element.53.refs_4_) | copy-start | bytes 147460
  107.5 13.1 %all-to-all-start.4 = ((f32[8,6,8,128]{3,2,1,0:T(8,128)}), f32[8,6,8,128]{3,2,1,0:T(8,128)S(1)}, u32[]{:S(2)}, u32[]{:S(2)}) async-start(f32[8,6,8,128]{3,2,1,0:T(8,128)} %get-tuple-element.54), calls=%async_computation.4 | async-start | bytes 393216 | tf_op jit(solution)/shard_map/all_to_all | solution.py:688
  113.3 7.2 %collective-permute-start.9 = (f32[6,8,128]{2,1,0:T(8,128)S(1)}, f32[6,8,128]{2,1,0:T(8,128)S(1)}, u32[]{:S(2)}, u32[]{:S(2)}) collective-permute-start(f32[6,8,128]{2,1,0:T(8,128)S(1)} %get-tuple-element.55), channel_id=1, source_target_pairs={{4,8},{12,16},{20,24},{28,32},{36,40},{44,48},{52,56},{60,64},{68,... | collective-permute-start | bytes 73736 | tf_op jit(solution)/shard_map/ppermute | solution.py:687

commit v5 on v4

--- a/solution.py
+++ b/solution.py
@@ -274,7 +274,7 @@
     return out
 
 
-def coarse_product(bx_ref, which, slot, vec):
+def coarse_product(bx_ref, which, w, vec):
     left = lanes() < 64
     both = [None] * COMP
     for j in range(HALF):
@@ -285,30 +285,31 @@
     for j in range(HALF):
         acc = None
         for d in range(COMP):
-            term = bx_ref[slot, j * COMP + d, which] * both[d]
+            term = bx_ref[w, j * COMP + d, which] * both[d]
             acc = term if acc is None else acc + term
         out.append(acc)
     return out
 
 
-def coarse_smooth(bx_ref, mask, slot, resid):
-    prod = coarse_product(bx_ref, 0, slot, resid)
+def coarse_smooth(bx_ref, mask, w, resid):
+    prod = coarse_product(bx_ref, 0, w, resid)
     return [mask * a + (1.0 - mask) * r for a, r in zip(prod, resid)]
 
 
 def expand_blocks(win_ref, bx_ref, slots):
-    flat = jnp.concatenate([win_ref[n, r] for n in slots for r in range(9)], axis=0)
+    flat = jnp.concatenate([win_ref[slot, r] for slot in slots for r in range(9)], axis=0)
     pieces = jnp.concatenate(split(flat, 2), axis=1)
     l, o = rows((256, 256)) % 128, lanes((256, 256))
     target = (o // 128) * 8 + ((o % 128) // 64) * 4 + (o % 64) // 16
     for k in range(8):
         weights = jnp.where(l == 16 * k + target, 1.0, 0.0).astype(BF16)
         out = dot(pieces, weights)
-        for i, n in enumerate(slots):
+        for w in range(7):
             for r in range(9):
-                tile = out[(i * 9 + r) * 8 : (i * 9 + r) * 8 + 8]
-                bx_ref[n, 9 * k + r, 0] = tile[:, :128]
-                bx_ref[n, 9 * k + r, 1] = tile[:, 128:]
+                tile = out[(w * 9 + r) * 8 : (w * 9 + r) * 8 + 8]
+                bx_ref[w, 9 * k + r, 0] = tile[:, :128]
+                if 0 < w < 6:
+                    bx_ref[w, 9 * k + r, 1] = tile[:, 128:]
 
 
 def solve_coarse(diff_ref, rhs, slots, win_ref, bx_ref):
@@ -321,12 +322,12 @@
     ]
     masks = [win_ref[slots[w], 9] for w in range(7)]
     b = [rhs(w) for w in range(7)]
-    v = [coarse_smooth(bx_ref, masks[w], slots[w], b[w]) for w in range(7)]
+    v = [coarse_smooth(bx_ref, masks[w], w, b[w]) for w in range(7)]
     for edge in (1, 2):
         mv = [[masks[w] * t for t in v[w]] if v[w] is not None else None for w in range(7)]
         new = [None] * 7
         for w in range(edge, 7 - edge):
-            prod = coarse_product(bx_ref, 1, slots[w], v[w])
+            prod = coarse_product(bx_ref, 1, w, v[w])
             resid = []
             for j in range(HALF):
                 t = mv[w][j]
@@ -336,7 +337,7 @@
                 total = total + jnp.where(inner_lane < 63, pltpu.roll(t, 127, 1), 0.0)
                 inner = prod[j] + coeffs[j] * (6.0 * v[w][j] - total)
                 resid.append(b[w][j] - (masks[w] * inner + (1.0 - masks[w]) * v[w][j]))
-            step = coarse_smooth(bx_ref, masks[w], slots[w], resid)
+            step = coarse_smooth(bx_ref, masks[w], w, resid)
             new[w] = [x + y for x, y in zip(v[w], step)]
         v = new
     return v[2:5]
@@ -549,8 +550,8 @@
         new_ref, face_ref, swap_ref, win_ref, around_ref, rhs_ref, bx_ref = rest
         fill_own(recv_ref, win_ref)
         fill_others(far_ref, near_ref, win_ref)
-    expand_blocks(win_ref, bx_ref, range(8))
     slots = slots_of(p)
+    expand_blocks(win_ref, bx_ref, slots)
     for j in range(HALF):
         for q in range(4):
             rhs_ref[q, j] = own_ref[q, j]
@@ -720,7 +721,7 @@
         [VEC, (16, 5, 8, 128)],
     )
     recv, own, far, near = to_coarse(message, True)
-    rhs_shape, bx_shape, win_shape = (8, HALF, 8, 128), (8, 72, 2, 8, 128), (8, CHANNELS, 8, 128)
+    rhs_shape, bx_shape, win_shape = (8, HALF, 8, 128), (7, 72, 2, 8, 128), (8, CHANNELS, 8, 128)
     u, face, swap, window, around = call(
         functools.partial(correct_kernel, False),
         "correct",

time: 122 us -> 121 us (level)
  no operation moved by 1% of the time
where the time goes in v5:
time: 121 us; the launch traced here: 120 us
  starting transfers between devices  60.6 us (50%)
  blocking collectives  32.6 us (27%)
  waiting for transfers between devices  16.1 us (13%)
  Pallas kernels  7.89 us (7%)
  local copies, waits for them, and re-layouts  2.48 us (2%)
    all_to_all x2, blocking collectives, to_coarse(): recv = lax.all_to_all(message, ('xc', 'core', 'gz'), 0, 0)  23.7 us
    ppermute x2, starting transfers between devices, layers(): lax.ppermute(cross, X_AXES, swap_pairs)  23 us
    all_to_all x2, starting transfers between devices, faces(): face = lax.all_to_all(face, ('core', 'gz'), 0, 0)  11.8 us
    ppermute x2, starting transfers between devices, to_coarse(): far = lax.ppermute(far, X_AXES, far_pairs)  9.39 us
    all_to_all x1, blocking collectives, local(): edges = lax.all_to_all(edges, 'gz', 0, 0)  8.92 us
    ppermute x2, starting transfers between devices, faces(): swap = lax.ppermute(swap, X_AXES, swap_pairs)  8.11 us
    pallas_call x11, Pallas kernels, call(): pl.pallas_call(body, name=name, in_specs=[VMEM_SPEC] * (len(small) + len(...  7.89 us
    ppermute x2, waiting for transfers between devices, faces(): swap = lax.ppermute(swap, X_AXES, swap_pairs)  6.49 us
  transfers between devices with their start and end apart: 12, of which 8 were waited for; matrix products, arithmetic and copies ran while one was open for 0% of the time, Pallas kernels for 0%

profile of v5, /device:TPU:14, one launch (start us, length us, event | category | flops | bytes accessed | tf_op | source)
XLA Modules:
  0.0 120.5 jit_solution(12766676861989648472)
XLA Ops:
  0.6 0.0 copy-start
  0.6 0.0 copy-start.1
  0.7 1.0 copy-done.1
  1.6 0.8 copy-done.3
  2.4 0.7 copy-done.6
  3.1 0.1 first.1
  3.2 0.0 copy-start.2
  3.2 8.9 %all_to_all.25.refs_5_ = f32[4,3,8,128]{3,2,1,0:T(8,128)S(1)} all-to-all(f32[4,3,8,128]{3,2,1,0:T(8,128)S(1)} %get-tuple-element.30), channel_id=1, replica_groups=mesh['xg'=64,'xc'=2,'core'=2,'gz'=4] {'gz'}, dimensions={0} | all-to-all | bytes 98304 | tf_op jit(solution)/shard_map/all_to_all | solution.py:711
  12.1 0.0 copy-done
  12.1 0.0 copy-done.8
  12.1 0.2 part.1
  12.3 1.9 %collective-permute-start = (f32[13,8,128]{2,1,0:T(8,128)S(1)}, f32[13,8,128]{2,1,0:T(8,128)S(1)}, u32[]{:S(2)}, u32[]{:S(2)}) collective-permute-start(f32[13,8,128]{2,1,0:T(8,128)S(1)} %get-tuple-element.32), channel_id=1, source_target_pairs={{0,4},{4,0},{8,12},{12,8},{16,20},{20,16},{24,28},{28,24},{32,36},... | collective-permute-start | bytes 159752 | tf_op jit(solution)/shard_map/ppermute | solution.py:693
  14.3 19.0 %collective-permute-start.1 = (f32[13,8,128]{2,1,0:T(8,128)S(1)}, f32[13,8,128]{2,1,0:T(8,128)S(1)}, u32[]{:S(2)}, u32[]{:S(2)}) collective-permute-start(f32[13,8,128]{2,1,0:T(8,128)S(1)} %get-tuple-element.33), channel_id=1, source_target_pairs={{4,8},{12,16},{20,24},{28,32},{36,40},{44,48},{52,56},{60,64},{68,... | collective-permute-start | bytes 159752 | tf_op jit(solution)/shard_map/ppermute | solution.py:693
  33.3 0.0 copy-done.2
  33.3 0.5 blocks.1.refs_6_
  33.8 0.0 collective-permute-done.refs_4_
  33.8 1.3 %collective-permute-done.1.refs_5_ = f32[13,8,128]{2,1,0:T(8,128)S(1)} collective-permute-done((f32[13,8,128]{2,1,0:T(8,128)S(1)}, f32[13,8,128]{2,1,0:T(8,128)S(1)}, u32[]{:S(2)}, u32[]{:S(2)}) %collective-permute-start.1) | collective-permute-done | bytes 53280 | tf_op jit(solution)/shard_map/ppermute | solution.py:693
  35.1 0.4 send.2
  35.5 11.2 %all_to_all.26.refs_0_.refs_6_ = f32[16,5,8,128]{3,2,1,0:T(8,128)S(1)} all-to-all(f32[16,5,8,128]{3,2,1,0:T(8,128)S(1)} %get-tuple-element.35), channel_id=1, replica_groups=mesh['xg'=64,'xc'=2,'core'=2,'gz'=4] {'xc','core','gz'}, dimensions={0} | all-to-all | bytes 655360 | tf_op jit(solution)/shard_map/all_to_all | solution.py:696
  46.7 0.1 gather.2
  46.8 5.5 %collective-permute-start.2 = (f32[36,8,128]{2,1,0:T(8,128)S(1)}, f32[36,8,128]{2,1,0:T(8,128)S(1)}, u32[]{:S(2)}, u32[]{:S(2)}) collective-permute-start(f32[36,8,128]{2,1,0:T(8,128)S(1)} %get-tuple-element.37), channel_id=1, source_target_pairs={{8,20},{12,16},{16,12},{20,8},{24,36},{28,32},{32,28},{36,24},{40,... | collective-permute-start | bytes 442376 | tf_op jit(solution)/shard_map/ppermute | solution.py:705
  52.2 2.2 %collective-permute-start.3 = (f32[12,8,128]{2,1,0:T(8,128)S(1)}, f32[12,8,128]{2,1,0:T(8,128)S(1)}, u32[]{:S(2)}, u32[]{:S(2)}) collective-permute-start(f32[12,8,128]{2,1,0:T(8,128)S(1)} %get-tuple-element.38), channel_id=1, source_target_pairs={{12,24},{16,4},{28,40},{32,20},{44,56},{48,36},{60,72},{64,52},{76... | collective-permute-start | bytes 147464 | tf_op jit(solution)/shard_map/ppermute | solution.py:706
  54.5 2.0 %collective-permute-done.3.refs_9_ = f32[12,8,128]{2,1,0:T(8,128)S(1)} collective-permute-done((f32[12,8,128]{2,1,0:T(8,128)S(1)}, f32[12,8,128]{2,1,0:T(8,128)S(1)}, u32[]{:S(2)}, u32[]{:S(2)}) %collective-permute-start.3) | collective-permute-done | bytes 49184 | tf_op jit(solution)/shard_map/ppermute | solution.py:706
  56.5 0.3 collective-permute-done.2.refs_8_
  56.8 2.6 %correct.2 = (f32[12,8,128]{2,1,0:T(8,128)S(1)}, f32[8,6,8,128]{3,2,1,0:T(8,128)}, f32[6,8,128]{2,1,0:T(8,128)S(1)}, f32[8,11,8,128]{3,2,1,0:T(8,128)S(1)}, f32[3,8,128]{2,1,0:T(8,128)S(1)}) custom-call(s32[1,4]{1,0:T(1,128)S(1)} %bitcast.27, f32[1,12]{1,0:T(1,128)S(1)} %bitcast.34, bf16[1152,128]{1,0:T(8,128)(2,1)S(1)} %bitcast.9, ...), custom_call_target="tpu_custom_call" | custom-call | tf_op jit(solution)/shard_map/correct/pallas_call | solution.py:650
  59.4 6.0 %all-to-all-start.2 = ((f32[8,6,8,128]{3,2,1,0:T(8,128)}), f32[8,6,8,128]{3,2,1,0:T(8,128)S(1)}, u32[]{:S(2)}, u32[]{:S(2)}) async-start(f32[8,6,8,128]{3,2,1,0:T(8,128)} %get-tuple-element.40), calls=%async_computation.2 | async-start | bytes 393216 | tf_op jit(solution)/shard_map/all_to_all | solution.py:689
  65.4 4.1 %collective-permute-start.4 = (f32[6,8,128]{2,1,0:T(8,128)S(1)}, f32[6,8,128]{2,1,0:T(8,128)S(1)}, u32[]{:S(2)}, u32[]{:S(2)}) collective-permute-start(f32[6,8,128]{2,1,0:T(8,128)S(1)} %get-tuple-element.41), channel_id=1, source_target_pairs={{4,8},{12,16},{20,24},{28,32},{36,40},{44,48},{52,56},{60,64},{68,... | collective-permute-start | bytes 73736 | tf_op jit(solution)/shard_map/ppermute | solution.py:688
  69.5 3.3 %collective-permute-done.4.refs_6_ = f32[6,8,128]{2,1,0:T(8,128)S(1)} collective-permute-done((f32[6,8,128]{2,1,0:T(8,128)S(1)}, f32[6,8,128]{2,1,0:T(8,128)S(1)}, u32[]{:S(2)}, u32[]{:S(2)}) %collective-permute-start.4) | collective-permute-done | bytes 24608 | tf_op jit(solution)/shard_map/ppermute | solution.py:688
  72.8 0.0 all-to-all-done.2.refs_5_
  72.8 0.0 copy-done.4
  72.8 0.0 copy-done.7
  72.8 0.4 sweep.1
  73.2 1.9 %collective-permute-start.5 = (f32[13,8,128]{2,1,0:T(8,128)S(1)}, f32[13,8,128]{2,1,0:T(8,128)S(1)}, u32[]{:S(2)}, u32[]{:S(2)}) collective-permute-start(f32[13,8,128]{2,1,0:T(8,128)S(1)} %get-tuple-element.44), channel_id=1, source_target_pairs={{0,4},{4,0},{8,12},{12,8},{16,20},{20,16},{24,28},{28,24},{32,36},... | collective-permute-start | bytes 159752 | tf_op jit(solution)/shard_map/ppermute | solution.py:693
  75.1 4.0 %collective-permute-start.6 = (f32[13,8,128]{2,1,0:T(8,128)S(1)}, f32[13,8,128]{2,1,0:T(8,128)S(1)}, u32[]{:S(2)}, u32[]{:S(2)}) collective-permute-start(f32[13,8,128]{2,1,0:T(8,128)S(1)} %get-tuple-element.45), channel_id=1, source_target_pairs={{4,8},{12,16},{20,24},{28,32},{36,40},{44,48},{52,56},{60,64},{68,... | collective-permute-start | bytes 159752 | tf_op jit(solution)/shard_map/ppermute | solution.py:693
  79.1 0.0 collective-permute-done.5.refs_4_
  79.1 3.6 %collective-permute-done.6.refs_5_ = f32[13,8,128]{2,1,0:T(8,128)S(1)} collective-permute-done((f32[13,8,128]{2,1,0:T(8,128)S(1)}, f32[13,8,128]{2,1,0:T(8,128)S(1)}, u32[]{:S(2)}, u32[]{:S(2)}) %collective-permute-start.6) | collective-permute-done | bytes 53280 | tf_op jit(solution)/shard_map/ppermute | solution.py:693
  82.6 0.4 send.3
  83.1 12.5 %all_to_all.27.refs_0_.refs_6_ = f32[16,6,8,128]{3,2,1,0:T(8,128)S(1)} all-to-all(f32[16,6,8,128]{3,2,1,0:T(8,128)S(1)} %get-tuple-element.48), channel_id=1, replica_groups=mesh['xg'=64,'xc'=2,'core'=2,'gz'=4] {'xc','core','gz'}, dimensions={0} | all-to-all | bytes 786432 | tf_op jit(solution)/shard_map/all_to_all | solution.py:696
  95.7 3.9 %collective-permute-start.7 = (f32[18,8,128]{2,1,0:T(8,128)S(1)}, f32[18,8,128]{2,1,0:T(8,128)S(1)}, u32[]{:S(2)}, u32[]{:S(2)}) collective-permute-start(f32[18,8,128]{2,1,0:T(8,128)S(1)} %get-tuple-element.50), channel_id=1, source_target_pairs={{8,20},{12,16},{16,12},{20,8},{24,36},{28,32},{32,28},{36,24},{40,... | collective-permute-start | bytes 221192 | tf_op jit(solution)/shard_map/ppermute | solution.py:705
  99.6 2.2 %collective-permute-start.8 = (f32[6,8,128]{2,1,0:T(8,128)S(1)}, f32[6,8,128]{2,1,0:T(8,128)S(1)}, u32[]{:S(2)}, u32[]{:S(2)}) collective-permute-start(f32[6,8,128]{2,1,0:T(8,128)S(1)} %get-tuple-element.51), channel_id=1, source_target_pairs={{12,24},{16,4},{28,40},{32,20},{44,56},{48,36},{60,72},{64,52},{76... | collective-permute-start | bytes 73736 | tf_op jit(solution)/shard_map/ppermute | solution.py:706
  101.8 1.5 %collective-permute-done.8.refs_9_ = f32[6,8,128]{2,1,0:T(8,128)S(1)} collective-permute-done((f32[6,8,128]{2,1,0:T(8,128)S(1)}, f32[6,8,128]{2,1,0:T(8,128)S(1)}, u32[]{:S(2)}, u32[]{:S(2)}) %collective-permute-start.8) | collective-permute-done | bytes 24608 | tf_op jit(solution)/shard_map/ppermute | solution.py:706
  103.3 0.8 collective-permute-done.7.refs_8_
  104.1 2.5 %correct.3 = (f32[12,8,128]{2,1,0:T(8,128)}, f32[8,6,8,128]{3,2,1,0:T(8,128)}, f32[6,8,128]{2,1,0:T(8,128)S(1)}) custom-call(s32[1,4]{1,0:T(1,128)S(1)} %bitcast.30, f32[1,12]{1,0:T(1,128)S(1)} %bitcast.37, bf16[1152,128]{1,0:T(8,128)(2,1)S(1)} %bitcast.11, bf16[1152,128]{1,0:T(8,128)(2,1)S(1)} %bitcast.17, ...), custom_call_target="tpu_custom_call" | custom-call | tf_op jit(solution)/shard_map/correct/pallas_call | solution.py:650
  106.6 5.8 %all-to-all-start.4 = ((f32[8,6,8,128]{3,2,1,0:T(8,128)}), f32[8,6,8,128]{3,2,1,0:T(8,128)S(1)}, u32[]{:S(2)}, u32[]{:S(2)}) async-start(f32[8,6,8,128]{3,2,1,0:T(8,128)} %get-tuple-element.54), calls=%async_computation.4 | async-start | bytes 393216 | tf_op jit(solution)/shard_map/all_to_all | solution.py:689
  112.4 4.0 %collective-permute-start.9 = (f32[6,8,128]{2,1,0:T(8,128)S(1)}, f32[6,8,128]{2,1,0:T(8,128)S(1)}, u32[]{:S(2)}, u32[]{:S(2)}) collective-permute-start(f32[6,8,128]{2,1,0:T(8,128)S(1)} %get-tuple-element.55), channel_id=1, source_target_pairs={{4,8},{12,16},{20,24},{28,32},{36,40},{44,48},{52,56},{60,64},{68,... | collective-permute-start | bytes 73736 | tf_op jit(solution)/shard_map/ppermute | solution.py:688
  116.4 3.2 %collective-permute-done.9.refs_6_ = f32[6,8,128]{2,1,0:T(8,128)S(1)} collective-permute-done((f32[6,8,128]{2,1,0:T(8,128)S(1)}, f32[6,8,128]{2,1,0:T(8,128)S(1)}, u32[]{:S(2)}, u32[]{:S(2)}) %collective-permute-start.9) | collective-permute-done | bytes 24608 | tf_op jit(solution)/shard_map/ppermute | solution.py:688
  119.6 0.0 all-to-all-done.4.refs_5_
  119.7 0.8 last.1
  (8 shorter events, 0.1 us)
Async XLA Ops:
  0.6 11.5 %copy-start = (bf16[12,12,2,4,128]{4,3,2,1,0:T(4,128)(2,1)S(1)}, bf16[12,12,2,4,128]{4,3,2,1,0:T(4,128)(2,1)}, u32[]{:S(2)}) copy-start(bf16[12,12,2,4,128]{4,3,2,1,0:T(4,128)(2,1)} %param.6) | copy-start | bytes 884740
  0.6 1.0 copy-start.1
  1.6 0.8 copy-start.3
  2.4 0.7 copy-start.6
  3.1 9.0 %copy-start.8 = (f32[12]{0:T(128)S(1)}, f32[12]{0:T(128)}, u32[]{:S(2)}) copy-start(f32[12]{0:T(128)} %param.8) | copy-start | bytes 148
  3.2 30.1 %copy-start.2 = (bf16[12,12,2,4,128]{4,3,2,1,0:T(4,128)(2,1)S(1)}, bf16[12,12,2,4,128]{4,3,2,1,0:T(4,128)(2,1)}, u32[]{:S(2)}) copy-start(bf16[12,12,2,4,128]{4,3,2,1,0:T(4,128)(2,1)} %param.7) | copy-start | bytes 884740
  12.3 21.5 %collective-permute-start = (f32[13,8,128]{2,1,0:T(8,128)S(1)}, f32[13,8,128]{2,1,0:T(8,128)S(1)}, u32[]{:S(2)}, u32[]{:S(2)}) collective-permute-start(f32[13,8,128]{2,1,0:T(8,128)S(1)} %get-tuple-element.32), channel_id=1, source_target_pairs={{0,4},{4,0},{8,12},{12,8},{16,20},{20,16},{24,28},{28,24},{32,36},... | collective-permute-start | bytes 159752 | tf_op jit(solution)/shard_map/ppermute | solution.py:693
  14.3 20.9 %collective-permute-start.1 = (f32[13,8,128]{2,1,0:T(8,128)S(1)}, f32[13,8,128]{2,1,0:T(8,128)S(1)}, u32[]{:S(2)}, u32[]{:S(2)}) collective-permute-start(f32[13,8,128]{2,1,0:T(8,128)S(1)} %get-tuple-element.33), channel_id=1, source_target_pairs={{4,8},{12,16},{20,24},{28,32},{36,40},{44,48},{52,56},{60,64},{68,... | collective-permute-start | bytes 159752 | tf_op jit(solution)/shard_map/ppermute | solution.py:693
  46.8 10.1 %collective-permute-start.2 = (f32[36,8,128]{2,1,0:T(8,128)S(1)}, f32[36,8,128]{2,1,0:T(8,128)S(1)}, u32[]{:S(2)}, u32[]{:S(2)}) collective-permute-start(f32[36,8,128]{2,1,0:T(8,128)S(1)} %get-tuple-element.37), channel_id=1, source_target_pairs={{8,20},{12,16},{16,12},{20,8},{24,36},{28,32},{32,28},{36,24},{40,... | collective-permute-start | bytes 442376 | tf_op jit(solution)/shard_map/ppermute | solution.py:705
  52.2 4.3 %collective-permute-start.3 = (f32[12,8,128]{2,1,0:T(8,128)S(1)}, f32[12,8,128]{2,1,0:T(8,128)S(1)}, u32[]{:S(2)}, u32[]{:S(2)}) collective-permute-start(f32[12,8,128]{2,1,0:T(8,128)S(1)} %get-tuple-element.38), channel_id=1, source_target_pairs={{12,24},{16,4},{28,40},{32,20},{44,56},{48,36},{60,72},{64,52},{76... | collective-permute-start | bytes 147464 | tf_op jit(solution)/shard_map/ppermute | solution.py:706
  59.4 13.4 %copy-start.4 = (f32[12,2,4,128]{3,2,1,0:T(4,128)S(1)}, f32[12,2,4,128]{3,2,1,0:T(4,128)}, u32[]{:S(2)}) copy-start(f32[12,2,4,128]{3,2,1,0:T(4,128)} %param.5) | copy-start | bytes 147460
  59.4 13.4 %all-to-all-start.2 = ((f32[8,6,8,128]{3,2,1,0:T(8,128)}), f32[8,6,8,128]{3,2,1,0:T(8,128)S(1)}, u32[]{:S(2)}, u32[]{:S(2)}) async-start(f32[8,6,8,128]{3,2,1,0:T(8,128)} %get-tuple-element.40), calls=%async_computation.2 | async-start | bytes 393216 | tf_op jit(solution)/shard_map/all_to_all | solution.py:689
  65.4 7.4 %copy-start.7 = (s32[1,1,4]{2,1,0:T(1,128)S(1)}, s32[1,1,4]{2,1,0:T(1,128)}, u32[]{:S(2)}) copy-start(s32[1,1,4]{2,1,0:T(1,128)} %param.9) | copy-start | bytes 52
  65.4 7.4 %collective-permute-start.4 = (f32[6,8,128]{2,1,0:T(8,128)S(1)}, f32[6,8,128]{2,1,0:T(8,128)S(1)}, u32[]{:S(2)}, u32[]{:S(2)}) collective-permute-start(f32[6,8,128]{2,1,0:T(8,128)S(1)} %get-tuple-element.41), channel_id=1, source_target_pairs={{4,8},{12,16},{20,24},{28,32},{36,40},{44,48},{52,56},{60,64},{68,... | collective-permute-start | bytes 73736 | tf_op jit(solution)/shard_map/ppermute | solution.py:688
  73.2 5.9 %collective-permute-start.5 = (f32[13,8,128]{2,1,0:T(8,128)S(1)}, f32[13,8,128]{2,1,0:T(8,128)S(1)}, u32[]{:S(2)}, u32[]{:S(2)}) collective-permute-start(f32[13,8,128]{2,1,0:T(8,128)S(1)} %get-tuple-element.44), channel_id=1, source_target_pairs={{0,4},{4,0},{8,12},{12,8},{16,20},{20,16},{24,28},{28,24},{32,36},... | collective-permute-start | bytes 159752 | tf_op jit(solution)/shard_map/ppermute | solution.py:693
  75.1 7.6 %collective-permute-start.6 = (f32[13,8,128]{2,1,0:T(8,128)S(1)}, f32[13,8,128]{2,1,0:T(8,128)S(1)}, u32[]{:S(2)}, u32[]{:S(2)}) collective-permute-start(f32[13,8,128]{2,1,0:T(8,128)S(1)} %get-tuple-element.45), channel_id=1, source_target_pairs={{4,8},{12,16},{20,24},{28,32},{36,40},{44,48},{52,56},{60,64},{68,... | collective-permute-start | bytes 159752 | tf_op jit(solution)/shard_map/ppermute | solution.py:693
  95.7 8.5 %collective-permute-start.7 = (f32[18,8,128]{2,1,0:T(8,128)S(1)}, f32[18,8,128]{2,1,0:T(8,128)S(1)}, u32[]{:S(2)}, u32[]{:S(2)}) collective-permute-start(f32[18,8,128]{2,1,0:T(8,128)S(1)} %get-tuple-element.50), channel_id=1, source_target_pairs={{8,20},{12,16},{16,12},{20,8},{24,36},{28,32},{32,28},{36,24},{40,... | collective-permute-start | bytes 221192 | tf_op jit(solution)/shard_map/ppermute | solution.py:705
  99.6 3.7 %collective-permute-start.8 = (f32[6,8,128]{2,1,0:T(8,128)S(1)}, f32[6,8,128]{2,1,0:T(8,128)S(1)}, u32[]{:S(2)}, u32[]{:S(2)}) collective-permute-start(f32[6,8,128]{2,1,0:T(8,128)S(1)} %get-tuple-element.51), channel_id=1, source_target_pairs={{12,24},{16,4},{28,40},{32,20},{44,56},{48,36},{60,72},{64,52},{76... | collective-permute-start | bytes 73736 | tf_op jit(solution)/shard_map/ppermute | solution.py:706
  106.6 13.1 %copy-start.5 = (f32[12,8,128]{2,1,0:T(8,128)S(1)}, f32[12,8,128]{2,1,0:T(8,128)}, u32[]{:S(2)}) copy-start(f32[12,8,128]{2,1,0:T(8,128)} %get-tuple-element.53.refs_4_) | copy-start | bytes 147460
  106.6 13.0 %all-to-all-start.4 = ((f32[8,6,8,128]{3,2,1,0:T(8,128)}), f32[8,6,8,128]{3,2,1,0:T(8,128)S(1)}, u32[]{:S(2)}, u32[]{:S(2)}) async-start(f32[8,6,8,128]{3,2,1,0:T(8,128)} %get-tuple-element.54), calls=%async_computation.4 | async-start | bytes 393216 | tf_op jit(solution)/shard_map/all_to_all | solution.py:689
  112.4 7.2 %collective-permute-start.9 = (f32[6,8,128]{2,1,0:T(8,128)S(1)}, f32[6,8,128]{2,1,0:T(8,128)S(1)}, u32[]{:S(2)}, u32[]{:S(2)}) collective-permute-start(f32[6,8,128]{2,1,0:T(8,128)S(1)} %get-tuple-element.55), channel_id=1, source_target_pairs={{4,8},{12,16},{20,24},{28,32},{36,40},{44,48},{52,56},{60,64},{68,... | collective-permute-start | bytes 73736 | tf_op jit(solution)/shard_map/ppermute | solution.py:688

commit v6 on v5

--- a/solution.py
+++ b/solution.py
@@ -681,8 +681,8 @@
         step = 1 if p >= 2 else -1
         if 0 <= g + step < groups:
             far_pairs.append((i, 4 * (g + step) + 3 - p))
-            if p in (0, 3):
-                near_pairs.append((i, i + 3 * step))
+            if p in (1, 2):
+                near_pairs.append((i, i + 4 * step))
 
     def faces(face, swap):
         swap = lax.ppermute(swap, X_AXES, swap_pairs)

time: 121 us -> 121 us (level)
  starting transfers between devices: 60.6 us -> 59.2 us
    ppermute x2, waiting for transfers between devices: 1.17 us -> 7.19 us  [to_coarse(): far = lax.ppermute(far, X_AXES, far_pairs)]
    ppermute x2, waiting for transfers between devices: 3.51 us -> 0.01 us  [to_coarse(): near = lax.ppermute(near, X_AXES, near_pairs)]
    ppermute x2, starting transfers between devices: 4.43 us -> 1.33 us  [to_coarse(): near = lax.ppermute(near, X_AXES, near_pairs)]
  transfers between devices with their start and end apart: 12 -> 12, of which waited for: 8 -> 6; matrix products, arithmetic and copies ran while one was open for 0% -> 0% of each run, Pallas kernels for 0% -> 0%
where the time goes in v6:
time: 121 us; the launch traced here: 120 us
  starting transfers between devices  59.2 us (49%)
  blocking collectives  32.6 us (27%)
  waiting for transfers between devices  16.8 us (14%)
  Pallas kernels  7.89 us (7%)
  local copies, waits for them, and re-layouts  2.48 us (2%)
    all_to_all x2, blocking collectives, to_coarse(): recv = lax.all_to_all(message, ('xc', 'core', 'gz'), 0, 0)  23.7 us
    ppermute x2, starting transfers between devices, layers(): lax.ppermute(cross, X_AXES, swap_pairs)  23.6 us
    all_to_all x2, starting transfers between devices, faces(): face = lax.all_to_all(face, ('core', 'gz'), 0, 0)  11.2 us
    ppermute x2, starting transfers between devices, to_coarse(): far = lax.ppermute(far, X_AXES, far_pairs)  9.97 us
    ppermute x2, starting transfers between devices, faces(): swap = lax.ppermute(swap, X_AXES, swap_pairs)  9.26 us
    all_to_all x1, blocking collectives, local(): edges = lax.all_to_all(edges, 'gz', 0, 0)  8.92 us
    pallas_call x11, Pallas kernels, call(): pl.pallas_call(body, name=name, in_specs=[VMEM_SPEC] * (len(small) + len(...  7.89 us
    ppermute x2, waiting for transfers between devices, to_coarse(): far = lax.ppermute(far, X_AXES, far_pairs)  7.19 us
  transfers between devices with their start and end apart: 12, of which 6 were waited for; matrix products, arithmetic and copies ran while one was open for 0% of the time, Pallas kernels for 0%

profile of v6, /device:TPU:14, one launch (start us, length us, event | category | flops | bytes accessed | tf_op | source)
XLA Modules:
  0.0 119.9 jit_solution(7098568702178549694)
XLA Ops:
  0.6 0.0 copy-start
  0.6 0.0 copy-start.1
  0.7 1.0 copy-done.1
  1.6 0.8 copy-done.3
  2.4 0.7 copy-done.6
  3.1 0.1 first.1
  3.2 0.0 copy-start.2
  3.2 8.9 %all_to_all.25.refs_5_ = f32[4,3,8,128]{3,2,1,0:T(8,128)S(1)} all-to-all(f32[4,3,8,128]{3,2,1,0:T(8,128)S(1)} %get-tuple-element.30), channel_id=1, replica_groups=mesh['xg'=64,'xc'=2,'core'=2,'gz'=4] {'gz'}, dimensions={0} | all-to-all | bytes 98304 | tf_op jit(solution)/shard_map/all_to_all | solution.py:711
  12.1 0.0 copy-done
  12.1 0.0 copy-done.8
  12.1 0.2 part.1
  12.3 1.9 %collective-permute-start = (f32[13,8,128]{2,1,0:T(8,128)S(1)}, f32[13,8,128]{2,1,0:T(8,128)S(1)}, u32[]{:S(2)}, u32[]{:S(2)}) collective-permute-start(f32[13,8,128]{2,1,0:T(8,128)S(1)} %get-tuple-element.32), channel_id=1, source_target_pairs={{0,4},{4,0},{8,12},{12,8},{16,20},{20,16},{24,28},{28,24},{32,36},... | collective-permute-start | bytes 159752 | tf_op jit(solution)/shard_map/ppermute | solution.py:693
  14.3 19.0 %collective-permute-start.1 = (f32[13,8,128]{2,1,0:T(8,128)S(1)}, f32[13,8,128]{2,1,0:T(8,128)S(1)}, u32[]{:S(2)}, u32[]{:S(2)}) collective-permute-start(f32[13,8,128]{2,1,0:T(8,128)S(1)} %get-tuple-element.33), channel_id=1, source_target_pairs={{4,8},{12,16},{20,24},{28,32},{36,40},{44,48},{52,56},{60,64},{68,... | collective-permute-start | bytes 159752 | tf_op jit(solution)/shard_map/ppermute | solution.py:693
  33.3 0.0 copy-done.2
  33.3 0.5 blocks.1.refs_6_
  33.8 0.0 collective-permute-done.refs_4_
  33.8 1.3 %collective-permute-done.1.refs_5_ = f32[13,8,128]{2,1,0:T(8,128)S(1)} collective-permute-done((f32[13,8,128]{2,1,0:T(8,128)S(1)}, f32[13,8,128]{2,1,0:T(8,128)S(1)}, u32[]{:S(2)}, u32[]{:S(2)}) %collective-permute-start.1) | collective-permute-done | bytes 53280 | tf_op jit(solution)/shard_map/ppermute | solution.py:693
  35.1 0.4 send.2
  35.5 11.2 %all_to_all.26.refs_0_.refs_6_ = f32[16,5,8,128]{3,2,1,0:T(8,128)S(1)} all-to-all(f32[16,5,8,128]{3,2,1,0:T(8,128)S(1)} %get-tuple-element.35), channel_id=1, replica_groups=mesh['xg'=64,'xc'=2,'core'=2,'gz'=4] {'xc','core','gz'}, dimensions={0} | all-to-all | bytes 655360 | tf_op jit(solution)/shard_map/all_to_all | solution.py:696
  46.7 0.1 gather.2
  46.8 5.5 %collective-permute-start.2 = (f32[36,8,128]{2,1,0:T(8,128)S(1)}, f32[36,8,128]{2,1,0:T(8,128)S(1)}, u32[]{:S(2)}, u32[]{:S(2)}) collective-permute-start(f32[36,8,128]{2,1,0:T(8,128)S(1)} %get-tuple-element.37), channel_id=1, source_target_pairs={{8,20},{12,16},{16,12},{20,8},{24,36},{28,32},{32,28},{36,24},{40,... | collective-permute-start | bytes 442376 | tf_op jit(solution)/shard_map/ppermute | solution.py:705
  52.2 0.7 collective-permute-start.3
  52.9 0.0 collective-permute-done.3.refs_9_
  52.9 3.9 %collective-permute-done.2.refs_8_ = f32[36,8,128]{2,1,0:T(8,128)S(1)} collective-permute-done((f32[36,8,128]{2,1,0:T(8,128)S(1)}, f32[36,8,128]{2,1,0:T(8,128)S(1)}, u32[]{:S(2)}, u32[]{:S(2)}) %collective-permute-start.2) | collective-permute-done | bytes 147488 | tf_op jit(solution)/shard_map/ppermute | solution.py:705
  56.8 2.6 %correct.2 = (f32[12,8,128]{2,1,0:T(8,128)S(1)}, f32[8,6,8,128]{3,2,1,0:T(8,128)}, f32[6,8,128]{2,1,0:T(8,128)S(1)}, f32[8,11,8,128]{3,2,1,0:T(8,128)S(1)}, f32[3,8,128]{2,1,0:T(8,128)S(1)}) custom-call(s32[1,4]{1,0:T(1,128)S(1)} %bitcast.27, f32[1,12]{1,0:T(1,128)S(1)} %bitcast.34, bf16[1152,128]{1,0:T(8,128)(2,1)S(1)} %bitcast.9, ...), custom_call_target="tpu_custom_call" | custom-call | tf_op jit(solution)/shard_map/correct/pallas_call | solution.py:650
  59.4 5.4 %all-to-all-start.2 = ((f32[8,6,8,128]{3,2,1,0:T(8,128)}), f32[8,6,8,128]{3,2,1,0:T(8,128)S(1)}, u32[]{:S(2)}, u32[]{:S(2)}) async-start(f32[8,6,8,128]{3,2,1,0:T(8,128)} %get-tuple-element.40), calls=%async_computation.2 | async-start | bytes 393216 | tf_op jit(solution)/shard_map/all_to_all | solution.py:689
  64.8 4.7 %collective-permute-start.4 = (f32[6,8,128]{2,1,0:T(8,128)S(1)}, f32[6,8,128]{2,1,0:T(8,128)S(1)}, u32[]{:S(2)}, u32[]{:S(2)}) collective-permute-start(f32[6,8,128]{2,1,0:T(8,128)S(1)} %get-tuple-element.41), channel_id=1, source_target_pairs={{4,8},{12,16},{20,24},{28,32},{36,40},{44,48},{52,56},{60,64},{68,... | collective-permute-start | bytes 73736 | tf_op jit(solution)/shard_map/ppermute | solution.py:688
  69.5 2.7 %collective-permute-done.4.refs_6_ = f32[6,8,128]{2,1,0:T(8,128)S(1)} collective-permute-done((f32[6,8,128]{2,1,0:T(8,128)S(1)}, f32[6,8,128]{2,1,0:T(8,128)S(1)}, u32[]{:S(2)}, u32[]{:S(2)}) %collective-permute-start.4) | collective-permute-done | bytes 24608 | tf_op jit(solution)/shard_map/ppermute | solution.py:688
  72.2 0.0 all-to-all-done.2.refs_5_
  72.2 0.0 copy-done.4
  72.2 0.0 copy-done.7
  72.2 0.4 sweep.1
  72.6 1.9 %collective-permute-start.5 = (f32[13,8,128]{2,1,0:T(8,128)S(1)}, f32[13,8,128]{2,1,0:T(8,128)S(1)}, u32[]{:S(2)}, u32[]{:S(2)}) collective-permute-start(f32[13,8,128]{2,1,0:T(8,128)S(1)} %get-tuple-element.44), channel_id=1, source_target_pairs={{0,4},{4,0},{8,12},{12,8},{16,20},{20,16},{24,28},{28,24},{32,36},... | collective-permute-start | bytes 159752 | tf_op jit(solution)/shard_map/ppermute | solution.py:693
  74.5 4.6 %collective-permute-start.6 = (f32[13,8,128]{2,1,0:T(8,128)S(1)}, f32[13,8,128]{2,1,0:T(8,128)S(1)}, u32[]{:S(2)}, u32[]{:S(2)}) collective-permute-start(f32[13,8,128]{2,1,0:T(8,128)S(1)} %get-tuple-element.45), channel_id=1, source_target_pairs={{4,8},{12,16},{20,24},{28,32},{36,40},{44,48},{52,56},{60,64},{68,... | collective-permute-start | bytes 159752 | tf_op jit(solution)/shard_map/ppermute | solution.py:693
  79.1 0.0 collective-permute-done.5.refs_4_
  79.1 3.0 %collective-permute-done.6.refs_5_ = f32[13,8,128]{2,1,0:T(8,128)S(1)} collective-permute-done((f32[13,8,128]{2,1,0:T(8,128)S(1)}, f32[13,8,128]{2,1,0:T(8,128)S(1)}, u32[]{:S(2)}, u32[]{:S(2)}) %collective-permute-start.6) | collective-permute-done | bytes 53280 | tf_op jit(solution)/shard_map/ppermute | solution.py:693
  82.1 0.4 send.3
  82.5 12.5 %all_to_all.27.refs_0_.refs_6_ = f32[16,6,8,128]{3,2,1,0:T(8,128)S(1)} all-to-all(f32[16,6,8,128]{3,2,1,0:T(8,128)S(1)} %get-tuple-element.48), channel_id=1, replica_groups=mesh['xg'=64,'xc'=2,'core'=2,'gz'=4] {'xc','core','gz'}, dimensions={0} | all-to-all | bytes 786432 | tf_op jit(solution)/shard_map/all_to_all | solution.py:696
  95.1 4.5 %collective-permute-start.7 = (f32[18,8,128]{2,1,0:T(8,128)S(1)}, f32[18,8,128]{2,1,0:T(8,128)S(1)}, u32[]{:S(2)}, u32[]{:S(2)}) collective-permute-start(f32[18,8,128]{2,1,0:T(8,128)S(1)} %get-tuple-element.50), channel_id=1, source_target_pairs={{8,20},{12,16},{16,12},{20,8},{24,36},{28,32},{32,28},{36,24},{40,... | collective-permute-start | bytes 221192 | tf_op jit(solution)/shard_map/ppermute | solution.py:705
  99.6 0.7 collective-permute-start.8
  100.3 0.0 collective-permute-done.8.refs_9_
  100.3 3.3 %collective-permute-done.7.refs_8_ = f32[18,8,128]{2,1,0:T(8,128)S(1)} collective-permute-done((f32[18,8,128]{2,1,0:T(8,128)S(1)}, f32[18,8,128]{2,1,0:T(8,128)S(1)}, u32[]{:S(2)}, u32[]{:S(2)}) %collective-permute-start.7) | collective-permute-done | bytes 73760 | tf_op jit(solution)/shard_map/ppermute | solution.py:705
  103.6 2.5 %correct.3 = (f32[12,8,128]{2,1,0:T(8,128)}, f32[8,6,8,128]{3,2,1,0:T(8,128)}, f32[6,8,128]{2,1,0:T(8,128)S(1)}) custom-call(s32[1,4]{1,0:T(1,128)S(1)} %bitcast.30, f32[1,12]{1,0:T(1,128)S(1)} %bitcast.37, bf16[1152,128]{1,0:T(8,128)(2,1)S(1)} %bitcast.11, bf16[1152,128]{1,0:T(8,128)(2,1)S(1)} %bitcast.17, ...), custom_call_target="tpu_custom_call" | custom-call | tf_op jit(solution)/shard_map/correct/pallas_call | solution.py:650
  106.0 5.8 %all-to-all-start.4 = ((f32[8,6,8,128]{3,2,1,0:T(8,128)}), f32[8,6,8,128]{3,2,1,0:T(8,128)S(1)}, u32[]{:S(2)}, u32[]{:S(2)}) async-start(f32[8,6,8,128]{3,2,1,0:T(8,128)} %get-tuple-element.54), calls=%async_computation.4 | async-start | bytes 393216 | tf_op jit(solution)/shard_map/all_to_all | solution.py:689
  111.8 4.6 %collective-permute-start.9 = (f32[6,8,128]{2,1,0:T(8,128)S(1)}, f32[6,8,128]{2,1,0:T(8,128)S(1)}, u32[]{:S(2)}, u32[]{:S(2)}) collective-permute-start(f32[6,8,128]{2,1,0:T(8,128)S(1)} %get-tuple-element.55), channel_id=1, source_target_pairs={{4,8},{12,16},{20,24},{28,32},{36,40},{44,48},{52,56},{60,64},{68,... | collective-permute-start | bytes 73736 | tf_op jit(solution)/shard_map/ppermute | solution.py:688
  116.4 2.7 %collective-permute-done.9.refs_6_ = f32[6,8,128]{2,1,0:T(8,128)S(1)} collective-permute-done((f32[6,8,128]{2,1,0:T(8,128)S(1)}, f32[6,8,128]{2,1,0:T(8,128)S(1)}, u32[]{:S(2)}, u32[]{:S(2)}) %collective-permute-start.9) | collective-permute-done | bytes 24608 | tf_op jit(solution)/shard_map/ppermute | solution.py:688
  119.1 0.0 all-to-all-done.4.refs_5_
  119.1 0.8 last.1
  (8 shorter events, 0.1 us)
Async XLA Ops:
  0.6 11.5 %copy-start = (bf16[12,12,2,4,128]{4,3,2,1,0:T(4,128)(2,1)S(1)}, bf16[12,12,2,4,128]{4,3,2,1,0:T(4,128)(2,1)}, u32[]{:S(2)}) copy-start(bf16[12,12,2,4,128]{4,3,2,1,0:T(4,128)(2,1)} %param.6) | copy-start | bytes 884740
  0.6 1.0 copy-start.1
  1.6 0.8 copy-start.3
  2.4 0.7 copy-start.6
  3.1 9.0 %copy-start.8 = (f32[12]{0:T(128)S(1)}, f32[12]{0:T(128)}, u32[]{:S(2)}) copy-start(f32[12]{0:T(128)} %param.8) | copy-start | bytes 148
  3.2 30.1 %copy-start.2 = (bf16[12,12,2,4,128]{4,3,2,1,0:T(4,128)(2,1)S(1)}, bf16[12,12,2,4,128]{4,3,2,1,0:T(4,128)(2,1)}, u32[]{:S(2)}) copy-start(bf16[12,12,2,4,128]{4,3,2,1,0:T(4,128)(2,1)} %param.7) | copy-start | bytes 884740
  12.3 21.5 %collective-permute-start = (f32[13,8,128]{2,1,0:T(8,128)S(1)}, f32[13,8,128]{2,1,0:T(8,128)S(1)}, u32[]{:S(2)}, u32[]{:S(2)}) collective-permute-start(f32[13,8,128]{2,1,0:T(8,128)S(1)} %get-tuple-element.32), channel_id=1, source_target_pairs={{0,4},{4,0},{8,12},{12,8},{16,20},{20,16},{24,28},{28,24},{32,36},... | collective-permute-start | bytes 159752 | tf_op jit(solution)/shard_map/ppermute | solution.py:693
  14.3 20.9 %collective-permute-start.1 = (f32[13,8,128]{2,1,0:T(8,128)S(1)}, f32[13,8,128]{2,1,0:T(8,128)S(1)}, u32[]{:S(2)}, u32[]{:S(2)}) collective-permute-start(f32[13,8,128]{2,1,0:T(8,128)S(1)} %get-tuple-element.33), channel_id=1, source_target_pairs={{4,8},{12,16},{20,24},{28,32},{36,40},{44,48},{52,56},{60,64},{68,... | collective-permute-start | bytes 159752 | tf_op jit(solution)/shard_map/ppermute | solution.py:693
  46.8 10.1 %collective-permute-start.2 = (f32[36,8,128]{2,1,0:T(8,128)S(1)}, f32[36,8,128]{2,1,0:T(8,128)S(1)}, u32[]{:S(2)}, u32[]{:S(2)}) collective-permute-start(f32[36,8,128]{2,1,0:T(8,128)S(1)} %get-tuple-element.37), channel_id=1, source_target_pairs={{8,20},{12,16},{16,12},{20,8},{24,36},{28,32},{32,28},{36,24},{40,... | collective-permute-start | bytes 442376 | tf_op jit(solution)/shard_map/ppermute | solution.py:705
  52.2 0.7 collective-permute-start.3
  59.4 12.8 %copy-start.4 = (f32[12,2,4,128]{3,2,1,0:T(4,128)S(1)}, f32[12,2,4,128]{3,2,1,0:T(4,128)}, u32[]{:S(2)}) copy-start(f32[12,2,4,128]{3,2,1,0:T(4,128)} %param.5) | copy-start | bytes 147460
  59.4 12.8 %all-to-all-start.2 = ((f32[8,6,8,128]{3,2,1,0:T(8,128)}), f32[8,6,8,128]{3,2,1,0:T(8,128)S(1)}, u32[]{:S(2)}, u32[]{:S(2)}) async-start(f32[8,6,8,128]{3,2,1,0:T(8,128)} %get-tuple-element.40), calls=%async_computation.2 | async-start | bytes 393216 | tf_op jit(solution)/shard_map/all_to_all | solution.py:689
  64.8 7.4 %copy-start.7 = (s32[1,1,4]{2,1,0:T(1,128)S(1)}, s32[1,1,4]{2,1,0:T(1,128)}, u32[]{:S(2)}) copy-start(s32[1,1,4]{2,1,0:T(1,128)} %param.9) | copy-start | bytes 52
  64.8 7.4 %collective-permute-start.4 = (f32[6,8,128]{2,1,0:T(8,128)S(1)}, f32[6,8,128]{2,1,0:T(8,128)S(1)}, u32[]{:S(2)}, u32[]{:S(2)}) collective-permute-start(f32[6,8,128]{2,1,0:T(8,128)S(1)} %get-tuple-element.41), channel_id=1, source_target_pairs={{4,8},{12,16},{20,24},{28,32},{36,40},{44,48},{52,56},{60,64},{68,... | collective-permute-start | bytes 73736 | tf_op jit(solution)/shard_map/ppermute | solution.py:688
  72.6 6.5 %collective-permute-start.5 = (f32[13,8,128]{2,1,0:T(8,128)S(1)}, f32[13,8,128]{2,1,0:T(8,128)S(1)}, u32[]{:S(2)}, u32[]{:S(2)}) collective-permute-start(f32[13,8,128]{2,1,0:T(8,128)S(1)} %get-tuple-element.44), channel_id=1, source_target_pairs={{0,4},{4,0},{8,12},{12,8},{16,20},{20,16},{24,28},{28,24},{32,36},... | collective-permute-start | bytes 159752 | tf_op jit(solution)/shard_map/ppermute | solution.py:693
  74.5 7.6 %collective-permute-start.6 = (f32[13,8,128]{2,1,0:T(8,128)S(1)}, f32[13,8,128]{2,1,0:T(8,128)S(1)}, u32[]{:S(2)}, u32[]{:S(2)}) collective-permute-start(f32[13,8,128]{2,1,0:T(8,128)S(1)} %get-tuple-element.45), channel_id=1, source_target_pairs={{4,8},{12,16},{20,24},{28,32},{36,40},{44,48},{52,56},{60,64},{68,... | collective-permute-start | bytes 159752 | tf_op jit(solution)/shard_map/ppermute | solution.py:693
  95.1 8.5 %collective-permute-start.7 = (f32[18,8,128]{2,1,0:T(8,128)S(1)}, f32[18,8,128]{2,1,0:T(8,128)S(1)}, u32[]{:S(2)}, u32[]{:S(2)}) collective-permute-start(f32[18,8,128]{2,1,0:T(8,128)S(1)} %get-tuple-element.50), channel_id=1, source_target_pairs={{8,20},{12,16},{16,12},{20,8},{24,36},{28,32},{32,28},{36,24},{40,... | collective-permute-start | bytes 221192 | tf_op jit(solution)/shard_map/ppermute | solution.py:705
  99.6 0.7 collective-permute-start.8
  106.0 13.1 %copy-start.5 = (f32[12,8,128]{2,1,0:T(8,128)S(1)}, f32[12,8,128]{2,1,0:T(8,128)}, u32[]{:S(2)}) copy-start(f32[12,8,128]{2,1,0:T(8,128)} %get-tuple-element.53.refs_4_) | copy-start | bytes 147460
  106.0 13.1 %all-to-all-start.4 = ((f32[8,6,8,128]{3,2,1,0:T(8,128)}), f32[8,6,8,128]{3,2,1,0:T(8,128)S(1)}, u32[]{:S(2)}, u32[]{:S(2)}) async-start(f32[8,6,8,128]{3,2,1,0:T(8,128)} %get-tuple-element.54), calls=%async_computation.4 | async-start | bytes 393216 | tf_op jit(solution)/shard_map/all_to_all | solution.py:689
  111.8 7.2 %collective-permute-start.9 = (f32[6,8,128]{2,1,0:T(8,128)S(1)}, f32[6,8,128]{2,1,0:T(8,128)S(1)}, u32[]{:S(2)}, u32[]{:S(2)}) collective-permute-start(f32[6,8,128]{2,1,0:T(8,128)S(1)} %get-tuple-element.55), channel_id=1, source_target_pairs={{4,8},{12,16},{20,24},{28,32},{36,40},{44,48},{52,56},{60,64},{68,... | collective-permute-start | bytes 73736 | tf_op jit(solution)/shard_map/ppermute | solution.py:688

commit v7 on v6

--- a/solution.py
+++ b/solution.py
@@ -59,11 +59,11 @@
     return jnp.dot(a, b, preferred_element_type=F32)
 
 
-def dot_right(x, weights, parts=3):
+def dot_right(x, weights, parts=2):
     return dot(jnp.concatenate(split(x, parts), axis=1), jnp.concatenate([weights] * parts, axis=0))
 
 
-def dot_left(weights, x, parts=3):
+def dot_left(weights, x, parts=2):
     return dot(jnp.concatenate([weights] * parts, axis=1), jnp.concatenate(split(x, parts), axis=0))
 
 

time: 121 us -> 120 us (level)
  no operation moved by 1% of the time
where the time goes in v7:
time: 120 us
  starting transfers between devices  59.2 us (49%)
  blocking collectives  32.6 us (27%)
  waiting for transfers between devices  16.9 us (14%)
  Pallas kernels  7.63 us (6%)
  local copies, waits for them, and re-layouts  2.48 us (2%)
    all_to_all x2, blocking collectives, to_coarse(): recv = lax.all_to_all(message, ('xc', 'core', 'gz'), 0, 0)  23.7 us
    ppermute x2, starting transfers between devices, layers(): lax.ppermute(cross, X_AXES, swap_pairs)  23.6 us
    all_to_all x2, starting transfers between devices, faces(): face = lax.all_to_all(face, ('core', 'gz'), 0, 0)  11.2 us
    ppermute x2, starting transfers between devices, to_coarse(): far = lax.ppermute(far, X_AXES, far_pairs)  9.96 us
    ppermute x2, starting transfers between devices, faces(): swap = lax.ppermute(swap, X_AXES, swap_pairs)  9.24 us
    all_to_all x1, blocking collectives, local(): edges = lax.all_to_all(edges, 'gz', 0, 0)  8.92 us
    pallas_call x11, Pallas kernels, call(): pl.pallas_call(body, name=name, in_specs=[VMEM_SPEC] * (len(small) + len(...  7.63 us
    ppermute x2, waiting for transfers between devices, to_coarse(): far = lax.ppermute(far, X_AXES, far_pairs)  7.2 us
  transfers between devices with their start and end apart: 12, of which 6 were waited for; matrix products, arithmetic and copies ran while one was open for 0% of the time, Pallas kernels for 0%

profile of v7, /device:TPU:14, one launch (start us, length us, event | category | flops | bytes accessed | tf_op | source)
XLA Modules:
  0.0 119.6 jit_solution(4704548398382527775)
XLA Ops:
  0.6 0.0 copy-start
  0.6 0.0 copy-start.1
  0.7 1.0 copy-done.1
  1.6 0.8 copy-done.3
  2.4 0.7 copy-done.6
  3.1 0.1 first.1
  3.2 0.0 copy-start.2
  3.2 8.9 %all_to_all.25.refs_5_ = f32[4,3,8,128]{3,2,1,0:T(8,128)S(1)} all-to-all(f32[4,3,8,128]{3,2,1,0:T(8,128)S(1)} %get-tuple-element.30), channel_id=1, replica_groups=mesh['xg'=64,'xc'=2,'core'=2,'gz'=4] {'gz'}, dimensions={0} | all-to-all | bytes 98304 | tf_op jit(solution)/shard_map/all_to_all | solution.py:711
  12.1 0.0 copy-done
  12.1 0.0 copy-done.8
  12.1 0.2 part.1
  12.3 1.9 %collective-permute-start = (f32[13,8,128]{2,1,0:T(8,128)S(1)}, f32[13,8,128]{2,1,0:T(8,128)S(1)}, u32[]{:S(2)}, u32[]{:S(2)}) collective-permute-start(f32[13,8,128]{2,1,0:T(8,128)S(1)} %get-tuple-element.32), channel_id=1, source_target_pairs={{0,4},{4,0},{8,12},{12,8},{16,20},{20,16},{24,28},{28,24},{32,36},... | collective-permute-start | bytes 159752 | tf_op jit(solution)/shard_map/ppermute | solution.py:693
  14.3 19.0 %collective-permute-start.1 = (f32[13,8,128]{2,1,0:T(8,128)S(1)}, f32[13,8,128]{2,1,0:T(8,128)S(1)}, u32[]{:S(2)}, u32[]{:S(2)}) collective-permute-start(f32[13,8,128]{2,1,0:T(8,128)S(1)} %get-tuple-element.33), channel_id=1, source_target_pairs={{4,8},{12,16},{20,24},{28,32},{36,40},{44,48},{52,56},{60,64},{68,... | collective-permute-start | bytes 159752 | tf_op jit(solution)/shard_map/ppermute | solution.py:693
  33.3 0.0 copy-done.2
  33.3 0.5 blocks.1.refs_6_
  33.8 0.0 collective-permute-done.refs_4_
  33.8 1.3 %collective-permute-done.1.refs_5_ = f32[13,8,128]{2,1,0:T(8,128)S(1)} collective-permute-done((f32[13,8,128]{2,1,0:T(8,128)S(1)}, f32[13,8,128]{2,1,0:T(8,128)S(1)}, u32[]{:S(2)}, u32[]{:S(2)}) %collective-permute-start.1) | collective-permute-done | bytes 53280 | tf_op jit(solution)/shard_map/ppermute | solution.py:693
  35.1 0.4 send.2
  35.5 11.2 %all_to_all.26.refs_0_.refs_6_ = f32[16,5,8,128]{3,2,1,0:T(8,128)S(1)} all-to-all(f32[16,5,8,128]{3,2,1,0:T(8,128)S(1)} %get-tuple-element.35), channel_id=1, replica_groups=mesh['xg'=64,'xc'=2,'core'=2,'gz'=4] {'xc','core','gz'}, dimensions={0} | all-to-all | bytes 655360 | tf_op jit(solution)/shard_map/all_to_all | solution.py:696
  46.7 0.1 gather.2
  46.7 5.5 %collective-permute-start.2 = (f32[36,8,128]{2,1,0:T(8,128)S(1)}, f32[36,8,128]{2,1,0:T(8,128)S(1)}, u32[]{:S(2)}, u32[]{:S(2)}) collective-permute-start(f32[36,8,128]{2,1,0:T(8,128)S(1)} %get-tuple-element.37), channel_id=1, source_target_pairs={{8,20},{12,16},{16,12},{20,8},{24,36},{28,32},{32,28},{36,24},{40,... | collective-permute-start | bytes 442376 | tf_op jit(solution)/shard_map/ppermute | solution.py:705
  52.2 0.7 collective-permute-start.3
  52.9 0.0 collective-permute-done.3.refs_9_
  52.9 3.9 %collective-permute-done.2.refs_8_ = f32[36,8,128]{2,1,0:T(8,128)S(1)} collective-permute-done((f32[36,8,128]{2,1,0:T(8,128)S(1)}, f32[36,8,128]{2,1,0:T(8,128)S(1)}, u32[]{:S(2)}, u32[]{:S(2)}) %collective-permute-start.2) | collective-permute-done | bytes 147488 | tf_op jit(solution)/shard_map/ppermute | solution.py:705
  56.8 2.5 %correct.2 = (f32[12,8,128]{2,1,0:T(8,128)S(1)}, f32[8,6,8,128]{3,2,1,0:T(8,128)}, f32[6,8,128]{2,1,0:T(8,128)S(1)}, f32[8,11,8,128]{3,2,1,0:T(8,128)S(1)}, f32[3,8,128]{2,1,0:T(8,128)S(1)}) custom-call(s32[1,4]{1,0:T(1,128)S(1)} %bitcast.27, f32[1,12]{1,0:T(1,128)S(1)} %bitcast.34, bf16[1152,128]{1,0:T(8,128)(2,1)S(1)} %bitcast.9, ...), custom_call_target="tpu_custom_call" | custom-call | tf_op jit(solution)/shard_map/correct/pallas_call | solution.py:650
  59.3 5.4 %all-to-all-start.2 = ((f32[8,6,8,128]{3,2,1,0:T(8,128)}), f32[8,6,8,128]{3,2,1,0:T(8,128)S(1)}, u32[]{:S(2)}, u32[]{:S(2)}) async-start(f32[8,6,8,128]{3,2,1,0:T(8,128)} %get-tuple-element.40), calls=%async_computation.2 | async-start | bytes 393216 | tf_op jit(solution)/shard_map/all_to_all | solution.py:689
  64.7 4.7 %collective-permute-start.4 = (f32[6,8,128]{2,1,0:T(8,128)S(1)}, f32[6,8,128]{2,1,0:T(8,128)S(1)}, u32[]{:S(2)}, u32[]{:S(2)}) collective-permute-start(f32[6,8,128]{2,1,0:T(8,128)S(1)} %get-tuple-element.41), channel_id=1, source_target_pairs={{4,8},{12,16},{20,24},{28,32},{36,40},{44,48},{52,56},{60,64},{68,... | collective-permute-start | bytes 73736 | tf_op jit(solution)/shard_map/ppermute | solution.py:688
  69.4 2.7 %collective-permute-done.4.refs_6_ = f32[6,8,128]{2,1,0:T(8,128)S(1)} collective-permute-done((f32[6,8,128]{2,1,0:T(8,128)S(1)}, f32[6,8,128]{2,1,0:T(8,128)S(1)}, u32[]{:S(2)}, u32[]{:S(2)}) %collective-permute-start.4) | collective-permute-done | bytes 24608 | tf_op jit(solution)/shard_map/ppermute | solution.py:688
  72.1 0.0 all-to-all-done.2.refs_5_
  72.1 0.0 copy-done.4
  72.1 0.0 copy-done.7
  72.1 0.4 sweep.1
  72.5 1.9 %collective-permute-start.5 = (f32[13,8,128]{2,1,0:T(8,128)S(1)}, f32[13,8,128]{2,1,0:T(8,128)S(1)}, u32[]{:S(2)}, u32[]{:S(2)}) collective-permute-start(f32[13,8,128]{2,1,0:T(8,128)S(1)} %get-tuple-element.44), channel_id=1, source_target_pairs={{0,4},{4,0},{8,12},{12,8},{16,20},{20,16},{24,28},{28,24},{32,36},... | collective-permute-start | bytes 159752 | tf_op jit(solution)/shard_map/ppermute | solution.py:693
  74.4 4.6 %collective-permute-start.6 = (f32[13,8,128]{2,1,0:T(8,128)S(1)}, f32[13,8,128]{2,1,0:T(8,128)S(1)}, u32[]{:S(2)}, u32[]{:S(2)}) collective-permute-start(f32[13,8,128]{2,1,0:T(8,128)S(1)} %get-tuple-element.45), channel_id=1, source_target_pairs={{4,8},{12,16},{20,24},{28,32},{36,40},{44,48},{52,56},{60,64},{68,... | collective-permute-start | bytes 159752 | tf_op jit(solution)/shard_map/ppermute | solution.py:693
  78.9 0.0 collective-permute-done.5.refs_4_
  79.0 3.0 %collective-permute-done.6.refs_5_ = f32[13,8,128]{2,1,0:T(8,128)S(1)} collective-permute-done((f32[13,8,128]{2,1,0:T(8,128)S(1)}, f32[13,8,128]{2,1,0:T(8,128)S(1)}, u32[]{:S(2)}, u32[]{:S(2)}) %collective-permute-start.6) | collective-permute-done | bytes 53280 | tf_op jit(solution)/shard_map/ppermute | solution.py:693
  81.9 0.4 send.3
  82.3 12.5 %all_to_all.27.refs_0_.refs_6_ = f32[16,6,8,128]{3,2,1,0:T(8,128)S(1)} all-to-all(f32[16,6,8,128]{3,2,1,0:T(8,128)S(1)} %get-tuple-element.48), channel_id=1, replica_groups=mesh['xg'=64,'xc'=2,'core'=2,'gz'=4] {'xc','core','gz'}, dimensions={0} | all-to-all | bytes 786432 | tf_op jit(solution)/shard_map/all_to_all | solution.py:696
  94.9 4.5 %collective-permute-start.7 = (f32[18,8,128]{2,1,0:T(8,128)S(1)}, f32[18,8,128]{2,1,0:T(8,128)S(1)}, u32[]{:S(2)}, u32[]{:S(2)}) collective-permute-start(f32[18,8,128]{2,1,0:T(8,128)S(1)} %get-tuple-element.50), channel_id=1, source_target_pairs={{8,20},{12,16},{16,12},{20,8},{24,36},{28,32},{32,28},{36,24},{40,... | collective-permute-start | bytes 221192 | tf_op jit(solution)/shard_map/ppermute | solution.py:705
  99.4 0.7 collective-permute-start.8
  100.1 0.0 collective-permute-done.8.refs_9_
  100.1 3.3 %collective-permute-done.7.refs_8_ = f32[18,8,128]{2,1,0:T(8,128)S(1)} collective-permute-done((f32[18,8,128]{2,1,0:T(8,128)S(1)}, f32[18,8,128]{2,1,0:T(8,128)S(1)}, u32[]{:S(2)}, u32[]{:S(2)}) %collective-permute-start.7) | collective-permute-done | bytes 73760 | tf_op jit(solution)/shard_map/ppermute | solution.py:705
  103.4 2.4 %correct.3 = (f32[12,8,128]{2,1,0:T(8,128)}, f32[8,6,8,128]{3,2,1,0:T(8,128)}, f32[6,8,128]{2,1,0:T(8,128)S(1)}) custom-call(s32[1,4]{1,0:T(1,128)S(1)} %bitcast.30, f32[1,12]{1,0:T(1,128)S(1)} %bitcast.37, bf16[1152,128]{1,0:T(8,128)(2,1)S(1)} %bitcast.11, bf16[1152,128]{1,0:T(8,128)(2,1)S(1)} %bitcast.17, ...), custom_call_target="tpu_custom_call" | custom-call | tf_op jit(solution)/shard_map/correct/pallas_call | solution.py:650
  105.8 5.8 %all-to-all-start.4 = ((f32[8,6,8,128]{3,2,1,0:T(8,128)}), f32[8,6,8,128]{3,2,1,0:T(8,128)S(1)}, u32[]{:S(2)}, u32[]{:S(2)}) async-start(f32[8,6,8,128]{3,2,1,0:T(8,128)} %get-tuple-element.54), calls=%async_computation.4 | async-start | bytes 393216 | tf_op jit(solution)/shard_map/all_to_all | solution.py:689
  111.6 4.6 %collective-permute-start.9 = (f32[6,8,128]{2,1,0:T(8,128)S(1)}, f32[6,8,128]{2,1,0:T(8,128)S(1)}, u32[]{:S(2)}, u32[]{:S(2)}) collective-permute-start(f32[6,8,128]{2,1,0:T(8,128)S(1)} %get-tuple-element.55), channel_id=1, source_target_pairs={{4,8},{12,16},{20,24},{28,32},{36,40},{44,48},{52,56},{60,64},{68,... | collective-permute-start | bytes 73736 | tf_op jit(solution)/shard_map/ppermute | solution.py:688
  116.2 2.7 %collective-permute-done.9.refs_6_ = f32[6,8,128]{2,1,0:T(8,128)S(1)} collective-permute-done((f32[6,8,128]{2,1,0:T(8,128)S(1)}, f32[6,8,128]{2,1,0:T(8,128)S(1)}, u32[]{:S(2)}, u32[]{:S(2)}) %collective-permute-start.9) | collective-permute-done | bytes 24608 | tf_op jit(solution)/shard_map/ppermute | solution.py:688
  118.8 0.0 all-to-all-done.4.refs_5_
  118.8 0.8 last.1
  (8 shorter events, 0.1 us)
Async XLA Ops:
  0.6 11.5 %copy-start = (bf16[12,12,2,4,128]{4,3,2,1,0:T(4,128)(2,1)S(1)}, bf16[12,12,2,4,128]{4,3,2,1,0:T(4,128)(2,1)}, u32[]{:S(2)}) copy-start(bf16[12,12,2,4,128]{4,3,2,1,0:T(4,128)(2,1)} %param.6) | copy-start | bytes 884740
  0.6 1.0 copy-start.1
  1.6 0.8 copy-start.3
  2.4 0.7 copy-start.6
  3.1 9.0 %copy-start.8 = (f32[12]{0:T(128)S(1)}, f32[12]{0:T(128)}, u32[]{:S(2)}) copy-start(f32[12]{0:T(128)} %param.8) | copy-start | bytes 148
  3.2 30.1 %copy-start.2 = (bf16[12,12,2,4,128]{4,3,2,1,0:T(4,128)(2,1)S(1)}, bf16[12,12,2,4,128]{4,3,2,1,0:T(4,128)(2,1)}, u32[]{:S(2)}) copy-start(bf16[12,12,2,4,128]{4,3,2,1,0:T(4,128)(2,1)} %param.7) | copy-start | bytes 884740
  12.3 21.5 %collective-permute-start = (f32[13,8,128]{2,1,0:T(8,128)S(1)}, f32[13,8,128]{2,1,0:T(8,128)S(1)}, u32[]{:S(2)}, u32[]{:S(2)}) collective-permute-start(f32[13,8,128]{2,1,0:T(8,128)S(1)} %get-tuple-element.32), channel_id=1, source_target_pairs={{0,4},{4,0},{8,12},{12,8},{16,20},{20,16},{24,28},{28,24},{32,36},... | collective-permute-start | bytes 159752 | tf_op jit(solution)/shard_map/ppermute | solution.py:693
  14.3 20.9 %collective-permute-start.1 = (f32[13,8,128]{2,1,0:T(8,128)S(1)}, f32[13,8,128]{2,1,0:T(8,128)S(1)}, u32[]{:S(2)}, u32[]{:S(2)}) collective-permute-start(f32[13,8,128]{2,1,0:T(8,128)S(1)} %get-tuple-element.33), channel_id=1, source_target_pairs={{4,8},{12,16},{20,24},{28,32},{36,40},{44,48},{52,56},{60,64},{68,... | collective-permute-start | bytes 159752 | tf_op jit(solution)/shard_map/ppermute | solution.py:693
  46.7 10.1 %collective-permute-start.2 = (f32[36,8,128]{2,1,0:T(8,128)S(1)}, f32[36,8,128]{2,1,0:T(8,128)S(1)}, u32[]{:S(2)}, u32[]{:S(2)}) collective-permute-start(f32[36,8,128]{2,1,0:T(8,128)S(1)} %get-tuple-element.37), channel_id=1, source_target_pairs={{8,20},{12,16},{16,12},{20,8},{24,36},{28,32},{32,28},{36,24},{40,... | collective-permute-start | bytes 442376 | tf_op jit(solution)/shard_map/ppermute | solution.py:705
  52.2 0.7 collective-permute-start.3
  59.3 12.8 %copy-start.4 = (f32[12,2,4,128]{3,2,1,0:T(4,128)S(1)}, f32[12,2,4,128]{3,2,1,0:T(4,128)}, u32[]{:S(2)}) copy-start(f32[12,2,4,128]{3,2,1,0:T(4,128)} %param.5) | copy-start | bytes 147460
  59.3 12.8 %all-to-all-start.2 = ((f32[8,6,8,128]{3,2,1,0:T(8,128)}), f32[8,6,8,128]{3,2,1,0:T(8,128)S(1)}, u32[]{:S(2)}, u32[]{:S(2)}) async-start(f32[8,6,8,128]{3,2,1,0:T(8,128)} %get-tuple-element.40), calls=%async_computation.2 | async-start | bytes 393216 | tf_op jit(solution)/shard_map/all_to_all | solution.py:689
  64.7 7.4 %copy-start.7 = (s32[1,1,4]{2,1,0:T(1,128)S(1)}, s32[1,1,4]{2,1,0:T(1,128)}, u32[]{:S(2)}) copy-start(s32[1,1,4]{2,1,0:T(1,128)} %param.9) | copy-start | bytes 52
  64.7 7.4 %collective-permute-start.4 = (f32[6,8,128]{2,1,0:T(8,128)S(1)}, f32[6,8,128]{2,1,0:T(8,128)S(1)}, u32[]{:S(2)}, u32[]{:S(2)}) collective-permute-start(f32[6,8,128]{2,1,0:T(8,128)S(1)} %get-tuple-element.41), channel_id=1, source_target_pairs={{4,8},{12,16},{20,24},{28,32},{36,40},{44,48},{52,56},{60,64},{68,... | collective-permute-start | bytes 73736 | tf_op jit(solution)/shard_map/ppermute | solution.py:688
  72.5 6.5 %collective-permute-start.5 = (f32[13,8,128]{2,1,0:T(8,128)S(1)}, f32[13,8,128]{2,1,0:T(8,128)S(1)}, u32[]{:S(2)}, u32[]{:S(2)}) collective-permute-start(f32[13,8,128]{2,1,0:T(8,128)S(1)} %get-tuple-element.44), channel_id=1, source_target_pairs={{0,4},{4,0},{8,12},{12,8},{16,20},{20,16},{24,28},{28,24},{32,36},... | collective-permute-start | bytes 159752 | tf_op jit(solution)/shard_map/ppermute | solution.py:693
  74.4 7.6 %collective-permute-start.6 = (f32[13,8,128]{2,1,0:T(8,128)S(1)}, f32[13,8,128]{2,1,0:T(8,128)S(1)}, u32[]{:S(2)}, u32[]{:S(2)}) collective-permute-start(f32[13,8,128]{2,1,0:T(8,128)S(1)} %get-tuple-element.45), channel_id=1, source_target_pairs={{4,8},{12,16},{20,24},{28,32},{36,40},{44,48},{52,56},{60,64},{68,... | collective-permute-start | bytes 159752 | tf_op jit(solution)/shard_map/ppermute | solution.py:693
  94.9 8.5 %collective-permute-start.7 = (f32[18,8,128]{2,1,0:T(8,128)S(1)}, f32[18,8,128]{2,1,0:T(8,128)S(1)}, u32[]{:S(2)}, u32[]{:S(2)}) collective-permute-start(f32[18,8,128]{2,1,0:T(8,128)S(1)} %get-tuple-element.50), channel_id=1, source_target_pairs={{8,20},{12,16},{16,12},{20,8},{24,36},{28,32},{32,28},{36,24},{40,... | collective-permute-start | bytes 221192 | tf_op jit(solution)/shard_map/ppermute | solution.py:705
  99.4 0.7 collective-permute-start.8
  105.8 13.0 %copy-start.5 = (f32[12,8,128]{2,1,0:T(8,128)S(1)}, f32[12,8,128]{2,1,0:T(8,128)}, u32[]{:S(2)}) copy-start(f32[12,8,128]{2,1,0:T(8,128)} %get-tuple-element.53.refs_4_) | copy-start | bytes 147460
  105.8 13.0 %all-to-all-start.4 = ((f32[8,6,8,128]{3,2,1,0:T(8,128)}), f32[8,6,8,128]{3,2,1,0:T(8,128)S(1)}, u32[]{:S(2)}, u32[]{:S(2)}) async-start(f32[8,6,8,128]{3,2,1,0:T(8,128)} %get-tuple-element.54), calls=%async_computation.4 | async-start | bytes 393216 | tf_op jit(solution)/shard_map/all_to_all | solution.py:689
  111.6 7.2 %collective-permute-start.9 = (f32[6,8,128]{2,1,0:T(8,128)S(1)}, f32[6,8,128]{2,1,0:T(8,128)S(1)}, u32[]{:S(2)}, u32[]{:S(2)}) collective-permute-start(f32[6,8,128]{2,1,0:T(8,128)S(1)} %get-tuple-element.55), channel_id=1, source_target_pairs={{4,8},{12,16},{20,24},{28,32},{36,40},{44,48},{52,56},{60,64},{68,... | collective-permute-start | bytes 73736 | tf_op jit(solution)/shard_map/ppermute | solution.py:688
